TPU v7x, 256 devices: a whole 4x4x8 slice. The times are simulated.
256 devices in a mesh: date: 16 (over z, core), row: 4 (over x), col: 4 (over y).
Axes of the slice: x: 4, y: 4, z: 8, core: 2. Of those that a mesh axis runs over, the one named last changes fastest.
Arguments:
- stack: float32 [64, 2, 320, 2560], P('date', None, 'row', 'col'), may hold values from -20 to 20
- pair_list: int32 [64, 2], replicated, may hold values from 0 to 63, as said below
Outputs:
- filtered: float32 [64, 2, 64, 128], P('date', None, 'row', 'col')
- coherence: float32 [64, 64, 128], P('date', 'row', 'col')
Inputs may be any that keep to these rules, and one draw needn't show every extreme that they name: `pair_list`: reference and secondary of each pair; the reference of rows d*4 to (d+1)*4 - 1 is one of acquisitions d*4 to (d+1)*4 - 1, and the secondary lies 1 to 3 acquisitions after it.
All inputs are finite; a program needn't handle non-finite values.
Results may differ from a plain program's by a relative error of at most 0.0003.
Values sent between devices are 32-bit elements; how exact they have to be, the bound alone decides.
No kernel may reach another device: no remote copies, remote signals or barrier semaphores. Data moves between devices by JAX's collectives and lax.ppermute only.
A program may use at most 64 MiB of HBM per device.

v0:
```python
import math

import jax
import jax.numpy as jnp
from jax import lax
from jax.sharding import PartitionSpec as P

SPAN = 3
LOOK_R = 5
LOOK_C = 20
PATCH = 32


def passed_along(x, axis, by):
    size = lax.axis_size(axis)
    pairs = [(i, i + by) for i in range(size) if 0 <= i + by < size]
    return lax.ppermute(x, axis, pairs)


def padded(cells, sides, width):
    for axis, dim in sides:
        count = lax.axis_size(axis)
        ends = count - 1
        head = lax.slice_in_dim(cells, 0, width, axis=dim)
        tail = lax.slice_in_dim(cells, cells.shape[dim] - width, cells.shape[dim], axis=dim)
        cells = jnp.concatenate(
            [
                lax.ppermute(tail, axis, [(i, (i + 1) % count) for i in range(ends)]),
                cells,
                lax.ppermute(head, axis, [((i + 1) % count, i) for i in range(ends)]),
            ],
            axis=dim,
        )
    return cells


def look_means(values):
    pair_total = values.shape[0]
    row_total = values.shape[1]
    col_total = values.shape[2]
    shaped = values.reshape(pair_total, row_total // LOOK_R, LOOK_R, col_total // LOOK_C, LOOK_C)
    return shaped.mean(axis=(2, 4))


def cross_terms(primary, secondary):
    cross_real = primary[:, 0] * secondary[:, 0] + primary[:, 1] * secondary[:, 1]
    cross_imag = primary[:, 1] * secondary[:, 0] - primary[:, 0] * secondary[:, 1]
    power_secondary = secondary[:, 0] * secondary[:, 0] + secondary[:, 1] * secondary[:, 1]
    return (look_means(cross_real), look_means(cross_imag), look_means(power_secondary))


def finish(primary, look_real, look_imag, mean_secondary):
    power_primary = primary[:, 0] * primary[:, 0] + primary[:, 1] * primary[:, 1]
    mean_primary = look_means(power_primary)
    magnitude = jnp.sqrt(look_real * look_real + look_imag * look_imag)
    coherence = magnitude / jnp.sqrt((mean_primary + 1e-06) * (mean_secondary + 1e-06))
    return (jnp.stack([look_real, look_imag], axis=1), coherence)


def transform_tables():
    indices = jnp.arange(PATCH, dtype=jnp.int32)
    phases = indices[:, None] * indices[None, :] % PATCH
    angles = phases.astype(jnp.float32) * (2.0 * math.pi / PATCH)
    return (jnp.cos(angles), jnp.sin(angles))


def along_first(matrix, values):
    return jnp.einsum("ku,niujv->nikjv", matrix, values, precision=lax.Precision.HIGHEST)


def along_second(matrix, values):
    return jnp.einsum("lv,niujv->niujl", matrix, values, precision=lax.Precision.HIGHEST)


def goldstein(extended):
    pair_total = extended.shape[0]
    half_patch = PATCH // 2
    blocks_down = extended.shape[2] // half_patch
    blocks_across = extended.shape[3] // half_patch
    blocks = extended.reshape(pair_total, 2, blocks_down, half_patch, blocks_across, half_patch)
    tall_pairs = jnp.concatenate([blocks[:, :, :-1], blocks[:, :, 1:]], axis=3)
    patches = jnp.concatenate([tall_pairs[:, :, :, :, :-1], tall_pairs[:, :, :, :, 1:]], axis=5)
    cosine, sine = transform_tables()
    real_in = patches[:, 0]
    imag_in = patches[:, 1]
    step_real = along_first(cosine, real_in) + along_first(sine, imag_in)
    step_imag = along_first(cosine, imag_in) - along_first(sine, real_in)
    spec_real = along_second(cosine, step_real) + along_second(sine, step_imag)
    spec_imag = along_second(cosine, step_imag) - along_second(sine, step_real)
    magnitude = jnp.sqrt(spec_real * spec_real + spec_imag * spec_imag)
    smooth = jnp.zeros_like(magnitude)
    for shift_down in (-1, 0, 1):
        for shift_across in (-1, 0, 1):
            smooth = smooth + jnp.roll(magnitude, (shift_down, shift_across), axis=(2, 4))
    response = jnp.sqrt(smooth / 9.0) / PATCH
    filt_real = spec_real * response
    filt_imag = spec_imag * response
    back_real = along_first(cosine, filt_real) - along_first(sine, filt_imag)
    back_imag = along_first(cosine, filt_imag) + along_first(sine, filt_real)
    out_real = along_second(cosine, back_real) - along_second(sine, back_imag)
    out_imag = along_second(cosine, back_imag) + along_second(sine, back_real)
    position = jnp.arange(PATCH, dtype=jnp.float32)
    taper_weights = jnp.where(
        position < half_patch, (position + 0.5) / half_patch, (PATCH - 0.5 - position) / half_patch
    )
    window = taper_weights[:, None, None] * taper_weights[None, None, :] / (PATCH * PATCH)

    def assemble(component):
        weighted = component * window
        down_sum = weighted[:, 1:, :half_patch] + weighted[:, :-1, half_patch:]
        assembled = down_sum[:, :, :, 1:, :half_patch] + down_sum[:, :, :, :-1, half_patch:]
        shape_now = assembled.shape
        return assembled.reshape(
            shape_now[0], shape_now[1] * shape_now[2], shape_now[3] * shape_now[4]
        )

    return jnp.stack([assemble(out_real), assemble(out_imag)], axis=1)


def shards(stack, pair_list):
    acq_local = stack.shape[0]
    date_index = lax.axis_index("date")
    leading = stack[:SPAN]
    following = passed_along(leading, "date", -1)
    pairs_local = pair_list.shape[0] // lax.axis_size("date")
    local_pairs = (
        lax.dynamic_slice_in_dim(pair_list, date_index * pairs_local, pairs_local, 0)
        - date_index * acq_local
    )
    batch_size = math.gcd(pairs_local, 8)
    batches = local_pairs.reshape(pairs_local // batch_size, batch_size, 2)
    acquisitions = jnp.concatenate([stack, following], axis=0)

    def one_batch(indices):
        primary = jnp.take(acquisitions, indices[:, 0], axis=0)
        secondary = jnp.take(acquisitions, indices[:, 1], axis=0)
        look_real, look_imag, mean_secondary = cross_terms(primary, secondary)
        return finish(primary, look_real, look_imag, mean_secondary)

    looked, coherence = lax.map(one_batch, batches)
    looked = looked.reshape((pairs_local,) + looked.shape[2:])
    coherence = coherence.reshape((pairs_local,) + coherence.shape[2:])
    extended = padded(looked, (("row", 2), ("col", 3)), PATCH // 2)
    return (goldstein(extended), coherence)


def solution(mesh):
    in_specs = (P("date", None, "row", "col"), P())
    out_specs = (P("date", None, "row", "col"), P("date", "row", "col"))
    return jax.shard_map(shards, mesh=mesh, in_specs=in_specs, out_specs=out_specs, check_vma=False)
```

profile of v0, /device:TPU:148, one launch (start us, length us, event | category | flops | bytes accessed | tf_op | source)
XLA Modules:
  0.0 108.5 jit_solution(16519993937854507521)
XLA Ops:
  0.6 2.4 %slice.167 = f32[3,2,80,640]{3,2,1,0:T(8,128)} slice(f32[4,2,80,640]{3,2,1,0:T(8,128)} %param.4), slice={[0:3], [0:2], [0:80], [0:640]} | slice | bytes 2457600 | tf_op jit(solution)/shard_map/slice | solution.py:123
  3.1 1.9 %collective-permute-start = (f32[3,2,80,640]{3,2,1,0:T(8,128)}, f32[3,2,80,640]{3,2,1,0:T(8,128)}, u32[]{:S(2)}, u32[]{:S(2)}) collective-permute-start(f32[3,2,80,640]{3,2,1,0:T(8,128)} %slice.167), channel_id=1, source_target_pairs={{16,0},{32,16},{48,32},{64,48},{80,64},{96,80},{112,96},{128,112},... | collective-permute-start | bytes 3686408 | tf_op jit(solution)/shard_map/ppermute | solution.py:17
  5.1 1.5 %constant_dynamic-update-slice_fusion.1 = f32[7,2,80,640]{3,2,1,0:T(8,128)S(1)} fusion(f32[4,2,80,640]{3,2,1,0:T(8,128)} %param.4), kind=kLoop, calls=%fused_computation.113 | loop fusion | bytes 3276800
  6.7 12.9 %collective-permute-done = f32[3,2,80,640]{3,2,1,0:T(8,128)} collective-permute-done((f32[3,2,80,640]{3,2,1,0:T(8,128)}, f32[3,2,80,640]{3,2,1,0:T(8,128)}, u32[]{:S(2)}, u32[]{:S(2)}) %collective-permute-start) | collective-permute-done | bytes 1228832 | tf_op jit(solution)/shard_map/ppermute | solution.py:17
  19.5 1.4 %constant_dynamic-update-slice_fusion = f32[7,2,80,640]{3,2,1,0:T(8,128)S(1)} fusion(f32[7,2,80,640]{3,2,1,0:T(8,128)S(1)} %constant_dynamic-update-slice_fusion.1, f32[3,2,80,640]{3,2,1,0:T(8,128)} %collective-permute-done), kind=kLoop, calls=%fused_computation.112 | loop fusion | bytes 2457600 | tf_op jit(solution)/shard_map/concatenate | solution.py:132
  20.9 1.8 %gather_fusion = f32[4,2,80,640]{3,2,1,0:T(8,128)} fusion(f32[7,2,80,640]{3,2,1,0:T(8,128)S(1)} %constant_dynamic-update-slice_fusion, s32[1024]{0:T(1024)S(1)} %pad_clamp_fusion.1), kind=kCustom, calls=%fused_computation.clone | custom fusion | bytes 3276816 | tf_op jit(solution)/shard_map/while/body/eval_jaxpr/jit(_take)/gather | solution.py:135
  22.7 1.8 %gather_fusion.1 = f32[4,2,80,640]{3,2,1,0:T(8,128)} fusion(f32[7,2,80,640]{3,2,1,0:T(8,128)S(1)} %constant_dynamic-update-slice_fusion, s32[1024]{0:T(1024)S(1)} %pad_clamp_fusion), kind=kCustom, calls=%fused_computation.1.clone | custom fusion | bytes 3276816 | tf_op jit(solution)/shard_map/while/body/eval_jaxpr/jit(_take)/gather | solution.py:136
  24.5 2.2 %broadcast_select_fusion = (f32[4,2,80,640]{3,2,1,0:T(8,128)S(1)}, f32[4,2,80,640]{3,2,1,0:T(8,128)S(1)}) fusion(f32[4,2,80,640]{3,2,1,0:T(8,128)} %gather_fusion.1, pred[4]{0:T(512)(128)(4,1)S(1)} %get-tuple-element.51, f32[4,2,80,640]{3,2,1,0:T(8,128)} %gather_fusion, pred[4]{0:T(512)(128)(4,1)S(1)} %get-tuple-element.20), kind=kLoop, calls=%fused_computation.26 | loop fusion | flops 819200 | bytes 6553608 | tf_op jit(solution)/shard_map/while/body/eval_jaxpr/jit(_take)/select_n | solution.py:136
  27.1 7.7 %add.170 = f32[4,16,5,32,20]{4,3,2,1,0:T(8,128)} reshape(f32[4,1,80,640]{3,2,1,0:T(8,128)S(1)} %get-tuple-element.24) | data formatting | bytes 1638400 | tf_op jit(solution)/shard_map/while/body/eval_jaxpr/add | solution.py:46
  34.8 7.6 %sub.55 = f32[4,16,5,32,20]{4,3,2,1,0:T(8,128)} reshape(f32[4,1,80,640]{3,2,1,0:T(8,128)S(1)} %get-tuple-element.25) | data formatting | bytes 1638400 | tf_op jit(solution)/shard_map/while/body/eval_jaxpr/sub | solution.py:47
  42.4 2.9 %reduce_sum.40 = f32[4,16,32]{2,1,0:T(8,128)S(1)} reduce(f32[4,16,5,32,20]{4,3,2,1,0:T(8,128)} %add.170, f32[]{:T(128)} %constant.67.clone.1), dimensions={2,4}, to_apply=%region_0.2 | reduce | flops 202752 | bytes 827396 | tf_op jit(solution)/shard_map/while/body/eval_jaxpr/reduce_sum | solution.py:42
  45.4 2.9 %reduce_sum.41 = f32[4,16,32]{2,1,0:T(8,128)S(1)} reduce(f32[4,16,5,32,20]{4,3,2,1,0:T(8,128)} %sub.55, f32[]{:T(128)} %constant.67.clone.1), dimensions={2,4}, to_apply=%region_1.0 | reduce | flops 202752 | bytes 827396 | tf_op jit(solution)/shard_map/while/body/eval_jaxpr/reduce_sum | solution.py:42
  48.3 7.6 %add.195 = f32[4,16,5,32,20]{4,3,2,1,0:T(8,128)} reshape(f32[4,1,80,640]{3,2,1,0:T(8,128)S(1)} %get-tuple-element.26) | data formatting | bytes 1638400 | tf_op jit(solution)/shard_map/while/body/eval_jaxpr/add | solution.py:53
  55.9 2.9 %reduce_sum.42 = f32[4,16,32]{2,1,0:T(8,128)S(1)} reduce(f32[4,16,5,32,20]{4,3,2,1,0:T(8,128)} %add.195, f32[]{:T(128)} %constant.67.clone.1), dimensions={2,4}, to_apply=%region_2.4 | reduce | flops 202752 | bytes 827396 | tf_op jit(solution)/shard_map/while/body/eval_jaxpr/reduce_sum | solution.py:42
  58.8 7.6 %add.198 = f32[4,16,5,32,20]{4,3,2,1,0:T(8,128)} reshape(f32[4,1,80,640]{3,2,1,0:T(8,128)S(1)} %get-tuple-element.27) | data formatting | bytes 1638400 | tf_op jit(solution)/shard_map/while/body/eval_jaxpr/add | solution.py:48
  66.5 2.9 %reduce_sum.43 = f32[4,16,32]{2,1,0:T(8,128)S(1)} reduce(f32[4,16,5,32,20]{4,3,2,1,0:T(8,128)} %add.198, f32[]{:T(128)} %constant.67.clone.1), dimensions={2,4}, to_apply=%region_3.5 | reduce | flops 202752 | bytes 827396 | tf_op jit(solution)/shard_map/while/body/eval_jaxpr/reduce_sum | solution.py:42
  70.0 3.1 %collective-permute-start.1 = (f32[4,2,16,32]{3,2,0,1:T(8,128)S(1)}, f32[4,2,16,32]{3,2,0,1:T(8,128)S(1)}, u32[]{:S(2)}, u32[]{:S(2)}) collective-permute-start(f32[4,2,16,32]{3,2,0,1:T(8,128)S(1)} %pad_maximum_fusion.5), channel_id=1, source_target_pairs={{0,4},{4,8},{8,12},{1,5},{5,9},{9,13},{2,6},{6,10},{10,14},{3,7},{... | collective-permute-start | bytes 49160 | tf_op jit(solution)/shard_map/ppermute | solution.py:28
  73.1 2.7 %collective-permute-start.2 = (f32[4,2,16,32]{3,2,0,1:T(8,128)S(1)}, f32[4,2,16,32]{3,2,0,1:T(8,128)S(1)}, u32[]{:S(2)}, u32[]{:S(2)}) collective-permute-start(f32[4,2,16,32]{3,2,0,1:T(8,128)S(1)} %pad_maximum_fusion.5), channel_id=1, source_target_pairs={{4,0},{8,4},{12,8},{5,1},{9,5},{13,9},{6,2},{10,6},{14,10},{7,3},{... | collective-permute-start | bytes 49160 | tf_op jit(solution)/shard_map/ppermute | solution.py:30
  76.2 3.4 %collective-permute-done.2 = f32[4,2,16,32]{3,2,0,1:T(8,128)S(1)} collective-permute-done((f32[4,2,16,32]{3,2,0,1:T(8,128)S(1)}, f32[4,2,16,32]{3,2,0,1:T(8,128)S(1)}, u32[]{:S(2)}, u32[]{:S(2)}) %collective-permute-start.2) | collective-permute-done | bytes 16416 | tf_op jit(solution)/shard_map/ppermute | solution.py:30
  79.7 3.2 %collective-permute-start.3 = (f32[4,2,48,16]{3,2,0,1:T(8,128)S(1)}, f32[4,2,48,16]{3,2,0,1:T(8,128)S(1)}, u32[]{:S(2)}, u32[]{:S(2)}) collective-permute-start(f32[4,2,48,16]{3,2,0,1:T(8,128)S(1)} %get-tuple-element.46), channel_id=1, source_target_pairs={{0,1},{1,2},{2,3},{4,5},{5,6},{6,7},{8,9},{9,10},{10,11},{12,13},{... | collective-permute-start | bytes 73736 | tf_op jit(solution)/shard_map/ppermute | solution.py:28
  82.9 2.8 %collective-permute-start.4 = (f32[4,2,48,16]{3,2,0,1:T(8,128)S(1)}, f32[4,2,48,16]{3,2,0,1:T(8,128)S(1)}, u32[]{:S(2)}, u32[]{:S(2)}) collective-permute-start(f32[4,2,48,16]{3,2,0,1:T(8,128)S(1)} %get-tuple-element.47), channel_id=1, source_target_pairs={{1,0},{2,1},{3,2},{5,4},{6,5},{7,6},{9,8},{10,9},{11,10},{13,12},{... | collective-permute-start | bytes 73736 | tf_op jit(solution)/shard_map/ppermute | solution.py:30
  85.8 2.8 %collective-permute-done.3 = f32[4,2,48,16]{3,2,0,1:T(8,128)S(1)} collective-permute-done((f32[4,2,48,16]{3,2,0,1:T(8,128)S(1)}, f32[4,2,48,16]{3,2,0,1:T(8,128)S(1)}, u32[]{:S(2)}, u32[]{:S(2)}) %collective-permute-start.3) | collective-permute-done | bytes 24608 | tf_op jit(solution)/shard_map/ppermute | solution.py:28
  88.7 2.9 %collective-permute-done.4 = f32[4,2,48,16]{3,2,0,1:T(8,128)S(1)} collective-permute-done((f32[4,2,48,16]{3,2,0,1:T(8,128)S(1)}, f32[4,2,48,16]{3,2,0,1:T(8,128)S(1)}, u32[]{:S(2)}, u32[]{:S(2)}) %collective-permute-start.4) | collective-permute-done | bytes 24608 | tf_op jit(solution)/shard_map/ppermute | solution.py:30
  95.3 0.8 fusion.55
  97.7 0.8 add_sqrt_fusion
  99.8 0.8 fusion.12
  100.7 0.8 fusion.33
  101.5 0.8 fusion.29
  102.3 0.8 fusion.1
  103.9 1.0 fusion
  104.9 0.8 fusion.46
  105.7 0.8 fusion.4
  (47 shorter events, 10.8 us)
Async XLA Ops:
  0.6 4.4 %copy-start = (s32[64,2]{0,1:T(2,128)S(1)}, s32[64,2]{0,1:T(2,128)}, u32[]{:S(2)}) copy-start(s32[64,2]{0,1:T(2,128)} %param.5) | copy-start | bytes 1540
  3.1 16.5 %collective-permute-start = (f32[3,2,80,640]{3,2,1,0:T(8,128)}, f32[3,2,80,640]{3,2,1,0:T(8,128)}, u32[]{:S(2)}, u32[]{:S(2)}) collective-permute-start(f32[3,2,80,640]{3,2,1,0:T(8,128)} %slice.167), channel_id=1, source_target_pairs={{16,0},{32,16},{48,32},{64,48},{80,64},{96,80},{112,96},{128,112},... | collective-permute-start | bytes 3686408 | tf_op jit(solution)/shard_map/ppermute | solution.py:17
  70.0 6.2 %collective-permute-start.1 = (f32[4,2,16,32]{3,2,0,1:T(8,128)S(1)}, f32[4,2,16,32]{3,2,0,1:T(8,128)S(1)}, u32[]{:S(2)}, u32[]{:S(2)}) collective-permute-start(f32[4,2,16,32]{3,2,0,1:T(8,128)S(1)} %pad_maximum_fusion.5), channel_id=1, source_target_pairs={{0,4},{4,8},{8,12},{1,5},{5,9},{9,13},{2,6},{6,10},{10,14},{3,7},{... | collective-permute-start | bytes 49160 | tf_op jit(solution)/shard_map/ppermute | solution.py:28
  73.1 6.5 %collective-permute-start.2 = (f32[4,2,16,32]{3,2,0,1:T(8,128)S(1)}, f32[4,2,16,32]{3,2,0,1:T(8,128)S(1)}, u32[]{:S(2)}, u32[]{:S(2)}) collective-permute-start(f32[4,2,16,32]{3,2,0,1:T(8,128)S(1)} %pad_maximum_fusion.5), channel_id=1, source_target_pairs={{4,0},{8,4},{12,8},{5,1},{9,5},{13,9},{6,2},{10,6},{14,10},{7,3},{... | collective-permute-start | bytes 49160 | tf_op jit(solution)/shard_map/ppermute | solution.py:30
  79.7 8.9 %collective-permute-start.3 = (f32[4,2,48,16]{3,2,0,1:T(8,128)S(1)}, f32[4,2,48,16]{3,2,0,1:T(8,128)S(1)}, u32[]{:S(2)}, u32[]{:S(2)}) collective-permute-start(f32[4,2,48,16]{3,2,0,1:T(8,128)S(1)} %get-tuple-element.46), channel_id=1, source_target_pairs={{0,1},{1,2},{2,3},{4,5},{5,6},{6,7},{8,9},{9,10},{10,11},{12,13},{... | collective-permute-start | bytes 73736 | tf_op jit(solution)/shard_map/ppermute | solution.py:28
  82.9 8.6 %collective-permute-start.4 = (f32[4,2,48,16]{3,2,0,1:T(8,128)S(1)}, f32[4,2,48,16]{3,2,0,1:T(8,128)S(1)}, u32[]{:S(2)}, u32[]{:S(2)}) collective-permute-start(f32[4,2,48,16]{3,2,0,1:T(8,128)S(1)} %get-tuple-element.47), channel_id=1, source_target_pairs={{1,0},{2,1},{3,2},{5,4},{6,5},{7,6},{9,8},{10,9},{11,10},{13,12},{... | collective-permute-start | bytes 73736 | tf_op jit(solution)/shard_map/ppermute | solution.py:30
where the time goes:
time: 110 us; the launch traced here: 108 us
  local copies, waits for them, and re-layouts  42 us (38%)
  waiting for transfers between devices  22.3 us (20%)
  other arithmetic  17.5 us (16%)
  starting transfers between devices  13.8 us (13%)
  matrix products  11.9 us (11%)
    ppermute x1, waiting for transfers between devices, passed_along(): return lax.ppermute(x, axis, pairs)  12.9 us
    reduce_sum x4, other arithmetic, look_means(): return shaped.mean(axis=(2, 4))  11.6 us
    add x1, local copies, waits for them, and re-layouts, cross_terms(): primary[:, 0] * secondary[:, 0] + primary[:, 1] * secondary[:, 1]  7.69 us
    add x1, local copies, waits for them, and re-layouts, finish(): primary[:, 0] * primary[:, 0] + primary[:, 1] * primary[:, 1]  7.64 us
    add x1, local copies, waits for them, and re-layouts, cross_terms(): secondary[:, 0] * secondary[:, 0] + secondary[:, 1] * secondary[:, 1]  7.64 us
    sub x1, local copies, waits for them, and re-layouts, cross_terms(): primary[:, 1] * secondary[:, 0] - primary[:, 0] * secondary[:, 1]  7.62 us
    dot_general x8, matrix products, along_second(): jnp.einsum('lv,niujv->niujl', matrix, values, precision=lax.Precision.HIG...  6.37 us
    ppermute x2, waiting for transfers between devices, padded(): lax.ppermute(head, axis, [((i + 1) % count, i) for i in range(ends)])  6.33 us
  transfers between devices with their start and end apart: 5, of which 5 were waited for; matrix products, arithmetic and copies ran while one was open for 2% of the time, Pallas kernels for 0%

commit v1 on v0

v1 whole, which is shorter than its diff:
```python
import functools
import math

import jax
import jax.numpy as jnp
import numpy as np
from jax import lax
from jax.experimental import pallas as pl
from jax.experimental.pallas import tpu as pltpu
from jax.sharding import PartitionSpec as P

SPAN = 3
LOOK_R = 5
LOOK_C = 20
PATCH = 32
HALF = PATCH // 2
PAIRS_DEV = 4
F32 = jnp.float32
BF16 = jnp.bfloat16


def split_const(matrix):
    hi = matrix.astype(jnp.bfloat16)
    lo = (matrix - hi.astype(np.float64)).astype(jnp.bfloat16)
    return hi, lo


def taper(v):
    return np.where(v < HALF, (v + 0.5) / HALF, (PATCH - 0.5 - v) / HALF)


def look_table():
    x = np.arange(640)[:, None] // LOOK_C
    n = np.arange(256)[None, :]
    return (x == (n // 128) * HALF + n % HALF).astype(np.float64)


def row_forward():
    i, k, q, row = np.meshgrid(np.arange(2), np.arange(PATCH), np.arange(2), np.arange(48), indexing="ij")
    u = row - HALF * i
    angle = 2 * np.pi * k * u / PATCH
    value = np.where(q == 0, np.cos(angle), -np.sin(angle)) * ((u >= 0) & (u < PATCH))
    return value.reshape(64, 96)


def col_forward():
    h, c, p, v, c2, p2, l = np.meshgrid(
        np.arange(2), np.arange(2), np.arange(4), np.arange(HALF), np.arange(2), np.arange(4), np.arange(PATCH),
        indexing="ij",
    )
    angle = 2 * np.pi * l * (HALF * h + v) / PATCH
    value = np.where(c == c2, np.cos(angle), np.where(c == 1, np.sin(angle), -np.sin(angle)))
    return (value * (p == p2)).reshape(256, 256)


def neighbour_sum():
    a = np.arange(128)[:, None]
    b = np.arange(128)[None, :]
    d = (a - b) % PATCH
    return ((a // PATCH == b // PATCH) & ((d <= 1) | (d == PATCH - 1))).astype(np.float64)


def row_back():
    c2, r, c, i, k = np.meshgrid(
        np.arange(2), np.arange(HALF), np.arange(2), np.arange(2), np.arange(PATCH), indexing="ij"
    )
    u = r + HALF * (1 - i)
    angle = 2 * np.pi * k * u / PATCH
    value = np.where(c == c2, np.cos(angle), np.where(c2 == 0, -np.sin(angle), np.sin(angle))) * taper(u)
    return value.reshape(32, 128)


def col_back():
    j, p, l, q, p2, c = np.meshgrid(
        np.arange(3), np.arange(4), np.arange(PATCH), np.arange(2), np.arange(4), np.arange(PATCH), indexing="ij"
    )
    v = c + HALF - HALF * j
    angle = 2 * np.pi * l * v / PATCH
    value = np.where(q == 0, np.cos(angle), np.sin(angle)) * taper(v) * ((v >= 0) & (v < PATCH)) * (p == p2)
    return (value / (PATCH * PATCH)).reshape(384, 256)


def split(x):
    hi = x.astype(BF16)
    return hi, (x - hi.astype(F32)).astype(BF16)


def mm(a, b):
    return jnp.dot(a, b, preferred_element_type=F32)


def looks_kernel(idx_ref, stack_ref, recv_ref, table_ref, left_ref, right_ref, coh_ref, held, sem):
    copies = []
    for t in range(5):
        lanes = pl.ds(128 * t, 128)
        copies.append(pltpu.make_async_copy(stack_ref.at[:, :, :, lanes], held.at[0:4, :, t], sem.at[0, t]))
        copies.append(pltpu.make_async_copy(recv_ref.at[:, :, :, lanes], held.at[4:7, :, t], sem.at[1, t]))
    for copy in copies:
        copy.start()
    for copy in copies:
        copy.wait()

    def rows(acq, comp, k):
        tiles = [held[acq, comp, t, pl.ds(k, 16, stride=LOOK_R), :] for t in range(5)]
        return jnp.concatenate(tiles, axis=1)

    planes = []
    for p in range(PAIRS_DEV):
        a = idx_ref[2 * p]
        b = idx_ref[2 * p + 1]
        real = imag = power_a = power_b = None
        for k in range(LOOK_R):
            ar, ai, br, bi = rows(a, 0, k), rows(a, 1, k), rows(b, 0, k), rows(b, 1, k)
            terms = (ar * br + ai * bi, ai * br - ar * bi, ar * ar + ai * ai, br * br + bi * bi)
            if k == 0:
                real, imag, power_a, power_b = terms
            else:
                real, imag, power_a, power_b = (
                    real + terms[0], imag + terms[1], power_a + terms[2], power_b + terms[3],
                )
        planes += [real, imag, power_a, power_b]
    total = jnp.concatenate(planes, axis=0)
    hi, rest = total.astype(BF16), None
    rest = total - hi.astype(F32)
    mid = rest.astype(BF16)
    low = (rest - mid.astype(F32)).astype(BF16)
    table = table_ref[...]
    cells = (mm(hi, table) + (mm(mid, table) + mm(low, table))) * (1.0 / (LOOK_R * LOOK_C))
    cells = cells.reshape(PAIRS_DEV, 4, 16, 256)
    lane = lax.broadcasted_iota(jnp.int32, (16, 128), 1)
    group = lane // HALF
    left = jnp.zeros((16, 128), F32)
    right = jnp.zeros((16, 128), F32)
    for p in range(PAIRS_DEV):
        for comp in range(2):
            here = group == comp * PAIRS_DEV + p
            left = jnp.where(here, cells[p, comp, :, :128], left)
            right = jnp.where(here, cells[p, comp, :, 128:], right)
        whole = jnp.where((lane < HALF)[None], cells[p, :, :, :128], cells[p, :, :, 128:])
        magnitude = jnp.sqrt(whole[0] * whole[0] + whole[1] * whole[1])
        coherence = magnitude / jnp.sqrt((whole[2] + 1e-06) * (whole[3] + 1e-06))
        coh_ref[p] = coherence[:, :PATCH]
    left_ref[...] = left
    right_ref[...] = right


def looks(idx, stack, recv):
    table = jnp.asarray(look_table().astype(jnp.bfloat16))
    return pl.pallas_call(
        looks_kernel,
        out_shape=(
            jax.ShapeDtypeStruct((16, 128), F32),
            jax.ShapeDtypeStruct((16, 128), F32),
            jax.ShapeDtypeStruct((PAIRS_DEV, 16, 32), F32),
        ),
        in_specs=[
            pl.BlockSpec(memory_space=pltpu.SMEM),
            pl.BlockSpec(memory_space=pl.ANY),
            pl.BlockSpec(memory_space=pl.ANY),
            pl.BlockSpec(memory_space=pltpu.VMEM),
        ],
        out_specs=[pl.BlockSpec(memory_space=pltpu.VMEM)] * 3,
        scratch_shapes=[pltpu.VMEM((7, 2, 5, 80, 128), F32), pltpu.SemaphoreType.DMA((2, 5))],
        compiler_params=pltpu.CompilerParams(vmem_limit_bytes=24 * 2**20),
    )(idx, stack, recv, table)


def goldstein_kernel(
    edge_ref, up_ref, mid_ref, down_ref, rf_ref, cf_ref, ns_ref, rb_ref, cb_ref, out_ref
):
    up = jnp.where(edge_ref[0] == 0, 0.0, up_ref[...])
    down = jnp.where(edge_ref[1] == 0, 0.0, down_ref[...])
    x = jnp.concatenate([up, mid_ref[...], down], axis=0)
    lane = lax.broadcasted_iota(jnp.int32, (48, 128), 1)
    sign = jnp.where(lane < 64, -1.0, 1.0)
    turned = [pltpu.roll(x[:, 128 * b : 128 * b + 128], 64, 1) * sign for b in range(4)]
    xx = jnp.concatenate([x, jnp.concatenate(turned, axis=1)], axis=0)
    xh, xl = split(xx)
    rh, rl = rf_ref[0], rf_ref[1]
    y = mm(rh, xh) + (mm(rh, xl) + mm(rl, xh))
    ys = jnp.concatenate([y[:, 128 * j : 128 * j + 256] for j in range(3)], axis=0)
    yh, yl = split(ys)
    ch, cl = cf_ref[0], cf_ref[1]
    z = mm(yh, ch) + (mm(yl, ch) + mm(yh, cl))
    zr, zi = z[:, :128], z[:, 128:]
    magnitude = jnp.sqrt(zr * zr + zi * zi)
    mh, ml = split(magnitude)
    across = mm(mh, ns_ref[...]) + mm(ml, ns_ref[...])
    grouped = across.reshape(6, PATCH, 128)
    down_one = jnp.concatenate([grouped[:, PATCH - 1 :], grouped[:, : PATCH - 1]], axis=1)
    up_one = jnp.concatenate([grouped[:, 1:], grouped[:, :1]], axis=1)
    smooth = (grouped + (down_one + up_one)).reshape(192, 128)
    response = jnp.sqrt(smooth * (1.0 / 9.0)) * (1.0 / PATCH)
    fr, fi = zr * response, zi * response
    w = jnp.concatenate(
        [
            jnp.concatenate([fr[64 * j : 64 * j + 64] for j in range(3)], axis=1),
            jnp.concatenate([fi[64 * j : 64 * j + 64] for j in range(3)], axis=1),
        ],
        axis=0,
    )
    wh, wl = split(w)
    bh, bl = rb_ref[0], rb_ref[1]
    t = mm(bh, wh) + (mm(bh, wl) + mm(bl, wh))
    th, tl = split(t)
    gh, gl = cb_ref[0], cb_ref[1]
    o = mm(th, gh) + (mm(tl, gh) + mm(th, gl))
    real = o[:16, :128] - o[16:, 128:]
    imag = o[16:, :128] + o[:16, 128:]
    for p in range(PAIRS_DEV):
        out_ref[p, 0] = real[:, PATCH * p : PATCH * p + PATCH]
        out_ref[p, 1] = imag[:, PATCH * p : PATCH * p + PATCH]


def goldstein(edges, up, mid, down):
    def pair_of(matrix):
        return jnp.asarray(np.stack(split_const(matrix)))

    tables = (
        pair_of(row_forward()),
        pair_of(col_forward()),
        jnp.asarray(neighbour_sum().astype(jnp.bfloat16)),
        pair_of(row_back()),
        pair_of(col_back()),
    )
    vmem = pl.BlockSpec(memory_space=pltpu.VMEM)
    return pl.pallas_call(
        goldstein_kernel,
        out_shape=jax.ShapeDtypeStruct((PAIRS_DEV, 2, 16, 32), F32),
        in_specs=[pl.BlockSpec(memory_space=pltpu.SMEM)] + [vmem] * 8,
        out_specs=vmem,
        compiler_params=pltpu.CompilerParams(vmem_limit_bytes=24 * 2**20),
    )(edges, up, mid, down, *tables)


def fetch(x, axis, by):
    size = lax.axis_size(axis)
    return lax.ppermute(x, axis, [((i + by) % size, i) for i in range(size)])


def shards(stack, pair_list):
    date = lax.axis_index("date")
    row = lax.axis_index("row")
    col = lax.axis_index("col")
    following = fetch(stack[:SPAN], "date", 1)
    idx = lax.dynamic_slice_in_dim(pair_list, date * PAIRS_DEV, PAIRS_DEV, 0) - date * PAIRS_DEV
    left, right, coherence = looks(idx.reshape(-1), stack, following)
    before = jnp.where(col == 0, 0.0, fetch(right, "col", -1))
    after = jnp.where(col == lax.axis_size("col") - 1, 0.0, fetch(left, "col", 1))
    mid = jnp.concatenate([before, left, right, after], axis=1)
    up = fetch(mid, "row", -1)
    down = fetch(mid, "row", 1)
    edges = jnp.stack([row, lax.axis_size("row") - 1 - row]).astype(jnp.int32)
    return goldstein(edges, up, mid, down), coherence


def solution(mesh):
    in_specs = (P("date", None, "row", "col"), P())
    out_specs = (P("date", None, "row", "col"), P("date", "row", "col"))
    return jax.shard_map(shards, mesh=mesh, in_specs=in_specs, out_specs=out_specs, check_vma=False)
```

time: 110 us -> 43.6 us (0.40)
  the two profiles are of different devices: /device:TPU:148 before, /device:TPU:14 now
where the time goes in v1:
time: 43.6 us; the launch traced here: 43.3 us
  waiting for transfers between devices  20.7 us (47%)
  starting transfers between devices  9.35 us (21%)
  local copies, waits for them, and re-layouts  6.96 us (16%)
  Pallas kernels  4.74 us (11%)
  other arithmetic  0.87 us (2%)
  between operations  0.69 us (2%)
    ppermute x5, waiting for transfers between devices, fetch(): return lax.ppermute(x, axis, [((i + by) % size, i) for i in range(size)])  20.7 us
    ppermute x5, starting transfers between devices, fetch(): return lax.ppermute(x, axis, [((i + by) % size, i) for i in range(size)])  9.35 us
    unnamed x20, local copies, waits for them, and re-layouts  3.7 us
    slice x1, local copies, waits for them, and re-layouts, shards(): following = fetch(stack[:SPAN], 'date', 1)  2.56 us
    pallas_call x1, Pallas kernels, looks(): pl.pallas_call(looks_kernel, out_shape=(jax.ShapeDtypeStruct((16, 128), F...  2.37 us
    pallas_call x1, Pallas kernels, goldstein(): pl.pallas_call(goldstein_kernel, out_shape=jax.ShapeDtypeStruct((PAIRS_DE...  2.37 us
  transfers between devices with their start and end apart: 5, of which 5 were waited for; matrix products, arithmetic and copies ran while one was open for 2% of the time, Pallas kernels for 0%

profile of v1, /device:TPU:14, one launch (start us, length us, event | category | flops | bytes accessed | tf_op | source)
XLA Modules:
  0.0 43.3 jit_solution(15918526103575195895)
XLA Ops:
  0.6 0.0 copy-start
  0.6 0.0 copy-start.9
  0.6 2.6 %slice.3 = f32[3,2,80,640]{3,2,1,0:T(8,128)} slice(f32[4,2,80,640]{3,2,1,0:T(8,128)} %stack_ref.1), slice={[0:3], [0:2], [0:80], [0:640]} | slice | bytes 2457600 | tf_op jit(solution)/shard_map/slice | solution.py:245
  3.2 5.3 %collective-permute-start = (f32[3,2,80,640]{3,2,1,0:T(8,128)}, f32[3,2,80,640]{3,2,1,0:T(8,128)S(1)}, u32[]{:S(2)}, u32[]{:S(2)}) collective-permute-start(f32[3,2,80,640]{3,2,1,0:T(8,128)} %slice.3), channel_id=1, source_target_pairs={{16,0},{32,16},{48,32},{64,48},{80,64},{96,80},{112,96},{128,112},... | collective-permute-start | bytes 3686408 | tf_op jit(solution)/shard_map/ppermute | solution.py:238
  8.5 0.0 copy-done.9
  8.5 0.1 dynamic-slice_subtract_fusion
  8.6 0.1 copy.11
  8.7 0.6 %reshape.7.idx_ref = s32[8]{0:T(128)} reshape(s32[4,2]{1,0:T(4,128)S(1)} %copy.11) | data formatting | bytes 64 | tf_op jit(solution)/shard_map/reshape | solution.py:247
  9.3 13.8 %collective-permute-done.recv_ref = f32[3,2,80,640]{3,2,1,0:T(8,128)S(1)} collective-permute-done((f32[3,2,80,640]{3,2,1,0:T(8,128)}, f32[3,2,80,640]{3,2,1,0:T(8,128)S(1)}, u32[]{:S(2)}, u32[]{:S(2)}) %collective-permute-start) | collective-permute-done | bytes 1228832 | tf_op jit(solution)/shard_map/ppermute | solution.py:238
  23.1 0.0 copy-done
  23.1 1.0 %copy-done.2 = bf16[640,256]{1,0:T(8,128)(2,1)S(1)} copy-done((bf16[640,256]{1,0:T(8,128)(2,1)S(1)}, bf16[640,256]{1,0:T(8,128)(2,1)}, u32[]{:S(2)}) %copy-start.2) | copy-done | bytes 327704
  24.1 0.7 %copy-done.8 = s32[8]{0:T(128)S(1)} copy-done((s32[8]{0:T(128)S(1)}, s32[8]{0:T(128)}, u32[]{:S(2)}) %copy-start.8) | copy-done | bytes 56
  24.7 2.4 %shard_map.95 = (f32[16,128]{1,0:T(8,128)S(1)}, f32[16,128]{1,0:T(8,128)}, f32[4,16,32]{2,1,0:T(8,128)}) custom-call(s32[8]{0:T(128)S(1)} %copy-done.8, f32[4,2,80,640]{3,2,1,0:T(8,128)S(1)} %copy-done, f32[3,2,80,640]{3,2,1,0:T(8,128)S(1)} %collective-permute-done.recv_ref, bf16[640,256]{1,0:T(8,128)(2,1)S(1)} %copy-done.2), custom_call_target="tpu_custom_call" | custom-call | tf_op jit(solution)/shard_map/pallas_call | solution.py:149
  27.1 0.0 copy-start.7
  27.1 0.6 %copy-done.7 = f32[16,128]{1,0:T(8,128)} copy-done((f32[16,128]{1,0:T(8,128)}, f32[16,128]{1,0:T(8,128)S(1)}, u32[]{:S(2)}) %copy-start.7) | copy-done | bytes 8216
  27.7 1.6 %collective-permute-start.1 = (f32[16,128]{1,0:T(8,128)}, f32[16,128]{1,0:T(8,128)S(1)}, u32[]{:S(2)}, u32[]{:S(2)}) collective-permute-start(f32[16,128]{1,0:T(8,128)} %get-tuple-element.5), channel_id=1, source_target_pairs={{3,0},{0,1},{1,2},{2,3},{7,4},{4,5},{5,6},{6,7},{11,8},{8,9},{9,10... | collective-permute-start | bytes 24584 | tf_op jit(solution)/shard_map/ppermute | solution.py:238
  29.3 0.4 %collective-permute-start.2 = (f32[16,128]{1,0:T(8,128)}, f32[16,128]{1,0:T(8,128)S(1)}, u32[]{:S(2)}, u32[]{:S(2)}) collective-permute-start(f32[16,128]{1,0:T(8,128)} %copy-done.7), channel_id=1, source_target_pairs={{1,0},{2,1},{3,2},{0,3},{5,4},{6,5},{7,6},{4,7},{9,8},{10,9},{11,1... | collective-permute-start | bytes 24584 | tf_op jit(solution)/shard_map/ppermute | solution.py:238
  29.7 1.8 %collective-permute-done.1 = f32[16,128]{1,0:T(8,128)S(1)} collective-permute-done((f32[16,128]{1,0:T(8,128)}, f32[16,128]{1,0:T(8,128)S(1)}, u32[]{:S(2)}, u32[]{:S(2)}) %collective-permute-start.1) | collective-permute-done | bytes 8224 | tf_op jit(solution)/shard_map/ppermute | solution.py:238
  31.6 1.6 %collective-permute-done.2 = f32[16,128]{1,0:T(8,128)S(1)} collective-permute-done((f32[16,128]{1,0:T(8,128)}, f32[16,128]{1,0:T(8,128)S(1)}, u32[]{:S(2)}, u32[]{:S(2)}) %collective-permute-start.2) | collective-permute-done | bytes 8224 | tf_op jit(solution)/shard_map/ppermute | solution.py:238
  33.1 0.7 %pad_maximum_fusion.mid_ref = f32[16,512]{1,0:T(8,128)S(1)} fusion(f32[16,128]{1,0:T(8,128)S(1)} %broadcast_select_fusion, f32[16,128]{1,0:T(8,128)} %get-tuple-element.5, f32[16,128]{1,0:T(8,128)} %copy-done.7, f32[16,128]{1,0:T(8,128)S(1)} %broadcast_select_fusion.1), kind=kLoop, calls=%fused_computation | loop fusion | flops 24576 | bytes 65536 | tf_op jit(solution)/shard_map/concatenate | solution.py:250
  33.8 0.5 %collective-permute-start.3 = (f32[16,512]{1,0:T(8,128)S(1)}, f32[16,512]{1,0:T(8,128)S(1)}, u32[]{:S(2)}, u32[]{:S(2)}) collective-permute-start(f32[16,512]{1,0:T(8,128)S(1)} %pad_maximum_fusion.mid_ref), channel_id=1, source_target_pairs={{12,0},{0,4},{4,8},{8,12},{13,1},{1,5},{5,9},{9,13},{14,2},{2,6},{... | collective-permute-start | bytes 98312 | tf_op jit(solution)/shard_map/ppermute | solution.py:238
  34.3 1.5 %collective-permute-start.4 = (f32[16,512]{1,0:T(8,128)S(1)}, f32[16,512]{1,0:T(8,128)S(1)}, u32[]{:S(2)}, u32[]{:S(2)}) collective-permute-start(f32[16,512]{1,0:T(8,128)S(1)} %pad_maximum_fusion.mid_ref), channel_id=1, source_target_pairs={{4,0},{8,4},{12,8},{0,12},{5,1},{9,5},{13,9},{1,13},{6,2},{10,6},{... | collective-permute-start | bytes 98312 | tf_op jit(solution)/shard_map/ppermute | solution.py:238
  35.9 0.1 pad_add_fusion.edge_ref
  35.9 1.8 %collective-permute-done.3.up_ref = f32[16,512]{1,0:T(8,128)S(1)} collective-permute-done((f32[16,512]{1,0:T(8,128)S(1)}, f32[16,512]{1,0:T(8,128)S(1)}, u32[]{:S(2)}, u32[]{:S(2)}) %collective-permute-start.3) | collective-permute-done | bytes 32800 | tf_op jit(solution)/shard_map/ppermute | solution.py:238
  37.8 1.7 %collective-permute-done.4.down_ref = f32[16,512]{1,0:T(8,128)S(1)} collective-permute-done((f32[16,512]{1,0:T(8,128)S(1)}, f32[16,512]{1,0:T(8,128)S(1)}, u32[]{:S(2)}, u32[]{:S(2)}) %collective-permute-start.4) | collective-permute-done | bytes 32800 | tf_op jit(solution)/shard_map/ppermute | solution.py:238
  39.5 0.0 copy-done.1
  39.5 0.0 copy-done.3
  39.5 0.0 copy-done.4
  39.5 0.0 copy-start.5
  39.5 0.7 %copy-done.5 = bf16[128,128]{1,0:T(8,128)(2,1)S(1)} copy-done((bf16[128,128]{1,0:T(8,128)(2,1)S(1)}, bf16[128,128]{1,0:T(8,128)(2,1)}, u32[]{:S(2)}) %copy-start.5) | copy-done | bytes 32792
  40.2 0.7 %copy-done.6 = bf16[2,32,128]{2,1,0:T(8,128)(2,1)S(1)} copy-done((bf16[2,32,128]{2,1,0:T(8,128)(2,1)S(1)}, bf16[2,32,128]{2,1,0:T(8,128)(2,1)}, u32[]{:S(2)}) %copy-start.6) | copy-done | bytes 16408
  40.9 2.4 %shard_map.96 = f32[4,2,16,32]{3,2,1,0:T(8,128)} custom-call(s32[2]{0:T(128)S(1)} %pad_add_fusion.edge_ref, f32[16,512]{1,0:T(8,128)S(1)} %collective-permute-done.3.up_ref, f32[16,512]{1,0:T(8,128)S(1)} %pad_maximum_fusion.mid_ref, f32[16,512]{1,0:T(8,128)S(1)} %collective-permute-done.4.down_ref, bf16[2,64,96]{2,1,0:T(8,128)(2,1)S(1)} %copy-done.4, ...), custom_call_target="tpu_custom_call" | custom-call | tf_op jit(solution)/shard_map/pallas_call | solution.py:227
  (8 shorter events, 0.0 us)
Async XLA Ops:
  0.6 22.4 %copy-start = (f32[4,2,80,640]{3,2,1,0:T(8,128)S(1)}, f32[4,2,80,640]{3,2,1,0:T(8,128)}, u32[]{:S(2)}) copy-start(f32[4,2,80,640]{3,2,1,0:T(8,128)} %stack_ref.1) | copy-start | bytes 4915204
  0.6 7.9 %copy-start.9 = (s32[64,2]{0,1:T(2,128)S(1)}, s32[64,2]{0,1:T(2,128)}, u32[]{:S(2)}) copy-start(s32[64,2]{0,1:T(2,128)} %param.9) | copy-start | bytes 1540
  3.2 19.9 %collective-permute-start = (f32[3,2,80,640]{3,2,1,0:T(8,128)}, f32[3,2,80,640]{3,2,1,0:T(8,128)S(1)}, u32[]{:S(2)}, u32[]{:S(2)}) collective-permute-start(f32[3,2,80,640]{3,2,1,0:T(8,128)} %slice.3), channel_id=1, source_target_pairs={{16,0},{32,16},{48,32},{64,48},{80,64},{96,80},{112,96},{128,112},... | collective-permute-start | bytes 3686408 | tf_op jit(solution)/shard_map/ppermute | solution.py:238
  9.3 30.2 %copy-start.1 = (bf16[2,384,256]{2,1,0:T(8,128)(2,1)S(1)}, bf16[2,384,256]{2,1,0:T(8,128)(2,1)}, u32[]{:S(2)}) copy-start(bf16[2,384,256]{2,1,0:T(8,128)(2,1)} %constant.39.clone.cb_ref) | copy-start | bytes 1179652
  23.1 1.0 %copy-start.2 = (bf16[640,256]{1,0:T(8,128)(2,1)S(1)}, bf16[640,256]{1,0:T(8,128)(2,1)}, u32[]{:S(2)}) copy-start(bf16[640,256]{1,0:T(8,128)(2,1)} %constant.34.clone.table_ref) | copy-start | bytes 983044
  24.1 0.7 %copy-start.8 = (s32[8]{0:T(128)S(1)}, s32[8]{0:T(128)}, u32[]{:S(2)}) copy-start(s32[8]{0:T(128)} %reshape.7.idx_ref) | copy-start | bytes 100
  24.7 14.7 %copy-start.3 = (bf16[2,256,256]{2,1,0:T(8,128)(2,1)S(1)}, bf16[2,256,256]{2,1,0:T(8,128)(2,1)}, u32[]{:S(2)}) copy-start(bf16[2,256,256]{2,1,0:T(8,128)(2,1)} %constant.36.clone.cf_ref) | copy-start | bytes 786436
  24.7 14.7 %copy-start.4 = (bf16[2,64,96]{2,1,0:T(8,128)(2,1)S(1)}, bf16[2,64,96]{2,1,0:T(8,128)(2,1)}, u32[]{:S(2)}) copy-start(bf16[2,64,96]{2,1,0:T(8,128)(2,1)} %constant.35.clone.rf_ref) | copy-start | bytes 73732
  27.1 0.6 %copy-start.7 = (f32[16,128]{1,0:T(8,128)}, f32[16,128]{1,0:T(8,128)S(1)}, u32[]{:S(2)}) copy-start(f32[16,128]{1,0:T(8,128)S(1)} %get-tuple-element.6) | copy-start | bytes 24580
  27.7 3.9 %collective-permute-start.1 = (f32[16,128]{1,0:T(8,128)}, f32[16,128]{1,0:T(8,128)S(1)}, u32[]{:S(2)}, u32[]{:S(2)}) collective-permute-start(f32[16,128]{1,0:T(8,128)} %get-tuple-element.5), channel_id=1, source_target_pairs={{3,0},{0,1},{1,2},{2,3},{7,4},{4,5},{5,6},{6,7},{11,8},{8,9},{9,10... | collective-permute-start | bytes 24584 | tf_op jit(solution)/shard_map/ppermute | solution.py:238
  29.3 3.9 %collective-permute-start.2 = (f32[16,128]{1,0:T(8,128)}, f32[16,128]{1,0:T(8,128)S(1)}, u32[]{:S(2)}, u32[]{:S(2)}) collective-permute-start(f32[16,128]{1,0:T(8,128)} %copy-done.7), channel_id=1, source_target_pairs={{1,0},{2,1},{3,2},{0,3},{5,4},{6,5},{7,6},{4,7},{9,8},{10,9},{11,1... | collective-permute-start | bytes 24584 | tf_op jit(solution)/shard_map/ppermute | solution.py:238
  33.8 3.9 %collective-permute-start.3 = (f32[16,512]{1,0:T(8,128)S(1)}, f32[16,512]{1,0:T(8,128)S(1)}, u32[]{:S(2)}, u32[]{:S(2)}) collective-permute-start(f32[16,512]{1,0:T(8,128)S(1)} %pad_maximum_fusion.mid_ref), channel_id=1, source_target_pairs={{12,0},{0,4},{4,8},{8,12},{13,1},{1,5},{5,9},{9,13},{14,2},{2,6},{... | collective-permute-start | bytes 98312 | tf_op jit(solution)/shard_map/ppermute | solution.py:238
  34.3 5.1 %collective-permute-start.4 = (f32[16,512]{1,0:T(8,128)S(1)}, f32[16,512]{1,0:T(8,128)S(1)}, u32[]{:S(2)}, u32[]{:S(2)}) collective-permute-start(f32[16,512]{1,0:T(8,128)S(1)} %pad_maximum_fusion.mid_ref), channel_id=1, source_target_pairs={{4,0},{8,4},{12,8},{0,12},{5,1},{9,5},{13,9},{1,13},{6,2},{10,6},{... | collective-permute-start | bytes 98312 | tf_op jit(solution)/shard_map/ppermute | solution.py:238
  39.5 0.8 %copy-start.5 = (bf16[128,128]{1,0:T(8,128)(2,1)S(1)}, bf16[128,128]{1,0:T(8,128)(2,1)}, u32[]{:S(2)}) copy-start(bf16[128,128]{1,0:T(8,128)(2,1)} %constant.37.clone.ns_ref) | copy-start | bytes 98308
  40.2 0.7 %copy-start.6 = (bf16[2,32,128]{2,1,0:T(8,128)(2,1)S(1)}, bf16[2,32,128]{2,1,0:T(8,128)(2,1)}, u32[]{:S(2)}) copy-start(bf16[2,32,128]{2,1,0:T(8,128)(2,1)} %constant.38.clone.rb_ref) | copy-start | bytes 49156

commit v2 on v1

v2 whole, which is shorter than its diff:
```python
import functools
import math

import jax
import jax.numpy as jnp
import numpy as np
from jax import lax
from jax.experimental import pallas as pl
from jax.experimental.pallas import tpu as pltpu
from jax.sharding import PartitionSpec as P

SPAN = 3
LOOK_R = 5
LOOK_C = 20
PATCH = 32
HALF = PATCH // 2
PAIRS_DEV = 4
F32 = jnp.float32
BF16 = jnp.bfloat16


def taper(v):
    return np.where(v < HALF, (v + 0.5) / HALF, (PATCH - 0.5 - v) / HALF)


def whole_part(x, divisor):
    return (x.astype(F32) * (1.0 / divisor) + 0.5 / divisor).astype(jnp.int32)


def look_table():
    lane = lax.broadcasted_iota(jnp.int32, (384, 256), 0)
    n = lax.broadcasted_iota(jnp.int32, (384, 256), 1)
    left = jnp.where(lane < 256, lane, 256 + lane % 64)
    right = jnp.where(lane < 256, 64 + lane, lane % 64)
    cell = whole_part(jnp.where(n < 128, left, right), LOOK_C)
    return (cell == n % HALF).astype(F32).astype(BF16)


def row_forward():
    i, k, q, row = np.meshgrid(np.arange(2), np.arange(PATCH), np.arange(2), np.arange(48), indexing="ij")
    u = row - HALF * i
    angle = 2 * np.pi * k * u / PATCH
    value = np.where(q == 0, np.cos(angle), -np.sin(angle)) * ((u >= 0) & (u < PATCH))
    return value.reshape(64, 96)


def col_forward():
    h, c, p, v, c2, p2, l = np.meshgrid(
        np.arange(2), np.arange(2), np.arange(4), np.arange(HALF), np.arange(2), np.arange(4), np.arange(PATCH),
        indexing="ij",
    )
    angle = 2 * np.pi * l * (HALF * h + v) / PATCH
    value = np.where(c == c2, np.cos(angle), np.where(c == 1, np.sin(angle), -np.sin(angle)))
    return (value * (p == p2)).reshape(256, 256)


def neighbour_sum():
    a = lax.broadcasted_iota(jnp.int32, (128, 128), 0)
    b = lax.broadcasted_iota(jnp.int32, (128, 128), 1)
    d = (a - b) & (PATCH - 1)
    near = (d <= 1) | (d == PATCH - 1)
    return (near & ((a & -PATCH) == (b & -PATCH))).astype(F32).astype(BF16)


def row_back():
    c2, r, c, i, k = np.meshgrid(
        np.arange(2), np.arange(HALF), np.arange(2), np.arange(2), np.arange(PATCH), indexing="ij"
    )
    u = r + HALF * (1 - i)
    angle = 2 * np.pi * k * u / PATCH
    value = np.where(c == c2, np.cos(angle), np.where(c2 == 0, -np.sin(angle), np.sin(angle))) * taper(u)
    return value.reshape(32, 128)


def col_back():
    j, p, l, q, p2, c = np.meshgrid(
        np.arange(3), np.arange(4), np.arange(PATCH), np.arange(2), np.arange(4), np.arange(PATCH), indexing="ij"
    )
    v = c + HALF - HALF * j
    angle = 2 * np.pi * l * v / PATCH
    value = np.where(q == 0, np.cos(angle), np.sin(angle)) * taper(v) * ((v >= 0) & (v < PATCH)) * (p == p2)
    return (value / (PATCH * PATCH)).reshape(384, 256)


def split(x):
    hi = x.astype(BF16)
    return hi, (x - hi.astype(F32)).astype(BF16)


def mm(a, b):
    return jnp.dot(a, b, preferred_element_type=F32)


def half_copies(stack_ref, first, out_ref, tile, sem, slot):
    count = out_ref.shape[0]
    return [
        pltpu.make_async_copy(
            stack_ref.at[first : first + count, comp, :, pl.ds(128 * (tile + t), 128)],
            out_ref.at[:, 2 * comp + t],
            sem.at[slot, 2 * comp + t],
        )
        for comp in range(2)
        for t in range(2)
    ]


def lower_lanes(shape):
    return lax.broadcasted_iota(jnp.int32, shape, len(shape) - 1) % 128 < 64


def fill_mixed(mid_ref, acq, left_ref, left_at, right_ref, right_at):
    real, imag = mid_ref[acq, 0], mid_ref[acq, 1]
    lower = lower_lanes(real.shape)
    if left_at is not None:
        left_ref[left_at, 4] = jnp.where(lower, real, pltpu.roll(imag, 64, 1))
    if right_at is not None:
        right_ref[right_at, 4] = jnp.where(lower, pltpu.roll(real, 64, 1), imag)


def pack_kernel(stack_ref, up_ref, down_ref, middle, sem):
    copies = [pltpu.make_async_copy(stack_ref.at[:, :, :, pl.ds(256, 128)], middle, sem.at[2, 0])]
    copies += half_copies(stack_ref, 0, up_ref, 0, sem, 0)
    copies += half_copies(stack_ref, 1, down_ref, 3, sem, 1)
    for copy in copies:
        copy.start()
    copies[0].wait()
    for acq in range(4):
        fill_mixed(middle, acq, up_ref, acq if acq < 3 else None, down_ref, acq - 1 if acq > 0 else None)
    for copy in copies[1:]:
        copy.wait()


def pack(stack):
    vmem = pl.BlockSpec(memory_space=pltpu.VMEM)
    half = jax.ShapeDtypeStruct((SPAN, 5, 80, 128), F32)
    return pl.pallas_call(
        pack_kernel,
        out_shape=(half, half),
        in_specs=[pl.BlockSpec(memory_space=pl.ANY)],
        out_specs=(vmem, vmem),
        scratch_shapes=[pltpu.VMEM((4, 2, 80, 128), F32), pltpu.SemaphoreType.DMA((3, 4))],
    )(stack)


def cross(a_ref, a, b_ref, b):
    real, imag = [0.0] * 3, [0.0] * 3
    for k in range(LOOK_R):
        rows = pl.ds(k, 16, stride=LOOK_R)
        x = [a_ref[a, t, rows, :] for t in range(5)]
        y = [b_ref[b, t, rows, :] for t in range(5)]
        for t in range(2):
            real[t] += x[t] * y[t] + x[t + 2] * y[t + 2]
            imag[t] += x[t + 2] * y[t] - x[t] * y[t + 2]
        real[2] += x[4] * y[4]
        imag[2] += x[4] * pltpu.roll(y[4], 64, 1)
    imag[2] = jnp.where(lower_lanes((16, 128)), -imag[2], imag[2])
    return jnp.concatenate(real, axis=1), jnp.concatenate(imag, axis=1)


def power(a_ref, a):
    total = [0.0] * 3
    for k in range(LOOK_R):
        x = [a_ref[a, t, pl.ds(k, 16, stride=LOOK_R), :] for t in range(5)]
        for t in range(2):
            total[t] += x[t] * x[t] + x[t + 2] * x[t + 2]
        total[2] += x[4] * x[4]
    return jnp.concatenate(total, axis=1)


def pooled(planes, table):
    high, low = split(jnp.concatenate(planes, axis=0))
    cells = (mm(high, table) + mm(low, table)) * (1.0 / (LOOK_R * LOOK_C))
    return cells.reshape(len(planes), 16, 256)


def pair_lanes():
    return lax.broadcasted_iota(jnp.int32, (16, 128), 1) // HALF


def message(cells, offset):
    group = pair_lanes()
    out = jnp.zeros((16, 128), F32)
    for p in range(PAIRS_DEV):
        for comp in range(2):
            value = cells[2 * p + comp, :, offset : offset + 128]
            out = jnp.where(group == comp * PAIRS_DEV + p, value, out)
    return out


def crossing_lanes(list_ref, date):
    group = pair_lanes() % PAIRS_DEV
    out = jnp.zeros((16, 128), jnp.int32)
    for p in range(PAIRS_DEV):
        second = list_ref[1, PAIRS_DEV * date + p] - 4 * date
        out = jnp.where(group == p, (second >= 4).astype(jnp.int32), out)
    return out == 1


def early_kernel(list_ref, stack_ref, trig_ref, *refs):
    left_ref, right_ref, power_ref, keep_l, keep_r, look_out, ns_out = refs[:7]
    rf_out, cf_out, rb_out, cb_out = refs[7:11]
    middle, sem = refs[11:]
    copies = [pltpu.make_async_copy(stack_ref.at[:, :, :, pl.ds(256, 128)], middle, sem.at[2, 0])]
    copies += half_copies(stack_ref, 0, keep_l, 0, sem, 0)
    copies += half_copies(stack_ref, 0, keep_r, 3, sem, 1)
    for copy in copies:
        copy.start()
    table = look_table()
    look_out[...] = table
    ns_out[...] = neighbour_sum()
    for source, target in (
        (trig_ref[:256], cf_out),
        (trig_ref[256:640], cb_out),
        (trig_ref[640:704, :96], rf_out),
        (trig_ref[640:672, 128:], rb_out),
    ):
        high, low = split(source)
        target[0] = high
        target[1] = low
    copies[0].wait()
    for acq in range(4):
        fill_mixed(middle, acq, keep_l, acq, keep_r, acq)
    for copy in copies[1:]:
        copy.wait()
    date = lax.axis_index("date")
    planes_l, planes_r = [], []
    for p in range(PAIRS_DEV):
        a = list_ref[0, PAIRS_DEV * date + p] - 4 * date
        b = jnp.minimum(list_ref[1, PAIRS_DEV * date + p] - 4 * date, 3)
        planes_l += cross(keep_l, a, keep_l, b)
        planes_r += cross(keep_r, a, keep_r, b)
    for acq in range(4):
        planes_l.append(power(keep_l, acq))
        planes_r.append(power(keep_r, acq))
    cells_l = pooled(planes_l, table)
    cells_r = pooled(planes_r, table)
    left_ref[...] = message(cells_l, 0)
    right_ref[...] = message(cells_r, 128)
    first = pair_lanes() % 2 == 0
    for acq in range(4):
        power_ref[acq] = jnp.where(first, cells_l[8 + acq, :, :128], cells_r[8 + acq, :, 128:])


def early(listed, stack):
    vmem = pl.BlockSpec(memory_space=pltpu.VMEM)
    smem = pl.BlockSpec(memory_space=pltpu.SMEM)
    trig = np.zeros((704, 256))
    trig[:256] = col_forward()
    trig[256:640] = col_back()
    trig[640:704, :96] = row_forward()
    trig[640:672, 128:] = row_back()
    message_shape = jax.ShapeDtypeStruct((16, 128), F32)
    half = jax.ShapeDtypeStruct((4, 5, 80, 128), F32)
    out_shape = (
        [message_shape, message_shape, jax.ShapeDtypeStruct((4, 16, 128), F32), half, half]
        + [jax.ShapeDtypeStruct(shape, BF16) for shape in ((384, 256), (128, 128))]
        + [
            jax.ShapeDtypeStruct((2,) + shape, BF16)
            for shape in ((64, 96), (256, 256), (32, 128), (384, 256))
        ]
    )
    return pl.pallas_call(
        early_kernel,
        out_shape=out_shape,
        in_specs=[smem, pl.BlockSpec(memory_space=pl.ANY), vmem],
        out_specs=[vmem] * len(out_shape),
        scratch_shapes=[pltpu.VMEM((4, 2, 80, 128), F32), pltpu.SemaphoreType.DMA((3, 4))],
        compiler_params=pltpu.CompilerParams(vmem_limit_bytes=24 * 2**20),
        cost_estimate=pl.CostEstimate(flops=10**9, bytes_accessed=10**7, transcendentals=0),
    )(listed, stack, jnp.asarray(trig, F32))


def late_kernel(
    list_ref, up_ref, down_ref, keep_l, keep_r, table_ref, left_in, left_ref, right_ref
):
    date = lax.axis_index("date")
    before = lax.rem(date + lax.axis_size("date") - 1, lax.axis_size("date"))
    planes_l, planes_r = [], []
    for p in range(PAIRS_DEV):
        own, other = PAIRS_DEV * date + p, PAIRS_DEV * before + p
        a = jnp.clip(list_ref[0, own] - 4 * date, 0, 3)
        b = jnp.clip(list_ref[1, own] - 4 * date - 4, 0, 2)
        planes_l += cross(keep_l, a, up_ref, b)
        a = jnp.clip(list_ref[0, other] - 4 * before - 1, 0, 2)
        b = jnp.clip(list_ref[1, other] - 4 * before - 4, 0, 3)
        planes_r += cross(down_ref, a, keep_r, b)
    cells = pooled(planes_l + planes_r, table_ref[...])
    crossing = crossing_lanes(list_ref, date)
    left_ref[...] = jnp.where(crossing, message(cells[:8], 0), left_in[...])
    right_ref[...] = message(cells[8:], 128)


def late(listed, up, down, keep_l, keep_r, table, left):
    vmem = pl.BlockSpec(memory_space=pltpu.VMEM)
    smem = pl.BlockSpec(memory_space=pltpu.SMEM)
    shape = jax.ShapeDtypeStruct((16, 128), F32)
    return pl.pallas_call(
        late_kernel,
        out_shape=(shape, shape),
        in_specs=[smem] + [vmem] * 6,
        out_specs=(vmem, vmem),
        compiler_params=pltpu.CompilerParams(vmem_limit_bytes=24 * 2**20),
    )(listed, up, down, keep_l, keep_r, table, left)


def merge_kernel(
    list_ref, before_late, before_early, left_ref, right_late, right_early, after_ref, mid_ref
):
    crossing = crossing_lanes(list_ref, lax.axis_index("date"))
    col = lax.axis_index("col")
    before = jnp.where(crossing, before_late[...], before_early[...])
    mid_ref[:, :128] = jnp.where(col == 0, 0.0, before)
    mid_ref[:, 128:256] = left_ref[...]
    mid_ref[:, 256:384] = jnp.where(crossing, right_late[...], right_early[...])
    mid_ref[:, 384:] = jnp.where(col == lax.axis_size("col") - 1, 0.0, after_ref[...])


def merge(listed, *parts):
    vmem = pl.BlockSpec(memory_space=pltpu.VMEM)
    smem = pl.BlockSpec(memory_space=pltpu.SMEM)
    return pl.pallas_call(
        merge_kernel,
        out_shape=jax.ShapeDtypeStruct((16, 512), F32),
        in_specs=[smem] + [vmem] * 6,
        out_specs=vmem,
        compiler_params=pltpu.CompilerParams(vmem_limit_bytes=8 * 2**20),
    )(listed, *parts)


def coherence_kernel(list_ref, mid_ref, own_ref, next_ref, out_ref):
    date = lax.axis_index("date")
    left, right = mid_ref[:, 128:256], mid_ref[:, 256:384]
    first = pair_lanes() % 2 == 0

    def whole(group):
        shift = 128 - HALF * group
        a = left if group == 0 else pltpu.roll(left, shift, 1)
        return jnp.where(first, a, pltpu.roll(right, (shift + HALF) % 128, 1))

    for p in range(PAIRS_DEV):
        a = list_ref[0, PAIRS_DEV * date + p] - 4 * date
        b = list_ref[1, PAIRS_DEV * date + p] - 4 * date
        real, imag = whole(p), whole(PAIRS_DEV + p)
        power_a = own_ref[a]
        power_b = jnp.where(b >= 4, next_ref[jnp.maximum(b - 4, 0)], own_ref[jnp.minimum(b, 3)])
        magnitude = jnp.sqrt(real * real + imag * imag)
        out_ref[p] = (magnitude / jnp.sqrt((power_a + 1e-06) * (power_b + 1e-06)))[:, :PATCH]


def coherences(listed, mid, own, following):
    vmem = pl.BlockSpec(memory_space=pltpu.VMEM)
    smem = pl.BlockSpec(memory_space=pltpu.SMEM)
    return pl.pallas_call(
        coherence_kernel,
        out_shape=jax.ShapeDtypeStruct((PAIRS_DEV, 16, 32), F32),
        in_specs=[smem] + [vmem] * 3,
        out_specs=vmem,
        compiler_params=pltpu.CompilerParams(vmem_limit_bytes=8 * 2**20),
        cost_estimate=pl.CostEstimate(flops=10**8, bytes_accessed=10**6, transcendentals=0),
    )(listed, mid, own, following)


def goldstein_kernel(
    up_ref, mid_ref, down_ref, rf_ref, cf_ref, ns_ref, rb_ref, cb_ref, out_ref
):
    row = lax.axis_index("row")
    up = jnp.where(row == 0, 0.0, up_ref[...])
    down = jnp.where(row == lax.axis_size("row") - 1, 0.0, down_ref[...])
    x = jnp.concatenate([up, mid_ref[...], down], axis=0)
    lane = lax.broadcasted_iota(jnp.int32, (48, 128), 1)
    sign = jnp.where(lane < 64, -1.0, 1.0)
    turned = [pltpu.roll(x[:, 128 * b : 128 * b + 128], 64, 1) * sign for b in range(4)]
    xx = jnp.concatenate([x, jnp.concatenate(turned, axis=1)], axis=0)
    xh, xl = split(xx)
    rh, rl = rf_ref[0], rf_ref[1]
    y = mm(rh, xh) + (mm(rh, xl) + mm(rl, xh))
    ys = jnp.concatenate([y[:, 128 * j : 128 * j + 256] for j in range(3)], axis=0)
    yh, yl = split(ys)
    ch, cl = cf_ref[0], cf_ref[1]
    z = mm(yh, ch) + (mm(yl, ch) + mm(yh, cl))
    zr, zi = z[:, :128], z[:, 128:]
    magnitude = jnp.sqrt(zr * zr + zi * zi)
    mh, ml = split(magnitude)
    across = mm(mh, ns_ref[...]) + mm(ml, ns_ref[...])
    grouped = across.reshape(6, PATCH, 128)
    down_one = jnp.concatenate([grouped[:, PATCH - 1 :], grouped[:, : PATCH - 1]], axis=1)
    up_one = jnp.concatenate([grouped[:, 1:], grouped[:, :1]], axis=1)
    smooth = (grouped + (down_one + up_one)).reshape(192, 128)
    response = jnp.sqrt(smooth * (1.0 / 9.0)) * (1.0 / PATCH)
    fr, fi = zr * response, zi * response
    w = jnp.concatenate(
        [
            jnp.concatenate([fr[64 * j : 64 * j + 64] for j in range(3)], axis=1),
            jnp.concatenate([fi[64 * j : 64 * j + 64] for j in range(3)], axis=1),
        ],
        axis=0,
    )
    wh, wl = split(w)
    bh, bl = rb_ref[0], rb_ref[1]
    t = mm(bh, wh) + (mm(bh, wl) + mm(bl, wh))
    th, tl = split(t)
    gh, gl = cb_ref[0], cb_ref[1]
    o = mm(th, gh) + (mm(tl, gh) + mm(th, gl))
    real = o[:16, :128] - o[16:, 128:]
    imag = o[16:, :128] + o[:16, 128:]
    for p in range(PAIRS_DEV):
        out_ref[p, 0] = real[:, PATCH * p : PATCH * p + PATCH]
        out_ref[p, 1] = imag[:, PATCH * p : PATCH * p + PATCH]


def goldstein(up, mid, down, *tables):
    vmem = pl.BlockSpec(memory_space=pltpu.VMEM)
    return pl.pallas_call(
        goldstein_kernel,
        out_shape=jax.ShapeDtypeStruct((PAIRS_DEV, 2, 16, 32), F32),
        in_specs=[vmem] * 8,
        out_specs=vmem,
        compiler_params=pltpu.CompilerParams(vmem_limit_bytes=24 * 2**20),
    )(up, mid, down, *tables)


def shards(stack, pair_list):
    names = ("date", "row", "col")
    sizes = tuple(lax.axis_size(name) for name in names)
    cells = [(d, r, c) for d in range(sizes[0]) for r in range(sizes[1]) for c in range(sizes[2])]

    def fetch(x, *by):
        def index(at):
            d, r, c = ((i + j) % n for i, j, n in zip(at, by, sizes))
            return (d * sizes[1] + r) * sizes[2] + c

        return lax.ppermute(x, names, [(index(at), i) for i, at in enumerate(cells)])

    listed = pair_list.T
    up, down = pack(stack)
    up = fetch(up, 1, 0, 0)
    down = fetch(down, -1, 0, 0)
    left_early, right_early, own_power, keep_l, keep_r, look, near, rf, cf, rb, cb = early(listed, stack)
    before_early = fetch(right_early, 0, 0, -1)
    next_power = fetch(own_power, 1, 0, 0)
    left, right_out = late(listed, up, down, keep_l, keep_r, look, left_early)
    after = fetch(left, 0, 0, 1)
    before_late = fetch(right_out, 1, 0, -1)
    right_late = fetch(right_out, 1, 0, 0)
    mid = merge(listed, before_late, before_early, left, right_late, right_early, after)
    above = fetch(mid, 0, -1, 0)
    below = fetch(mid, 0, 1, 0)
    coherence = coherences(listed, mid, own_power, next_power)
    return goldstein(above, mid, below, rf, cf, near, rb, cb), coherence


def solution(mesh):
    in_specs = (P("date", None, "row", "col"), P())
    out_specs = (P("date", None, "row", "col"), P("date", "row", "col"))
    return jax.shard_map(shards, mesh=mesh, in_specs=in_specs, out_specs=out_specs, check_vma=False)
```

time: 43.6 us -> 36.8 us (0.84)
  the two profiles are of different devices: /device:TPU:14 before, /device:TPU:1 now
where the time goes in v2:
time: 36.8 us; the launch traced here: 36.7 us
  starting transfers between devices  19.9 us (54%)
  Pallas kernels  9.38 us (25%)
  waiting for transfers between devices  5.67 us (15%)
  local copies, waits for them, and re-layouts  1.11 us (3%)
  between operations  0.7 us (2%)
    ppermute x9, starting transfers between devices, fetch(): lax.ppermute(x, names, [(index(at), i) for i, at in enumerate(cells)])  19.9 us
    ppermute x9, waiting for transfers between devices, fetch(): lax.ppermute(x, names, [(index(at), i) for i, at in enumerate(cells)])  5.67 us
    pallas_call x1, Pallas kernels, pack(): pl.pallas_call(pack_kernel, out_shape=(half, half), in_specs=[pl.BlockSpe...  2.61 us
    pallas_call x1, Pallas kernels, early(): pl.pallas_call(early_kernel, out_shape=out_shape, in_specs=[smem, pl.Bloc...  1.94 us
    pallas_call x1, Pallas kernels, goldstein(): pl.pallas_call(goldstein_kernel, out_shape=jax.ShapeDtypeStruct((PAIRS_DE...  1.83 us
    pallas_call x1, Pallas kernels, coherences(): pl.pallas_call(coherence_kernel, out_shape=jax.ShapeDtypeStruct((PAIRS_DE...  1.27 us
    pallas_call x1, Pallas kernels, late(): pl.pallas_call(late_kernel, out_shape=(shape, shape), in_specs=[smem] + [...  1.16 us
    unnamed x6, local copies, waits for them, and re-layouts  1.11 us
  transfers between devices with their start and end apart: 9, of which 3 were waited for; matrix products, arithmetic and copies ran while one was open for 0% of the time, Pallas kernels for 13%

profile of v2, /device:TPU:1, one launch (start us, length us, event | category | flops | bytes accessed | tf_op | source)
XLA Modules:
  0.0 36.7 jit_solution(2881672977671340)
XLA Ops:
  0.6 0.0 copy-start
  0.6 0.0 copy-start.1
  0.6 2.6 %shard_map.50 = (f32[3,5,80,128]{3,2,1,0:T(8,128)}, f32[3,5,80,128]{3,2,1,0:T(8,128)}) custom-call(f32[4,2,80,640]{3,2,1,0:T(8,128)} %stack_ref.3), custom_call_target="tpu_custom_call" | custom-call | tf_op jit(solution)/shard_map/pallas_call | solution.py:136
  3.3 3.3 %collective-permute-start = (f32[3,5,80,128]{3,2,1,0:T(8,128)}, f32[3,5,80,128]{3,2,1,0:T(8,128)S(1)}, u32[]{:S(2)}, u32[]{:S(2)}) collective-permute-start(f32[3,5,80,128]{3,2,1,0:T(8,128)} %get-tuple-element.17), channel_id=1, source_target_pairs={{16,0},{17,1},{18,2},{19,3},{20,4},{21,5},{22,6},{23,7},{24,8},{25... | collective-permute-start | bytes 1843208 | tf_op jit(solution)/shard_map/ppermute | solution.py:432
  6.5 0.0 collective-permute-start.1
  6.5 0.0 copy-done
  6.5 0.0 copy-done.1
  6.5 0.0 copy-start.2
  6.5 1.1 %copy-done.2 = f32[704,256]{1,0:T(8,128)S(1)} copy-done((f32[704,256]{1,0:T(8,128)S(1)}, f32[704,256]{1,0:T(8,128)}, u32[]{:S(2)}) %copy-start.2) | copy-done | bytes 720920
  7.6 1.9 %shard_map.51 = (f32[16,128]{1,0:T(8,128)S(1)}, f32[16,128]{1,0:T(8,128)S(1)}, f32[4,16,128]{2,1,0:T(8,128)S(1)}, f32[4,5,80,128]{3,2,1,0:T(8,128)S(1)}, f32[4,5...) custom-call(s32[2,64]{1,0:T(2,128)S(1)} %bitcast.1, ...), custom_call_target="tpu_custom_call" | custom-call | flops 1000000000 | bytes 10000000 | tf_op jit(solution)/shard_map/pallas_call | solution.py:262
  9.6 3.6 %collective-permute-start.8 = (f32[4,16,128]{2,1,0:T(8,128)S(1)}, f32[4,16,128]{2,1,0:T(8,128)S(1)}, u32[]{:S(2)}, u32[]{:S(2)}) collective-permute-start(f32[4,16,128]{2,1,0:T(8,128)S(1)} %get-tuple-element.31.own_ref), channel_id=1, source_target_pairs={{16,0},{17,1},{18,2},{19,3},{20,4},{21,5},{22,6},{23,7},{24,8},{25... | collective-permute-start | bytes 98312 | tf_op jit(solution)/shard_map/ppermute | solution.py:432
  13.2 1.3 %collective-permute-start.3 = (f32[16,128]{1,0:T(8,128)S(1)}, f32[16,128]{1,0:T(8,128)S(1)}, u32[]{:S(2)}, u32[]{:S(2)}) collective-permute-start(f32[16,128]{1,0:T(8,128)S(1)} %get-tuple-element.24.right_early), channel_id=1, source_target_pairs={{3,0},{0,1},{1,2},{2,3},{7,4},{4,5},{5,6},{6,7},{11,8},{8,9},{9,10... | collective-permute-start | bytes 24584 | tf_op jit(solution)/shard_map/ppermute | solution.py:432
  14.5 0.2 collective-permute-done.up_ref
  14.6 0.0 collective-permute-done.1.down_ref
  14.6 1.2 %shard_map.52 = (f32[16,128]{1,0:T(8,128)S(1)}, f32[16,128]{1,0:T(8,128)S(1)}) custom-call(s32[2,64]{1,0:T(2,128)S(1)} %bitcast.2, f32[3,5,80,128]{3,2,1,0:T(8,128)S(1)} %collective-permute-done.up_ref, f32[3,5,80,128]{3,2,1,0:T(8,128)S(1)} %collective-permute-done.1.down_ref, f32[4,5,80,128]{3,2,1,0:T(8,128)S(1)} %get-tuple-element.19.keep_l, ...), custom_call_target="tpu_custom_call" | custom-call | tf_op jit(solution)/shard_map/pallas_call | solution.py:297
  15.8 6.4 %collective-permute-start.4 = (f32[16,128]{1,0:T(8,128)S(1)}, f32[16,128]{1,0:T(8,128)S(1)}, u32[]{:S(2)}, u32[]{:S(2)}) collective-permute-start(f32[16,128]{1,0:T(8,128)S(1)} %get-tuple-element.23), channel_id=1, source_target_pairs={{16,0},{17,1},{18,2},{19,3},{20,4},{21,5},{22,6},{23,7},{24,8},{25... | collective-permute-start | bytes 24584 | tf_op jit(solution)/shard_map/ppermute | solution.py:432
  22.3 1.3 %collective-permute-start.2 = (f32[16,128]{1,0:T(8,128)S(1)}, f32[16,128]{1,0:T(8,128)S(1)}, u32[]{:S(2)}, u32[]{:S(2)}) collective-permute-start(f32[16,128]{1,0:T(8,128)S(1)} %get-tuple-element.23), channel_id=1, source_target_pairs={{19,0},{16,1},{17,2},{18,3},{23,4},{20,5},{21,6},{22,7},{27,8},{24... | collective-permute-start | bytes 24584 | tf_op jit(solution)/shard_map/ppermute | solution.py:432
  23.5 1.5 %collective-permute-start.5 = (f32[16,128]{1,0:T(8,128)S(1)}, f32[16,128]{1,0:T(8,128)S(1)}, u32[]{:S(2)}, u32[]{:S(2)}) collective-permute-start(f32[16,128]{1,0:T(8,128)S(1)} %get-tuple-element.25.left_ref), channel_id=1, source_target_pairs={{1,0},{2,1},{3,2},{0,3},{5,4},{6,5},{7,6},{4,7},{9,8},{10,9},{11,1... | collective-permute-start | bytes 24584 | tf_op jit(solution)/shard_map/ppermute | solution.py:432
  25.0 0.0 collective-permute-done.3.before_early
  25.0 0.0 collective-permute-done.4.right_late
  25.0 2.4 %collective-permute-done.2.before_late = f32[16,128]{1,0:T(8,128)S(1)} collective-permute-done((f32[16,128]{1,0:T(8,128)S(1)}, f32[16,128]{1,0:T(8,128)S(1)}, u32[]{:S(2)}, u32[]{:S(2)}) %collective-permute-start.2) | collective-permute-done | bytes 8224 | tf_op jit(solution)/shard_map/ppermute | solution.py:432
  27.4 0.0 collective-permute-done.5.after_ref
  27.4 0.6 %shard_map.53.mid_ref = f32[16,512]{1,0:T(8,128)S(1)} custom-call(s32[2,64]{1,0:T(2,128)S(1)} %bitcast.3, f32[16,128]{1,0:T(8,128)S(1)} %collective-permute-done.2.before_late, f32[16,128]{1,0:T(8,128)S(1)} %collective-permute-done.3.before_early, f32[16,128]{1,0:T(8,128)S(1)} %get-tuple-element.25.left_ref, ...), custom_call_target="tpu_custom_call" | custom-call | tf_op jit(solution)/shard_map/pallas_call | solution.py:321
  28.0 2.6 %collective-permute-start.7 = (f32[16,512]{1,0:T(8,128)S(1)}, f32[16,512]{1,0:T(8,128)S(1)}, u32[]{:S(2)}, u32[]{:S(2)}) collective-permute-start(f32[16,512]{1,0:T(8,128)S(1)} %shard_map.53.mid_ref), channel_id=1, source_target_pairs={{4,0},{5,1},{6,2},{7,3},{8,4},{9,5},{10,6},{11,7},{12,8},{13,9},{1... | collective-permute-start | bytes 98312 | tf_op jit(solution)/shard_map/ppermute | solution.py:432
  30.6 0.0 collective-permute-start.6
  30.6 0.0 collective-permute-done.8.next_ref
  30.6 1.3 %shard_map.55 = f32[4,16,32]{2,1,0:T(8,128)} custom-call(s32[2,64]{1,0:T(2,128)S(1)} %bitcast.4, f32[16,512]{1,0:T(8,128)S(1)} %shard_map.53.mid_ref, f32[4,16,128]{2,1,0:T(8,128)S(1)} %get-tuple-element.31.own_ref, f32[4,16,128]{2,1,0:T(8,128)S(1)} %collective-permute-done.8.next_ref), custom_call_target="tpu_custom_call" | custom-call | flops 100000000 | bytes 1000000 | tf_op jit(solution)/shard_map/pallas_call | solution.py:353
  31.9 0.0 collective-permute-done.7.down_ref
  31.9 3.0 %collective-permute-done.6.up_ref = f32[16,512]{1,0:T(8,128)S(1)} collective-permute-done((f32[16,512]{1,0:T(8,128)S(1)}, f32[16,512]{1,0:T(8,128)S(1)}, u32[]{:S(2)}, u32[]{:S(2)}) %collective-permute-start.6) | collective-permute-done | bytes 32800 | tf_op jit(solution)/shard_map/ppermute | solution.py:432
  34.9 1.8 %shard_map.54 = f32[4,2,16,32]{3,2,1,0:T(8,128)} custom-call(f32[16,512]{1,0:T(8,128)S(1)} %collective-permute-done.6.up_ref, f32[16,512]{1,0:T(8,128)S(1)} %shard_map.53.mid_ref, f32[16,512]{1,0:T(8,128)S(1)} %collective-permute-done.7.down_ref, bf16[2,64,96]{2,1,0:T(8,128)(2,1)S(1)} %get-tuple-element.26.rf_ref, ...), custom_call_target="tpu_custom_call" | custom-call | tf_op jit(solution)/shard_map/pallas_call | solution.py:413
Async XLA Ops:
  0.6 5.9 %copy-start = (f32[4,2,80,640]{3,2,1,0:T(8,128)S(1)}, f32[4,2,80,640]{3,2,1,0:T(8,128)}, u32[]{:S(2)}) copy-start(f32[4,2,80,640]{3,2,1,0:T(8,128)} %stack_ref.3) | copy-start | bytes 4915204
  0.6 5.9 %copy-start.1 = (s32[64,2]{0,1:T(2,128)S(1)}, s32[64,2]{0,1:T(2,128)}, u32[]{:S(2)}) copy-start(s32[64,2]{0,1:T(2,128)} %param.4) | copy-start | bytes 1540
  3.3 11.4 %collective-permute-start = (f32[3,5,80,128]{3,2,1,0:T(8,128)}, f32[3,5,80,128]{3,2,1,0:T(8,128)S(1)}, u32[]{:S(2)}, u32[]{:S(2)}) collective-permute-start(f32[3,5,80,128]{3,2,1,0:T(8,128)} %get-tuple-element.17), channel_id=1, source_target_pairs={{16,0},{17,1},{18,2},{19,3},{20,4},{21,5},{22,6},{23,7},{24,8},{25... | collective-permute-start | bytes 1843208 | tf_op jit(solution)/shard_map/ppermute | solution.py:432
  6.5 8.1 %collective-permute-start.1 = (f32[3,5,80,128]{3,2,1,0:T(8,128)}, f32[3,5,80,128]{3,2,1,0:T(8,128)S(1)}, u32[]{:S(2)}, u32[]{:S(2)}) collective-permute-start(f32[3,5,80,128]{3,2,1,0:T(8,128)} %get-tuple-element.18), channel_id=1, source_target_pairs={{240,0},{241,1},{242,2},{243,3},{244,4},{245,5},{246,6},{247,7},{2... | collective-permute-start | bytes 1843208 | tf_op jit(solution)/shard_map/ppermute | solution.py:432
  6.5 1.1 %copy-start.2 = (f32[704,256]{1,0:T(8,128)S(1)}, f32[704,256]{1,0:T(8,128)}, u32[]{:S(2)}) copy-start(f32[704,256]{1,0:T(8,128)} %constant.2.clone.trig_ref) | copy-start | bytes 2162692
  9.6 21.0 %collective-permute-start.8 = (f32[4,16,128]{2,1,0:T(8,128)S(1)}, f32[4,16,128]{2,1,0:T(8,128)S(1)}, u32[]{:S(2)}, u32[]{:S(2)}) collective-permute-start(f32[4,16,128]{2,1,0:T(8,128)S(1)} %get-tuple-element.31.own_ref), channel_id=1, source_target_pairs={{16,0},{17,1},{18,2},{19,3},{20,4},{21,5},{22,6},{23,7},{24,8},{25... | collective-permute-start | bytes 98312 | tf_op jit(solution)/shard_map/ppermute | solution.py:432
  13.2 11.8 %collective-permute-start.3 = (f32[16,128]{1,0:T(8,128)S(1)}, f32[16,128]{1,0:T(8,128)S(1)}, u32[]{:S(2)}, u32[]{:S(2)}) collective-permute-start(f32[16,128]{1,0:T(8,128)S(1)} %get-tuple-element.24.right_early), channel_id=1, source_target_pairs={{3,0},{0,1},{1,2},{2,3},{7,4},{4,5},{5,6},{6,7},{11,8},{8,9},{9,10... | collective-permute-start | bytes 24584 | tf_op jit(solution)/shard_map/ppermute | solution.py:432
  15.8 9.2 %collective-permute-start.4 = (f32[16,128]{1,0:T(8,128)S(1)}, f32[16,128]{1,0:T(8,128)S(1)}, u32[]{:S(2)}, u32[]{:S(2)}) collective-permute-start(f32[16,128]{1,0:T(8,128)S(1)} %get-tuple-element.23), channel_id=1, source_target_pairs={{16,0},{17,1},{18,2},{19,3},{20,4},{21,5},{22,6},{23,7},{24,8},{25... | collective-permute-start | bytes 24584 | tf_op jit(solution)/shard_map/ppermute | solution.py:432
  22.3 5.2 %collective-permute-start.2 = (f32[16,128]{1,0:T(8,128)S(1)}, f32[16,128]{1,0:T(8,128)S(1)}, u32[]{:S(2)}, u32[]{:S(2)}) collective-permute-start(f32[16,128]{1,0:T(8,128)S(1)} %get-tuple-element.23), channel_id=1, source_target_pairs={{19,0},{16,1},{17,2},{18,3},{23,4},{20,5},{21,6},{22,7},{27,8},{24... | collective-permute-start | bytes 24584 | tf_op jit(solution)/shard_map/ppermute | solution.py:432
  23.5 3.9 %collective-permute-start.5 = (f32[16,128]{1,0:T(8,128)S(1)}, f32[16,128]{1,0:T(8,128)S(1)}, u32[]{:S(2)}, u32[]{:S(2)}) collective-permute-start(f32[16,128]{1,0:T(8,128)S(1)} %get-tuple-element.25.left_ref), channel_id=1, source_target_pairs={{1,0},{2,1},{3,2},{0,3},{5,4},{6,5},{7,6},{4,7},{9,8},{10,9},{11,1... | collective-permute-start | bytes 24584 | tf_op jit(solution)/shard_map/ppermute | solution.py:432
  28.0 3.8 %collective-permute-start.7 = (f32[16,512]{1,0:T(8,128)S(1)}, f32[16,512]{1,0:T(8,128)S(1)}, u32[]{:S(2)}, u32[]{:S(2)}) collective-permute-start(f32[16,512]{1,0:T(8,128)S(1)} %shard_map.53.mid_ref), channel_id=1, source_target_pairs={{4,0},{5,1},{6,2},{7,3},{8,4},{9,5},{10,6},{11,7},{12,8},{13,9},{1... | collective-permute-start | bytes 98312 | tf_op jit(solution)/shard_map/ppermute | solution.py:432
  30.6 4.3 %collective-permute-start.6 = (f32[16,512]{1,0:T(8,128)S(1)}, f32[16,512]{1,0:T(8,128)S(1)}, u32[]{:S(2)}, u32[]{:S(2)}) collective-permute-start(f32[16,512]{1,0:T(8,128)S(1)} %shard_map.53.mid_ref), channel_id=1, source_target_pairs={{12,0},{13,1},{14,2},{15,3},{0,4},{1,5},{2,6},{3,7},{4,8},{5,9},{6... | collective-permute-start | bytes 98312 | tf_op jit(solution)/shard_map/ppermute | solution.py:432

commit v3 on v2

v3 whole, which is shorter than its diff:
```python
import functools
import math

import jax
import jax.numpy as jnp
import numpy as np
from jax import lax
from jax.experimental import pallas as pl
from jax.experimental.pallas import tpu as pltpu
from jax.sharding import PartitionSpec as P

SPAN = 3
LOOK_R = 5
LOOK_C = 20
PATCH = 32
HALF = PATCH // 2
PAIRS_DEV = 4
F32 = jnp.float32
BF16 = jnp.bfloat16
HBM = pltpu.MemorySpace.HBM


def taper(v):
    return np.where(v < HALF, (v + 0.5) / HALF, (PATCH - 0.5 - v) / HALF)


def whole_part(x, divisor):
    return (x.astype(F32) * (1.0 / divisor) + 0.5 / divisor).astype(jnp.int32)


def look_table():
    lane = lax.broadcasted_iota(jnp.int32, (384, 256), 0)
    n = lax.broadcasted_iota(jnp.int32, (384, 256), 1)
    left = jnp.where(lane < 256, lane, 256 + lane % 64)
    right = jnp.where(lane < 256, 64 + lane, lane % 64)
    cell = whole_part(jnp.where(n < 128, left, right), LOOK_C)
    return (cell == n % HALF).astype(F32).astype(BF16)


def row_forward():
    i, k, q, row = np.meshgrid(np.arange(2), np.arange(PATCH), np.arange(2), np.arange(48), indexing="ij")
    u = row - HALF * i
    angle = 2 * np.pi * k * u / PATCH
    value = np.where(q == 0, np.cos(angle), -np.sin(angle)) * ((u >= 0) & (u < PATCH))
    return value.reshape(64, 96)


def col_forward():
    h, c, p, v, c2, p2, l = np.meshgrid(
        np.arange(2), np.arange(2), np.arange(4), np.arange(HALF), np.arange(2), np.arange(4), np.arange(PATCH),
        indexing="ij",
    )
    angle = 2 * np.pi * l * (HALF * h + v) / PATCH
    value = np.where(c == c2, np.cos(angle), np.where(c == 1, np.sin(angle), -np.sin(angle)))
    return (value * (p == p2)).reshape(256, 256)


def neighbour_sum():
    a = lax.broadcasted_iota(jnp.int32, (128, 128), 0)
    b = lax.broadcasted_iota(jnp.int32, (128, 128), 1)
    d = (a - b) & (PATCH - 1)
    near = (d <= 1) | (d == PATCH - 1)
    return (near & ((a & -PATCH) == (b & -PATCH))).astype(F32).astype(BF16)


def row_back():
    c2, r, c, i, k = np.meshgrid(
        np.arange(2), np.arange(HALF), np.arange(2), np.arange(2), np.arange(PATCH), indexing="ij"
    )
    u = r + HALF * (1 - i)
    angle = 2 * np.pi * k * u / PATCH
    value = np.where(c == c2, np.cos(angle), np.where(c2 == 0, -np.sin(angle), np.sin(angle))) * taper(u)
    return value.reshape(32, 128)


def col_back():
    j, p, l, q, p2, c = np.meshgrid(
        np.arange(3), np.arange(4), np.arange(PATCH), np.arange(2), np.arange(4), np.arange(PATCH), indexing="ij"
    )
    v = c + HALF - HALF * j
    angle = 2 * np.pi * l * v / PATCH
    value = np.where(q == 0, np.cos(angle), np.sin(angle)) * taper(v) * ((v >= 0) & (v < PATCH)) * (p == p2)
    return (value / (PATCH * PATCH)).reshape(384, 256)


def split(x):
    hi = x.astype(BF16)
    return hi, (x - hi.astype(F32)).astype(BF16)


def mm(a, b):
    return jnp.dot(a, b, preferred_element_type=F32)


def half_copies(stack_ref, first, out_ref, tile, sem, slot):
    count = out_ref.shape[0]
    return [
        pltpu.make_async_copy(
            stack_ref.at[first : first + count, comp, :, pl.ds(128 * (tile + t), 128)],
            out_ref.at[:, 2 * comp + t],
            sem.at[slot, 2 * comp + t],
        )
        for comp in range(2)
        for t in range(2)
    ]


def lower_lanes(shape):
    return lax.broadcasted_iota(jnp.int32, shape, len(shape) - 1) % 128 < 64


def mixed_tile(real, imag, right):
    turned = pltpu.roll(jnp.where(right, real, imag), 64, 1)
    return jnp.where(lower_lanes(real.shape) == right, turned, jnp.where(right, imag, real))


def half_pair(stack_ref, count, left_ref, right_ref, middle, sem):
    lanes = pl.ds(256, 128)
    copies = [pltpu.make_async_copy(stack_ref.at[:count, :, :, lanes], middle, sem.at[2, 0])]
    copies += half_copies(stack_ref, 0, left_ref, 0, sem, 0)
    copies += half_copies(stack_ref, 0, right_ref, 3, sem, 1)
    for copy in copies:
        copy.start()
    return copies


def half_pair_end(copies, count, left_ref, right_ref, middle):
    copies[0].wait()
    for acq in range(count):
        left_ref[acq, 4] = mixed_tile(middle[acq, 0], middle[acq, 1], False)
        right_ref[acq, 4] = mixed_tile(middle[acq, 0], middle[acq, 1], True)
    for copy in copies[1:]:
        copy.wait()


def odd_date():
    return lax.axis_index("date") % 2


def pack_kernel(half_ref, out_ref):
    odd = odd_date() == 1
    for acq in range(SPAN):
        tiles = [[half_ref[acq, comp, :, pl.ds(128 * t, 128)] for t in range(3)] for comp in range(2)]
        for comp in range(2):
            out_ref[acq, 2 * comp] = jnp.where(odd, tiles[comp][1], tiles[comp][0])
            out_ref[acq, 2 * comp + 1] = jnp.where(odd, tiles[comp][2], tiles[comp][1])
        real, imag = (jnp.where(odd, tiles[comp][0], tiles[comp][2]) for comp in range(2))
        out_ref[acq, 4] = mixed_tile(real, imag, odd)


def pack(half):
    vmem = pl.BlockSpec(memory_space=pltpu.VMEM)
    return pl.pallas_call(
        pack_kernel,
        out_shape=jax.ShapeDtypeStruct((SPAN, 5, 80, 128), F32),
        in_specs=[vmem],
        out_specs=vmem,
        compiler_params=pltpu.CompilerParams(vmem_limit_bytes=16 * 2**20),
    )(half)


def cross(a_ref, a, b_ref, b):
    real, imag = [0.0] * 3, [0.0] * 3
    for k in range(LOOK_R):
        rows = pl.ds(k, 16, stride=LOOK_R)
        x = [a_ref[a, t, rows, :] for t in range(5)]
        y = [b_ref[b, t, rows, :] for t in range(5)]
        for t in range(2):
            real[t] += x[t] * y[t] + x[t + 2] * y[t + 2]
            imag[t] += x[t + 2] * y[t] - x[t] * y[t + 2]
        real[2] += x[4] * y[4]
        imag[2] += x[4] * pltpu.roll(y[4], 64, 1)
    imag[2] = jnp.where(lower_lanes((16, 128)), -imag[2], imag[2])
    return jnp.concatenate(real, axis=1), jnp.concatenate(imag, axis=1)


def power(a_ref, a):
    total = [0.0] * 3
    for k in range(LOOK_R):
        x = [a_ref[a, t, pl.ds(k, 16, stride=LOOK_R), :] for t in range(5)]
        for t in range(2):
            total[t] += x[t] * x[t] + x[t + 2] * x[t + 2]
        total[2] += x[4] * x[4]
    return jnp.concatenate(total, axis=1)


def pooled(planes, table):
    high, low = split(jnp.concatenate(planes, axis=0))
    cells = (mm(high, table) + mm(low, table)) * (1.0 / (LOOK_R * LOOK_C))
    return cells.reshape(len(planes), 16, 256)


def pair_lanes():
    return lax.broadcasted_iota(jnp.int32, (16, 128), 1) // HALF


def message(cells, offset):
    group = pair_lanes()
    out = jnp.zeros((16, 128), F32)
    for p in range(PAIRS_DEV):
        for comp in range(2):
            value = cells[2 * p + comp, :, offset : offset + 128]
            out = jnp.where(group == comp * PAIRS_DEV + p, value, out)
    return out


def power_cells(left_cells, right_cells):
    return jnp.where(lower_lanes((16, 128)), left_cells[:, :128], right_cells[:, 128:])


def by_pair(values):
    group = pair_lanes() % PAIRS_DEV
    out = values[0]
    for p in range(1, PAIRS_DEV):
        out = jnp.where(group == p, values[p], out)
    return out


def pair_of(list_ref, group, p):
    return tuple(list_ref[i, PAIRS_DEV * group + p] - 4 * group for i in range(2))


def early_kernel(
    list_ref, stack_ref, left_ref, right_ref, first_ref, second_ref, back_ref, crossing_ref, index_ref, keep, look_out,
    powers, middle, sem,
):
    keep_l, keep_r = keep.at[0], keep.at[1]
    copies = half_pair(stack_ref, 4, keep_l, keep_r, middle, sem)
    table = look_table()
    look_out[...] = table
    date = lax.axis_index("date")
    odd = odd_date() == 1
    before = jnp.maximum(date - 1, 0)
    own = [pair_of(list_ref, date, p) for p in range(PAIRS_DEV)]
    others = [pair_of(list_ref, before, p) for p in range(PAIRS_DEV)]
    crossing_ref[...] = by_pair([jnp.full((16, 128), (b >= 4).astype(jnp.int32)) for a, b in own])
    lane = lax.broadcasted_iota(jnp.int32, (8, 128), 1)
    index = jnp.zeros((8, 128), jnp.int32)
    for p in range(PAIRS_DEV):
        mine = jnp.where(odd, own[p][0], jnp.clip(others[p][1] - 4, 0, 3))
        theirs = jnp.where(odd, jnp.clip(own[p][1] - 4, 0, 2), jnp.clip(others[p][0] - 1, 0, 2))
        index = jnp.where(lane == p, mine, jnp.where(lane == PAIRS_DEV + p, theirs, index))
    index_ref[...] = index
    half_pair_end(copies, 4, keep_l, keep_r, middle)
    planes_l, planes_r = [], []
    for a, b in own:
        planes_l += cross(keep_l, a, keep_l, jnp.minimum(b, 3))
        planes_r += cross(keep_r, a, keep_r, jnp.minimum(b, 3))
    for acq in range(4):
        planes_l.append(power(keep_l, acq))
        planes_r.append(power(keep_r, acq))
    cells_l = pooled(planes_l, table)
    cells_r = pooled(planes_r, table)
    left_ref[...] = message(cells_l, 0)
    right_ref[...] = message(cells_r, 128)
    for acq in range(4):
        powers[acq] = power_cells(cells_l[8 + acq], cells_r[8 + acq])
    first_ref[...] = by_pair([powers[a] for a, b in own])
    second_ref[...] = by_pair([powers[jnp.minimum(b, 3)] for a, b in own])
    back_ref[...] = by_pair([powers[jnp.clip(b - 4, 0, 3)] for a, b in others])


def early(listed, stack):
    vmem = pl.BlockSpec(memory_space=pltpu.VMEM)
    smem = pl.BlockSpec(memory_space=pltpu.SMEM)
    out_shape = [jax.ShapeDtypeStruct((16, 128), F32)] * 5 + [
        jax.ShapeDtypeStruct((16, 128), jnp.int32),
        jax.ShapeDtypeStruct((8, 128), jnp.int32),
        jax.ShapeDtypeStruct((2, 4, 5, 80, 128), F32),
        jax.ShapeDtypeStruct((384, 256), BF16),
    ]
    return pl.pallas_call(
        early_kernel,
        out_shape=out_shape,
        in_specs=[smem, pl.BlockSpec(memory_space=HBM)],
        out_specs=[vmem] * len(out_shape),
        scratch_shapes=[
            pltpu.VMEM((4, 16, 128), F32), pltpu.VMEM((4, 2, 80, 128), F32), pltpu.SemaphoreType.DMA((3, 4)),
        ],
        compiler_params=pltpu.CompilerParams(vmem_limit_bytes=24 * 2**20),
        cost_estimate=pl.CostEstimate(flops=10**9, bytes_accessed=10**7, transcendentals=0),
    )(listed, stack)


def chip_kernel(
    list_ref, other_ref, keep, table_ref, crossing_ref, left_in, right_in, second_in, left_ref, right_ref, second_ref,
    first_swap, second_swap, *scratch,
):
    left_ref[...] = left_in[...]
    right_ref[...] = right_in[...]
    second_ref[...] = second_in[...]

    @pl.when(odd_date() == 0)
    def _():
        other_l, other_r, powers, middle, sem = scratch
        copies = half_pair(other_ref, SPAN, other_l, other_r, middle, sem)
        half_pair_end(copies, SPAN, other_l, other_r, middle)
        date = lax.axis_index("date")
        planes_l, planes_r, seconds = [], [], []
        for p in range(PAIRS_DEV):
            a, b = pair_of(list_ref, date, p)
            seconds.append(jnp.maximum(b - 4, 0))
            planes_l += cross(keep.at[0], a, other_l, seconds[p])
            planes_r += cross(keep.at[1], a, other_r, seconds[p])
        for acq in range(SPAN):
            planes_l.append(power(other_l, acq))
            planes_r.append(power(other_r, acq))
        cells_l = pooled(planes_l, table_ref[...])
        cells_r = pooled(planes_r, table_ref[...])
        crossing = crossing_ref[...] == 1
        left_ref[...] = jnp.where(crossing, message(cells_l, 0), left_in[...])
        right_ref[...] = jnp.where(crossing, message(cells_r, 128), right_in[...])
        for acq in range(SPAN):
            powers[acq] = power_cells(cells_l[8 + acq], cells_r[8 + acq])
        second_ref[...] = jnp.where(crossing, by_pair([powers[b] for b in seconds]), second_in[...])

    odd_col = lax.axis_index("col") % 2 == 1
    left, right = left_ref[...], right_ref[...]
    first_swap[...] = jnp.where(odd_col, left, right)
    second_swap[...] = jnp.where(odd_col, right, left)


def within_chip(listed, other, *arrays):
    vmem = pl.BlockSpec(memory_space=pltpu.VMEM)
    half = pltpu.VMEM((SPAN, 5, 80, 128), F32)
    return pl.pallas_call(
        chip_kernel,
        out_shape=[jax.ShapeDtypeStruct((16, 128), F32)] * 5,
        in_specs=[pl.BlockSpec(memory_space=pltpu.SMEM), pl.BlockSpec(memory_space=HBM)] + [vmem] * 6,
        out_specs=[vmem] * 5,
        scratch_shapes=[
            half, half, pltpu.VMEM((SPAN, 16, 128), F32), pltpu.VMEM((SPAN, 2, 80, 128), F32),
            pltpu.SemaphoreType.DMA((3, 4)),
        ],
        compiler_params=pltpu.CompilerParams(vmem_limit_bytes=24 * 2**20),
        cost_estimate=pl.CostEstimate(flops=10**9, bytes_accessed=10**7, transcendentals=0),
    )(listed, other, *arrays)


def table_kernel(after_ref, trig_ref, ns_out, rf_out, cf_out, rb_out, cb_out):
    ns_out[...] = neighbour_sum()
    for source, target in (
        (trig_ref[:256], cf_out),
        (trig_ref[256:640], cb_out),
        (trig_ref[640:704, :96], rf_out),
        (trig_ref[640:672, 128:], rb_out),
    ):
        high, low = split(source)
        target[0] = high
        target[1] = low


def filter_tables(after):
    vmem = pl.BlockSpec(memory_space=pltpu.VMEM)
    trig = np.zeros((704, 256))
    trig[:256] = col_forward()
    trig[256:640] = col_back()
    trig[640:704, :96] = row_forward()
    trig[640:672, 128:] = row_back()
    out_shape = [jax.ShapeDtypeStruct((128, 128), BF16)] + [
        jax.ShapeDtypeStruct((2,) + shape, BF16) for shape in ((64, 96), (256, 256), (32, 128), (384, 256))
    ]
    return pl.pallas_call(
        table_kernel,
        out_shape=out_shape,
        in_specs=[vmem] * 2,
        out_specs=[vmem] * 5,
        compiler_params=pltpu.CompilerParams(vmem_limit_bytes=16 * 2**20),
        cost_estimate=pl.CostEstimate(flops=10**8, bytes_accessed=10**6, transcendentals=0),
    )(after, jnp.asarray(trig, F32))


def late_kernel(index_ref, other_ref, keep, table_ref, back_in, out_ref):
    odd = odd_date() == 1
    side = jnp.where(odd, 0, 1)
    index = index_ref[...]
    planes = []
    for p in range(PAIRS_DEV):
        planes += cross(keep.at[side], index[0, p], other_ref, index[0, PAIRS_DEV + p])
    cells = pooled(planes, table_ref[...])
    cells = jnp.where(odd, cells[:, :, :128], cells[:, :, 128:])
    new = message(cells, 0)
    out_ref[:16] = jnp.where(odd | lower_lanes((16, 128)), new, -new)
    out_ref[16:] = back_in[...]


def late(*arrays):
    vmem = pl.BlockSpec(memory_space=pltpu.VMEM)
    return pl.pallas_call(
        late_kernel,
        out_shape=jax.ShapeDtypeStruct((32, 128), F32),
        in_specs=[vmem] * 5,
        out_specs=vmem,
        compiler_params=pltpu.CompilerParams(vmem_limit_bytes=24 * 2**20),
    )(*arrays)


def merge_kernel(
    crossing_ref, before_late, left_late, right_late, after_late, first_ref, second_ref, left_early, right_early, mid_ref
):
    crossing = (crossing_ref[...] == 1) & (odd_date() == 1)
    col = lax.axis_index("col")
    odd_col = col % 2 == 1
    before = jnp.where(crossing, before_late[:16], jnp.where(odd_col, first_ref[...], second_ref[...]))
    after = jnp.where(crossing, after_late[:16], jnp.where(odd_col, second_ref[...], first_ref[...]))
    mid_ref[:, :128] = jnp.where(col == 0, 0.0, before)
    mid_ref[:, 128:256] = jnp.where(crossing, left_late[:16], left_early[...])
    mid_ref[:, 256:384] = jnp.where(crossing, right_late[:16], right_early[...])
    mid_ref[:, 384:] = jnp.where(col == lax.axis_size("col") - 1, 0.0, after)


def merge(*arrays):
    vmem = pl.BlockSpec(memory_space=pltpu.VMEM)
    return pl.pallas_call(
        merge_kernel,
        out_shape=jax.ShapeDtypeStruct((16, 512), F32),
        in_specs=[vmem] * 9,
        out_specs=vmem,
        compiler_params=pltpu.CompilerParams(vmem_limit_bytes=8 * 2**20),
    )(*arrays)


def coherence_of(mid_ref, first, second, out_ref):
    lane = lax.broadcasted_iota(jnp.int32, (16, 128), 1)
    squares = []
    for at in (128, 256):
        x = mid_ref[:, at : at + 128]
        squares.append(x * x + pltpu.roll(x * x, 64, 1))
    magnitude = jnp.sqrt(jnp.where(lane < 64, squares[0], squares[1]))
    coherence = magnitude / jnp.sqrt((first + 1e-06) * (second + 1e-06))
    for p in range(PAIRS_DEV):
        left = coherence if p == 0 else pltpu.roll(coherence, 128 - HALF * p, 1)
        right = pltpu.roll(coherence, (HALF + 64 - HALF * p) % 128, 1)
        out_ref[p] = jnp.where(lane < HALF, left, right)[:, :PATCH]


def goldstein_kernel(
    first_swap, mid_ref, second_swap, ns_ref, rf_ref, cf_ref, rb_ref, cb_ref, crossing_ref, first_ref, second_ref, late_ref,
    out_ref, coh_ref,
):
    odd_crossing = (crossing_ref[...] == 1) & (odd_date() == 1)
    coherence_of(mid_ref, first_ref[...], jnp.where(odd_crossing, late_ref[16:], second_ref[...]), coh_ref)
    row = lax.axis_index("row")
    odd_row = row % 2 == 1
    up = jnp.where(odd_row, first_swap[...], second_swap[...])
    down = jnp.where(odd_row, second_swap[...], first_swap[...])
    up = jnp.where(row == 0, 0.0, up)
    down = jnp.where(row == lax.axis_size("row") - 1, 0.0, down)
    x = jnp.concatenate([up, mid_ref[...], down], axis=0)
    lane = lax.broadcasted_iota(jnp.int32, (48, 128), 1)
    sign = jnp.where(lane < 64, -1.0, 1.0)
    turned = [pltpu.roll(x[:, 128 * b : 128 * b + 128], 64, 1) * sign for b in range(4)]
    xx = jnp.concatenate([x, jnp.concatenate(turned, axis=1)], axis=0)
    xh, xl = split(xx)
    rh, rl = rf_ref[0], rf_ref[1]
    y = mm(rh, xh) + (mm(rh, xl) + mm(rl, xh))
    ys = jnp.concatenate([y[:, 128 * j : 128 * j + 256] for j in range(3)], axis=0)
    yh, yl = split(ys)
    ch, cl = cf_ref[0], cf_ref[1]
    z = mm(yh, ch) + (mm(yl, ch) + mm(yh, cl))
    zr, zi = z[:, :128], z[:, 128:]
    magnitude = jnp.sqrt(zr * zr + zi * zi)
    mh, ml = split(magnitude)
    across = mm(mh, ns_ref[...]) + mm(ml, ns_ref[...])
    grouped = across.reshape(6, PATCH, 128)
    down_one = jnp.concatenate([grouped[:, PATCH - 1 :], grouped[:, : PATCH - 1]], axis=1)
    up_one = jnp.concatenate([grouped[:, 1:], grouped[:, :1]], axis=1)
    smooth = (grouped + (down_one + up_one)).reshape(192, 128)
    response = jnp.sqrt(smooth * (1.0 / 9.0)) * (1.0 / PATCH)
    fr, fi = zr * response, zi * response
    w = jnp.concatenate(
        [
            jnp.concatenate([fr[64 * j : 64 * j + 64] for j in range(3)], axis=1),
            jnp.concatenate([fi[64 * j : 64 * j + 64] for j in range(3)], axis=1),
        ],
        axis=0,
    )
    wh, wl = split(w)
    bh, bl = rb_ref[0], rb_ref[1]
    t = mm(bh, wh) + (mm(bh, wl) + mm(bl, wh))
    th, tl = split(t)
    gh, gl = cb_ref[0], cb_ref[1]
    o = mm(th, gh) + (mm(tl, gh) + mm(th, gl))
    real = o[:16, :128] - o[16:, 128:]
    imag = o[16:, :128] + o[:16, 128:]
    for p in range(PAIRS_DEV):
        out_ref[p, 0] = real[:, PATCH * p : PATCH * p + PATCH]
        out_ref[p, 1] = imag[:, PATCH * p : PATCH * p + PATCH]


def goldstein(*arrays):
    vmem = pl.BlockSpec(memory_space=pltpu.VMEM)
    return pl.pallas_call(
        goldstein_kernel,
        out_shape=(
            jax.ShapeDtypeStruct((PAIRS_DEV, 2, 16, 32), F32), jax.ShapeDtypeStruct((PAIRS_DEV, 16, 32), F32),
        ),
        in_specs=[vmem] * 12,
        out_specs=(vmem, vmem),
        compiler_params=pltpu.CompilerParams(vmem_limit_bytes=24 * 2**20),
    )(*arrays)


def neighbour(i, n, first):
    if first:
        return i ^ 1
    return ((i - 1) ^ 1) + 1 if 0 < i < n - 1 else i


def shards(stack, pair_list):
    names = ("date", "row", "col")
    dates, rows, cols = (lax.axis_size(name) for name in names)

    def send(x, target):
        pairs = []
        for d in range(dates):
            for r in range(rows):
                for c in range(cols):
                    a, b, e = target(d, r, c)
                    pairs.append(((d * rows + r) * cols + c, (a * rows + b) * cols + e))
        return lax.ppermute(x, names, pairs)

    def swap_cols(first):
        def target(d, r, c):
            e = neighbour(c, cols, first)
            return (d, r, e) if e != c else (d, r ^ 1, c)

        return target

    def swap_rows(first):
        def target(d, r, c):
            b = neighbour(r, rows, first)
            return (d, b, c) if b != r else (d, r, c ^ 1)

        return target

    def between_dates(odd_target, even_target):
        def target(d, r, c):
            if d in (0, dates - 1):
                return d, r, c ^ 1
            if d % 2:
                up, e = odd_target(c)
                return d + up, r, e
            down, e = even_target(c)
            return d - down, r, e

        return target

    end = cols - 1
    straight = between_dates(lambda c: (1, c), lambda c: (1, c))
    from_right = between_dates(
        lambda c: (0, c - 1) if c > 0 else (1, 0),
        lambda c: (0, c + 1) if c < end else (1, end),
    )
    from_left = between_dates(
        lambda c: (1, 0) if c == 0 else (0, 0) if c == 1 else (1, c - 1) if c < end else (1, end),
        lambda c: (1, c + 1) if c < end else (0, end - 1),
    )

    odd = lax.axis_index("date") % 2 == 1
    half = jnp.where(odd, stack[1:, :, :, 256:], stack[:SPAN, :, :, :384])
    listed = pair_list.T
    other = send(pack(half), straight)
    chip = send(stack, lambda d, r, c: (d ^ 1, r, c))
    left, right, first, second, back, crossing, index, keep, look = early(listed, stack)
    left, right, second, one, two = within_chip(listed, chip, keep, look, crossing, left, right, second)
    one = send(one, swap_cols(True))
    two = send(two, swap_cols(False))
    tables = filter_tables(right)
    other, one, two = lax.optimization_barrier((other, one, two))
    new = late(index, other, keep, look, back)
    after = send(new, from_right)
    before = send(new, from_left)
    right_late = send(new, straight)
    mid = merge(crossing, before, new, right_late, after, one, two, left, right)
    one = send(mid, swap_rows(True))
    two = send(mid, swap_rows(False))
    return goldstein(one, mid, two, *tables, crossing, first, second, right_late)


def solution(mesh):
    in_specs = (P("date", None, "row", "col"), P())
    out_specs = (P("date", None, "row", "col"), P("date", "row", "col"))
    return jax.shard_map(shards, mesh=mesh, in_specs=in_specs, out_specs=out_specs, check_vma=False)
```

time: 36.8 us -> 30.2 us (0.82)
  the two profiles are of different devices: /device:TPU:1 before, /device:TPU:97 now
where the time goes in v3:
time: 30.2 us; the launch traced here: 30.1 us
  starting transfers between devices  15.9 us (53%)
  waiting for transfers between devices  6.9 us (23%)
  Pallas kernels  5.1 us (17%)
  other arithmetic  1.54 us (5%)
  between operations  0.7 us (2%)
    ppermute x9, starting transfers between devices, send(): return lax.ppermute(x, names, pairs)  15.9 us
    ppermute x9, waiting for transfers between devices, send(): return lax.ppermute(x, names, pairs)  6.9 us
    pallas_call x1, Pallas kernels, goldstein(): pl.pallas_call(goldstein_kernel, out_shape=(jax.ShapeDtypeStruct((PAIRS_D...  1.84 us
    pallas_call x1, Pallas kernels, early(): pl.pallas_call(early_kernel, out_shape=out_shape, in_specs=[smem, pl.Bloc...  1.81 us
    select_n x1, other arithmetic, shards(): half = jnp.where(odd, stack[1:, :, :, 256:], stack[:SPAN, :, :, :384])  1.54 us
    pallas_call x1, Pallas kernels, within_chip(): pl.pallas_call(chip_kernel, out_shape=[jax.ShapeDtypeStruct((16, 128), F3...  0.69 us
  transfers between devices with their start and end apart: 9, of which 4 were waited for; matrix products, arithmetic and copies ran while one was open for 5% of the time, Pallas kernels for 9%

profile of v3, /device:TPU:97, one launch (start us, length us, event | category | flops | bytes accessed | tf_op | source)
XLA Modules:
  0.0 30.1 jit_solution(15893727175350411235)
XLA Ops:
  0.6 0.8 %collective-permute-start.1 = (f32[4,2,80,640]{3,2,1,0:T(8,128)}, f32[4,2,80,640]{3,2,1,0:T(8,128)S(1)}, u32[]{:S(2)}, u32[]{:S(2)}) collective-permute-start(f32[4,2,80,640]{3,2,1,0:T(8,128)} %stack_ref.1), channel_id=1, source_target_pairs={{0,16},{1,17},{2,18},{3,19},{4,20},{5,21},{6,22},{7,23},{8,24},{9,... | collective-permute-start | bytes 4915208 | tf_op jit(solution)/shard_map/ppermute | solution.py:521
  1.4 0.0 copy-start
  1.4 0.0 copy-start.2
  1.4 1.5 %slice_select_fusion.half_ref = f32[3,2,80,384]{3,2,1,0:T(8,128)S(1)} fusion(f32[4,2,80,640]{3,2,1,0:T(8,128)} %stack_ref.1, pred[]{:T(512)S(6)} %eq.5), kind=kLoop, calls=%fused_computation | loop fusion | flops 184320 | bytes 2211841 | tf_op jit(solution)/shard_map/jit(_where)/select_n | solution.py:561
  2.9 0.1 shard_map.51
  3.1 2.9 %collective-permute-start = (f32[3,5,80,128]{3,2,1,0:T(8,128)S(1)}, f32[3,5,80,128]{3,2,1,0:T(8,128)S(1)}, u32[]{:S(2)}, u32[]{:S(2)}) collective-permute-start(f32[3,5,80,128]{3,2,1,0:T(8,128)S(1)} %shard_map.51), channel_id=1, source_target_pairs={{0,1},{1,0},{2,3},{3,2},{4,5},{5,4},{6,7},{7,6},{8,9},{9,8},{10,11... | collective-permute-start | bytes 1843208 | tf_op jit(solution)/shard_map/ppermute | solution.py:521
  5.9 0.0 copy-done
  5.9 0.0 copy-done.2
  5.9 1.8 %shard_map.50 = (f32[16,128]{1,0:T(8,128)S(1)}, f32[16,128]{1,0:T(8,128)S(1)}, f32[16,128]{1,0:T(8,128)S(1)}, f32[16,128]{1,0:T(8,128)S(1)}, f32[16,128]{1,0:T(8...) custom-call(s32[2,64]{1,0:T(2,128)S(1)} %bitcast.1, ...), custom_call_target="tpu_custom_call" | custom-call | flops 1000000000 | bytes 10000000 | tf_op jit(solution)/shard_map/pallas_call | solution.py:272
  7.8 0.0 collective-permute-done.1.other_ref
  7.8 0.7 %shard_map.52 = (f32[16,128]{1,0:T(8,128)S(1)}, f32[16,128]{1,0:T(8,128)S(1)}, f32[16,128]{1,0:T(8,128)S(1)}, f32[16,128]{1,0:T(8,128)S(1)}, f32[16,128]{1,0:T(8,128)S(1)}) custom-call(s32[2,64]{1,0:T(2,128)S(1)} %bitcast.2, f32[4,2,80,640]{3,2,1,0:T(8,128)S(1)} %collective-permute-done.1.other_ref, f32[2,4,5,80,128]{4,3,2,1,0:T(8,128)S(1)} %get-tuple-element.26.keep, ...), custom_call_target="tpu_custom_call" | custom-call | flops 1000000000 | bytes 10000000 | tf_op jit(solution)/shard_map/pallas_call | solution.py:326
  8.5 0.0 copy-start.1
  8.5 1.4 %collective-permute-start.2 = (f32[16,128]{1,0:T(8,128)S(1)}, f32[16,128]{1,0:T(8,128)S(1)}, u32[]{:S(2)}, u32[]{:S(2)}) collective-permute-start(f32[16,128]{1,0:T(8,128)S(1)} %get-tuple-element.31), channel_id=1, source_target_pairs={{0,1},{1,0},{2,3},{3,2},{4,5},{5,4},{6,7},{7,6},{8,9},{9,8},{10,11... | collective-permute-start | bytes 24584 | tf_op jit(solution)/shard_map/ppermute | solution.py:521
  9.9 1.2 %collective-permute-start.3 = (f32[16,128]{1,0:T(8,128)S(1)}, f32[16,128]{1,0:T(8,128)S(1)}, u32[]{:S(2)}, u32[]{:S(2)}) collective-permute-start(f32[16,128]{1,0:T(8,128)S(1)} %get-tuple-element.32), channel_id=1, source_target_pairs={{0,4},{1,2},{2,1},{3,7},{4,0},{5,6},{6,5},{7,3},{8,12},{9,10},{10,... | collective-permute-start | bytes 24584 | tf_op jit(solution)/shard_map/ppermute | solution.py:521
  11.1 2.9 %collective-permute-done.other_ref = f32[3,5,80,128]{3,2,1,0:T(8,128)S(1)} collective-permute-done((f32[3,5,80,128]{3,2,1,0:T(8,128)S(1)}, f32[3,5,80,128]{3,2,1,0:T(8,128)S(1)}, u32[]{:S(2)}, u32[]{:S(2)}) %collective-permute-start) | collective-permute-done | bytes 614432 | tf_op jit(solution)/shard_map/ppermute | solution.py:521
  13.9 0.0 collective-permute-done.2.first_ref
  13.9 0.0 collective-permute-done.3.second_ref
  14.0 0.5 %shard_map.53.left_late = f32[32,128]{1,0:T(8,128)S(1)} custom-call(s32[8,128]{1,0:T(8,128)S(1)} %get-tuple-element.25.index_ref, f32[3,5,80,128]{3,2,1,0:T(8,128)S(1)} %collective-permute-done.other_ref, f32[2,4,5,80,128]{4,3,2,1,0:T(8,128)S(1)} %get-tuple-element.26.keep, bf16[384,256]{1,0:T(8,128)(2,1)S(1)} %get-tuple-element.27.table_ref, ...), custom_call_target="tpu_custom_call" | custom-call | tf_op jit(solution)/shard_map/pallas_call | solution.py:389
  14.4 2.8 %collective-permute-start.6 = (f32[32,128]{1,0:T(8,128)S(1)}, f32[32,128]{1,0:T(8,128)S(1)}, u32[]{:S(2)}, u32[]{:S(2)}) collective-permute-start(f32[32,128]{1,0:T(8,128)S(1)} %shard_map.53.left_late), channel_id=1, source_target_pairs={{0,1},{1,0},{2,3},{3,2},{4,5},{5,4},{6,7},{7,6},{8,9},{9,8},{10,11... | collective-permute-start | bytes 49160 | tf_op jit(solution)/shard_map/ppermute | solution.py:521
  17.3 1.6 %collective-permute-start.5 = (f32[32,128]{1,0:T(8,128)S(1)}, f32[32,128]{1,0:T(8,128)S(1)}, u32[]{:S(2)}, u32[]{:S(2)}) collective-permute-start(f32[32,128]{1,0:T(8,128)S(1)} %shard_map.53.left_late), channel_id=1, source_target_pairs={{0,1},{1,0},{2,3},{3,2},{4,5},{5,4},{6,7},{7,6},{8,9},{9,8},{10,11... | collective-permute-start | bytes 49160 | tf_op jit(solution)/shard_map/ppermute | solution.py:521
  18.8 1.4 %collective-permute-start.4 = (f32[32,128]{1,0:T(8,128)S(1)}, f32[32,128]{1,0:T(8,128)S(1)}, u32[]{:S(2)}, u32[]{:S(2)}) collective-permute-start(f32[32,128]{1,0:T(8,128)S(1)} %shard_map.53.left_late), channel_id=1, source_target_pairs={{0,1},{1,0},{2,3},{3,2},{4,5},{5,4},{6,7},{7,6},{8,9},{9,8},{10,11... | collective-permute-start | bytes 49160 | tf_op jit(solution)/shard_map/ppermute | solution.py:521
  20.2 0.0 collective-permute-done.6.after_late
  20.2 1.4 %collective-permute-done.5.right_late.late_ref = f32[32,128]{1,0:T(8,128)S(1)} collective-permute-done((f32[32,128]{1,0:T(8,128)S(1)}, f32[32,128]{1,0:T(8,128)S(1)}, u32[]{:S(2)}, u32[]{:S(2)}) %collective-permute-start.5) | collective-permute-done | bytes 16416 | tf_op jit(solution)/shard_map/ppermute | solution.py:521
  21.6 0.0 collective-permute-done.4.before_late
  21.7 3.8 %collective-permute-start.8 = (f32[16,512]{1,0:T(8,128)S(1)}, f32[16,512]{1,0:T(8,128)S(1)}, u32[]{:S(2)}, u32[]{:S(2)}) collective-permute-start(f32[16,512]{1,0:T(8,128)S(1)} %shard_map.54.mid_ref), channel_id=1, source_target_pairs={{0,1},{1,0},{2,3},{3,2},{4,8},{5,9},{6,10},{7,11},{8,4},{9,5},{10,... | collective-permute-start | bytes 98312 | tf_op jit(solution)/shard_map/ppermute | solution.py:521
  25.5 0.0 collective-permute-start.7
  25.5 0.0 copy-done.1
  25.5 0.1 shard_map.55
  25.7 1.2 %collective-permute-done.8.second_swap = f32[16,512]{1,0:T(8,128)S(1)} collective-permute-done((f32[16,512]{1,0:T(8,128)S(1)}, f32[16,512]{1,0:T(8,128)S(1)}, u32[]{:S(2)}, u32[]{:S(2)}) %collective-permute-start.8) | collective-permute-done | bytes 32800 | tf_op jit(solution)/shard_map/ppermute | solution.py:521
  26.8 1.5 %collective-permute-done.7.first_swap = f32[16,512]{1,0:T(8,128)S(1)} collective-permute-done((f32[16,512]{1,0:T(8,128)S(1)}, f32[16,512]{1,0:T(8,128)S(1)}, u32[]{:S(2)}, u32[]{:S(2)}) %collective-permute-start.7) | collective-permute-done | bytes 32800 | tf_op jit(solution)/shard_map/ppermute | solution.py:521
  28.3 1.8 %shard_map.56 = (f32[4,2,16,32]{3,2,1,0:T(8,128)}, f32[4,16,32]{2,1,0:T(8,128)}) custom-call(f32[16,512]{1,0:T(8,128)S(1)} %collective-permute-done.7.first_swap, f32[16,512]{1,0:T(8,128)S(1)} %shard_map.54.mid_ref, f32[16,512]{1,0:T(8,128)S(1)} %collective-permute-done.8.second_swap, bf16[128,128]{1,0:T(8,128)(2,1)S(1)} %get-tuple-element.39.ns_ref, ...), custom_call_target="tpu_custom_call" | custom-call | tf_op jit(solution)/shard_map/pallas_call | solution.py:493
  (1 shorter events, 0.0 us)
Async XLA Ops:
  0.6 7.1 %collective-permute-start.1 = (f32[4,2,80,640]{3,2,1,0:T(8,128)}, f32[4,2,80,640]{3,2,1,0:T(8,128)S(1)}, u32[]{:S(2)}, u32[]{:S(2)}) collective-permute-start(f32[4,2,80,640]{3,2,1,0:T(8,128)} %stack_ref.1), channel_id=1, source_target_pairs={{0,16},{1,17},{2,18},{3,19},{4,20},{5,21},{6,22},{7,23},{8,24},{9,... | collective-permute-start | bytes 4915208 | tf_op jit(solution)/shard_map/ppermute | solution.py:521
  1.4 4.5 %copy-start = (f32[4,2,80,640]{3,2,1,0:T(8,128)S(1)}, f32[4,2,80,640]{3,2,1,0:T(8,128)}, u32[]{:S(2)}) copy-start(f32[4,2,80,640]{3,2,1,0:T(8,128)} %stack_ref.1) | copy-start | bytes 4915204
  1.4 4.5 %copy-start.2 = (s32[64,2]{0,1:T(2,128)S(1)}, s32[64,2]{0,1:T(2,128)}, u32[]{:S(2)}) copy-start(s32[64,2]{0,1:T(2,128)} %param.4) | copy-start | bytes 1540
  3.1 10.9 %collective-permute-start = (f32[3,5,80,128]{3,2,1,0:T(8,128)S(1)}, f32[3,5,80,128]{3,2,1,0:T(8,128)S(1)}, u32[]{:S(2)}, u32[]{:S(2)}) collective-permute-start(f32[3,5,80,128]{3,2,1,0:T(8,128)S(1)} %shard_map.51), channel_id=1, source_target_pairs={{0,1},{1,0},{2,3},{3,2},{4,5},{5,4},{6,7},{7,6},{8,9},{9,8},{10,11... | collective-permute-start | bytes 1843208 | tf_op jit(solution)/shard_map/ppermute | solution.py:521
  8.5 17.1 %copy-start.1 = (f32[704,256]{1,0:T(8,128)S(1)}, f32[704,256]{1,0:T(8,128)}, u32[]{:S(2)}) copy-start(f32[704,256]{1,0:T(8,128)} %constant.21.clone.trig_ref) | copy-start | bytes 2162692
  8.5 5.5 %collective-permute-start.2 = (f32[16,128]{1,0:T(8,128)S(1)}, f32[16,128]{1,0:T(8,128)S(1)}, u32[]{:S(2)}, u32[]{:S(2)}) collective-permute-start(f32[16,128]{1,0:T(8,128)S(1)} %get-tuple-element.31), channel_id=1, source_target_pairs={{0,1},{1,0},{2,3},{3,2},{4,5},{5,4},{6,7},{7,6},{8,9},{9,8},{10,11... | collective-permute-start | bytes 24584 | tf_op jit(solution)/shard_map/ppermute | solution.py:521
  9.9 4.1 %collective-permute-start.3 = (f32[16,128]{1,0:T(8,128)S(1)}, f32[16,128]{1,0:T(8,128)S(1)}, u32[]{:S(2)}, u32[]{:S(2)}) collective-permute-start(f32[16,128]{1,0:T(8,128)S(1)} %get-tuple-element.32), channel_id=1, source_target_pairs={{0,4},{1,2},{2,1},{3,7},{4,0},{5,6},{6,5},{7,3},{8,12},{9,10},{10,... | collective-permute-start | bytes 24584 | tf_op jit(solution)/shard_map/ppermute | solution.py:521
  14.4 5.8 %collective-permute-start.6 = (f32[32,128]{1,0:T(8,128)S(1)}, f32[32,128]{1,0:T(8,128)S(1)}, u32[]{:S(2)}, u32[]{:S(2)}) collective-permute-start(f32[32,128]{1,0:T(8,128)S(1)} %shard_map.53.left_late), channel_id=1, source_target_pairs={{0,1},{1,0},{2,3},{3,2},{4,5},{5,4},{6,7},{7,6},{8,9},{9,8},{10,11... | collective-permute-start | bytes 49160 | tf_op jit(solution)/shard_map/ppermute | solution.py:521
  17.3 4.4 %collective-permute-start.5 = (f32[32,128]{1,0:T(8,128)S(1)}, f32[32,128]{1,0:T(8,128)S(1)}, u32[]{:S(2)}, u32[]{:S(2)}) collective-permute-start(f32[32,128]{1,0:T(8,128)S(1)} %shard_map.53.left_late), channel_id=1, source_target_pairs={{0,1},{1,0},{2,3},{3,2},{4,5},{5,4},{6,7},{7,6},{8,9},{9,8},{10,11... | collective-permute-start | bytes 49160 | tf_op jit(solution)/shard_map/ppermute | solution.py:521
  18.8 2.8 %collective-permute-start.4 = (f32[32,128]{1,0:T(8,128)S(1)}, f32[32,128]{1,0:T(8,128)S(1)}, u32[]{:S(2)}, u32[]{:S(2)}) collective-permute-start(f32[32,128]{1,0:T(8,128)S(1)} %shard_map.53.left_late), channel_id=1, source_target_pairs={{0,1},{1,0},{2,3},{3,2},{4,5},{5,4},{6,7},{7,6},{8,9},{9,8},{10,11... | collective-permute-start | bytes 49160 | tf_op jit(solution)/shard_map/ppermute | solution.py:521
  21.7 5.2 %collective-permute-start.8 = (f32[16,512]{1,0:T(8,128)S(1)}, f32[16,512]{1,0:T(8,128)S(1)}, u32[]{:S(2)}, u32[]{:S(2)}) collective-permute-start(f32[16,512]{1,0:T(8,128)S(1)} %shard_map.54.mid_ref), channel_id=1, source_target_pairs={{0,1},{1,0},{2,3},{3,2},{4,8},{5,9},{6,10},{7,11},{8,4},{9,5},{10,... | collective-permute-start | bytes 98312 | tf_op jit(solution)/shard_map/ppermute | solution.py:521
  25.5 2.8 %collective-permute-start.7 = (f32[16,512]{1,0:T(8,128)S(1)}, f32[16,512]{1,0:T(8,128)S(1)}, u32[]{:S(2)}, u32[]{:S(2)}) collective-permute-start(f32[16,512]{1,0:T(8,128)S(1)} %shard_map.54.mid_ref), channel_id=1, source_target_pairs={{0,4},{1,5},{2,6},{3,7},{4,0},{5,1},{6,2},{7,3},{8,12},{9,13},{10,... | collective-permute-start | bytes 98312 | tf_op jit(solution)/shard_map/ppermute | solution.py:521

commit v4 on v3

--- a/solution.py
+++ b/solution.py
@@ -137,26 +137,33 @@
     return lax.axis_index("date") % 2
 
 
-def pack_kernel(half_ref, out_ref):
-    odd = odd_date() == 1
+def pack_kernel(stack_ref, out_ref, middle, sem):
+    odd = odd_date()
+    acqs = pl.ds(odd, SPAN)
+    copies = [pltpu.make_async_copy(stack_ref.at[acqs, :, :, pl.ds(256, 128)], middle, sem.at[4])]
+    for comp in range(2):
+        for t in range(2):
+            lanes = pl.ds(pl.multiple_of(128 * (3 * odd + t), 128), 128)
+            at = 2 * comp + t
+            copies.append(pltpu.make_async_copy(stack_ref.at[acqs, comp, :, lanes], out_ref.at[:, at], sem.at[at]))
+    for copy in copies:
+        copy.start()
+    copies[0].wait()
     for acq in range(SPAN):
-        tiles = [[half_ref[acq, comp, :, pl.ds(128 * t, 128)] for t in range(3)] for comp in range(2)]
-        for comp in range(2):
-            out_ref[acq, 2 * comp] = jnp.where(odd, tiles[comp][1], tiles[comp][0])
-            out_ref[acq, 2 * comp + 1] = jnp.where(odd, tiles[comp][2], tiles[comp][1])
-        real, imag = (jnp.where(odd, tiles[comp][0], tiles[comp][2]) for comp in range(2))
-        out_ref[acq, 4] = mixed_tile(real, imag, odd)
-
-
-def pack(half):
-    vmem = pl.BlockSpec(memory_space=pltpu.VMEM)
+        out_ref[acq, 4] = mixed_tile(middle[acq, 0], middle[acq, 1], odd == 1)
+    for copy in copies[1:]:
+        copy.wait()
+
+
+def pack(stack):
     return pl.pallas_call(
         pack_kernel,
-        out_shape=jax.ShapeDtypeStruct((SPAN, 5, 80, 128), F32),
-        in_specs=[vmem],
-        out_specs=vmem,
-        compiler_params=pltpu.CompilerParams(vmem_limit_bytes=16 * 2**20),
-    )(half)
+        out_shape=pltpu.VMEM((SPAN, 5, 80, 128), F32),
+        in_specs=[pl.BlockSpec(memory_space=pl.ANY)],
+        out_specs=pl.BlockSpec(memory_space=pltpu.VMEM),
+        scratch_shapes=[pltpu.VMEM((SPAN, 2, 80, 128), F32), pltpu.SemaphoreType.DMA((5,))],
+        compiler_params=pltpu.CompilerParams(vmem_limit_bytes=60000000),
+    )(stack)
 
 
 def cross(a_ref, a, b_ref, b):
@@ -396,7 +403,7 @@
 
 
 def merge_kernel(
-    crossing_ref, before_late, left_late, right_late, after_late, first_ref, second_ref, left_early, right_early, mid_ref
+    crossing_ref, before_late, right_late, after_late, left_late, first_ref, second_ref, left_early, right_early, mid_ref
 ):
     crossing = (crossing_ref[...] == 1) & (odd_date() == 1)
     col = lax.axis_index("col")
@@ -453,7 +460,7 @@
     xx = jnp.concatenate([x, jnp.concatenate(turned, axis=1)], axis=0)
     xh, xl = split(xx)
     rh, rl = rf_ref[0], rf_ref[1]
-    y = mm(rh, xh) + (mm(rh, xl) + mm(rl, xh))
+    y = mm(jnp.concatenate([rh, rh], axis=1), jnp.concatenate([xh, xl], axis=0)) + mm(rl, xh)
     ys = jnp.concatenate([y[:, 128 * j : 128 * j + 256] for j in range(3)], axis=0)
     yh, yl = split(ys)
     ch, cl = cf_ref[0], cf_ref[1]
@@ -461,7 +468,7 @@
     zr, zi = z[:, :128], z[:, 128:]
     magnitude = jnp.sqrt(zr * zr + zi * zi)
     mh, ml = split(magnitude)
-    across = mm(mh, ns_ref[...]) + mm(ml, ns_ref[...])
+    across = mm(jnp.concatenate([mh, ml], axis=1), jnp.concatenate([ns_ref[...], ns_ref[...]], axis=0))
     grouped = across.reshape(6, PATCH, 128)
     down_one = jnp.concatenate([grouped[:, PATCH - 1 :], grouped[:, : PATCH - 1]], axis=1)
     up_one = jnp.concatenate([grouped[:, 1:], grouped[:, :1]], axis=1)
@@ -477,10 +484,11 @@
     )
     wh, wl = split(w)
     bh, bl = rb_ref[0], rb_ref[1]
-    t = mm(bh, wh) + (mm(bh, wl) + mm(bl, wh))
+    t = mm(jnp.concatenate([bh, bh], axis=1), jnp.concatenate([wh, wl], axis=0)) + mm(bl, wh)
     th, tl = split(t)
     gh, gl = cb_ref[0], cb_ref[1]
-    o = mm(th, gh) + (mm(tl, gh) + mm(th, gl))
+    oo = mm(jnp.concatenate([th, tl], axis=0), gh)
+    o = oo[:32] + (oo[32:] + mm(th, gl))
     real = o[:16, :128] - o[16:, 128:]
     imag = o[16:, :128] + o[:16, 128:]
     for p in range(PAIRS_DEV):
@@ -548,19 +556,18 @@
 
     end = cols - 1
     straight = between_dates(lambda c: (1, c), lambda c: (1, c))
-    from_right = between_dates(
-        lambda c: (0, c - 1) if c > 0 else (1, 0),
-        lambda c: (0, c + 1) if c < end else (1, end),
-    )
+    def ring(d, r, c):
+        if d % 2:
+            return (d, r, c - 1) if c > 0 else (d - 1, r, c)
+        return (d, r, c + 1) if c < end else (d + 1, r, c)
+
     from_left = between_dates(
         lambda c: (1, 0) if c == 0 else (0, 0) if c == 1 else (1, c - 1) if c < end else (1, end),
         lambda c: (1, c + 1) if c < end else (0, end - 1),
     )
 
-    odd = lax.axis_index("date") % 2 == 1
-    half = jnp.where(odd, stack[1:, :, :, 256:], stack[:SPAN, :, :, :384])
     listed = pair_list.T
-    other = send(pack(half), straight)
+    other = send(pack(stack), straight)
     chip = send(stack, lambda d, r, c: (d ^ 1, r, c))
     left, right, first, second, back, crossing, index, keep, look = early(listed, stack)
     left, right, second, one, two = within_chip(listed, chip, keep, look, crossing, left, right, second)
@@ -569,10 +576,10 @@
     tables = filter_tables(right)
     other, one, two = lax.optimization_barrier((other, one, two))
     new = late(index, other, keep, look, back)
-    after = send(new, from_right)
+    after = send(new, ring)
     before = send(new, from_left)
     right_late = send(new, straight)
-    mid = merge(crossing, before, new, right_late, after, one, two, left, right)
+    mid = merge(crossing, before, right_late, after, new, one, two, left, right)
     one = send(mid, swap_rows(True))
     two = send(mid, swap_rows(False))
     return goldstein(one, mid, two, *tables, crossing, first, second, right_late)

time: 30.2 us -> 27.6 us (0.914)
  the two profiles are of different devices: /device:TPU:97 before, /device:TPU:148 now
where the time goes in v4:
time: 27.6 us; the launch traced here: 27.1 us
  waiting for transfers between devices  11.8 us (43%)
  starting transfers between devices  7.27 us (26%)
  Pallas kernels  7.18 us (26%)
  between operations  0.71 us (3%)
    ppermute x9, waiting for transfers between devices, send(): return lax.ppermute(x, names, pairs)  11.8 us
    ppermute x9, starting transfers between devices, send(): return lax.ppermute(x, names, pairs)  7.27 us
    pallas_call x1, Pallas kernels, early(): pl.pallas_call(early_kernel, out_shape=out_shape, in_specs=[smem, pl.Bloc...  1.82 us
    pallas_call x1, Pallas kernels, goldstein(): pl.pallas_call(goldstein_kernel, out_shape=(jax.ShapeDtypeStruct((PAIRS_D...  1.71 us
    pallas_call x1, Pallas kernels, within_chip(): pl.pallas_call(chip_kernel, out_shape=[jax.ShapeDtypeStruct((16, 128), F3...  1.67 us
    pallas_call x1, Pallas kernels, pack(): pl.pallas_call(pack_kernel, out_shape=pltpu.VMEM((SPAN, 5, 80, 128), F32)...  1.37 us
  transfers between devices with their start and end apart: 9, of which 6 were waited for; matrix products, arithmetic and copies ran while one was open for 0% of the time, Pallas kernels for 18%

profile of v4, /device:TPU:148, one launch (start us, length us, event | category | flops | bytes accessed | tf_op | source)
XLA Modules:
  0.0 27.1 jit_solution(11604090776763672189)
XLA Ops:
  0.6 0.0 copy-start
  0.6 0.0 copy-start.2
  0.6 0.1 collective-permute-start.1
  0.7 1.4 %shard_map.51 = f32[3,5,80,128]{3,2,1,0:T(8,128)S(1)} custom-call(f32[4,2,80,640]{3,2,1,0:T(8,128)} %stack_ref.3), custom_call_target="tpu_custom_call" | custom-call | tf_op jit(solution)/shard_map/pallas_call | solution.py:159
  2.1 0.2 collective-permute-start
  2.3 0.1 copy-done
  2.4 0.0 copy-done.2
  2.4 1.8 %shard_map.50 = (f32[16,128]{1,0:T(8,128)S(1)}, f32[16,128]{1,0:T(8,128)S(1)}, f32[16,128]{1,0:T(8,128)S(1)}, f32[16,128]{1,0:T(8,128)S(1)}, f32[16,128]{1,0:T(8...) custom-call(s32[2,64]{1,0:T(2,128)S(1)} %bitcast.1, ...), custom_call_target="tpu_custom_call" | custom-call | flops 1000000000 | bytes 10000000 | tf_op jit(solution)/shard_map/pallas_call | solution.py:279
  4.2 0.2 collective-permute-done.1.other_ref
  4.5 1.7 %shard_map.52 = (f32[16,128]{1,0:T(8,128)S(1)}, f32[16,128]{1,0:T(8,128)S(1)}, f32[16,128]{1,0:T(8,128)S(1)}, f32[16,128]{1,0:T(8,128)S(1)}, f32[16,128]{1,0:T(8,128)S(1)}) custom-call(s32[2,64]{1,0:T(2,128)S(1)} %bitcast.2, f32[4,2,80,640]{3,2,1,0:T(8,128)S(1)} %collective-permute-done.1.other_ref, f32[2,4,5,80,128]{4,3,2,1,0:T(8,128)S(1)} %get-tuple-element.26.keep, ...), custom_call_target="tpu_custom_call" | custom-call | flops 1000000000 | bytes 10000000 | tf_op jit(solution)/shard_map/pallas_call | solution.py:333
  6.1 0.0 copy-start.1
  6.1 1.4 %collective-permute-start.2 = (f32[16,128]{1,0:T(8,128)S(1)}, f32[16,128]{1,0:T(8,128)S(1)}, u32[]{:S(2)}, u32[]{:S(2)}) collective-permute-start(f32[16,128]{1,0:T(8,128)S(1)} %get-tuple-element.31), channel_id=1, source_target_pairs={{0,1},{1,0},{2,3},{3,2},{4,5},{5,4},{6,7},{7,6},{8,9},{9,8},{10,11... | collective-permute-start | bytes 24584 | tf_op jit(solution)/shard_map/ppermute | solution.py:529
  7.5 0.0 collective-permute-start.3
  7.5 5.5 %collective-permute-done.other_ref = f32[3,5,80,128]{3,2,1,0:T(8,128)S(1)} collective-permute-done((f32[3,5,80,128]{3,2,1,0:T(8,128)S(1)}, f32[3,5,80,128]{3,2,1,0:T(8,128)S(1)}, u32[]{:S(2)}, u32[]{:S(2)}) %collective-permute-start) | collective-permute-done | bytes 614432 | tf_op jit(solution)/shard_map/ppermute | solution.py:529
  13.0 0.0 collective-permute-done.2.first_ref
  13.0 0.0 collective-permute-done.3.second_ref
  13.0 0.5 %shard_map.53.left_late = f32[32,128]{1,0:T(8,128)S(1)} custom-call(s32[8,128]{1,0:T(8,128)S(1)} %get-tuple-element.25.index_ref, f32[3,5,80,128]{3,2,1,0:T(8,128)S(1)} %collective-permute-done.other_ref, f32[2,4,5,80,128]{4,3,2,1,0:T(8,128)S(1)} %get-tuple-element.26.keep, bf16[384,256]{1,0:T(8,128)(2,1)S(1)} %get-tuple-element.27.table_ref, ...), custom_call_target="tpu_custom_call" | custom-call | tf_op jit(solution)/shard_map/pallas_call | solution.py:396
  13.5 0.9 %collective-permute-start.4 = (f32[32,128]{1,0:T(8,128)S(1)}, f32[32,128]{1,0:T(8,128)S(1)}, u32[]{:S(2)}, u32[]{:S(2)}) collective-permute-start(f32[32,128]{1,0:T(8,128)S(1)} %shard_map.53.left_late), channel_id=1, source_target_pairs={{0,1},{1,0},{2,3},{3,2},{4,5},{5,4},{6,7},{7,6},{8,9},{9,8},{10,11... | collective-permute-start | bytes 49160 | tf_op jit(solution)/shard_map/ppermute | solution.py:529
  14.4 2.0 %collective-permute-start.5 = (f32[32,128]{1,0:T(8,128)S(1)}, f32[32,128]{1,0:T(8,128)S(1)}, u32[]{:S(2)}, u32[]{:S(2)}) collective-permute-start(f32[32,128]{1,0:T(8,128)S(1)} %shard_map.53.left_late), channel_id=1, source_target_pairs={{0,1},{1,0},{2,3},{3,2},{4,5},{5,4},{6,7},{7,6},{8,9},{9,8},{10,11... | collective-permute-start | bytes 49160 | tf_op jit(solution)/shard_map/ppermute | solution.py:529
  16.4 1.4 %collective-permute-start.6 = (f32[32,128]{1,0:T(8,128)S(1)}, f32[32,128]{1,0:T(8,128)S(1)}, u32[]{:S(2)}, u32[]{:S(2)}) collective-permute-start(f32[32,128]{1,0:T(8,128)S(1)} %shard_map.53.left_late), channel_id=1, source_target_pairs={{0,1},{1,2},{2,3},{3,19},{4,5},{5,6},{6,7},{7,23},{8,9},{9,10},{10... | collective-permute-start | bytes 49160 | tf_op jit(solution)/shard_map/ppermute | solution.py:529
  17.8 0.0 collective-permute-done.4.before_late
  17.8 1.0 %collective-permute-done.5.right_late.late_ref = f32[32,128]{1,0:T(8,128)S(1)} collective-permute-done((f32[32,128]{1,0:T(8,128)S(1)}, f32[32,128]{1,0:T(8,128)S(1)}, u32[]{:S(2)}, u32[]{:S(2)}) %collective-permute-start.5) | collective-permute-done | bytes 16416 | tf_op jit(solution)/shard_map/ppermute | solution.py:529
  18.8 1.4 %collective-permute-done.6.after_late = f32[32,128]{1,0:T(8,128)S(1)} collective-permute-done((f32[32,128]{1,0:T(8,128)S(1)}, f32[32,128]{1,0:T(8,128)S(1)}, u32[]{:S(2)}, u32[]{:S(2)}) %collective-permute-start.6) | collective-permute-done | bytes 16416 | tf_op jit(solution)/shard_map/ppermute | solution.py:529
  20.2 1.3 %collective-permute-start.7 = (f32[16,512]{1,0:T(8,128)S(1)}, f32[16,512]{1,0:T(8,128)S(1)}, u32[]{:S(2)}, u32[]{:S(2)}) collective-permute-start(f32[16,512]{1,0:T(8,128)S(1)} %shard_map.54.mid_ref), channel_id=1, source_target_pairs={{0,4},{1,5},{2,6},{3,7},{4,0},{5,1},{6,2},{7,3},{8,12},{9,13},{10,... | collective-permute-start | bytes 98312 | tf_op jit(solution)/shard_map/ppermute | solution.py:529
  21.4 0.0 collective-permute-start.8
  21.4 0.0 copy-done.1
  21.4 0.1 shard_map.55
  21.6 2.6 %collective-permute-done.7.first_swap = f32[16,512]{1,0:T(8,128)S(1)} collective-permute-done((f32[16,512]{1,0:T(8,128)S(1)}, f32[16,512]{1,0:T(8,128)S(1)}, u32[]{:S(2)}, u32[]{:S(2)}) %collective-permute-start.7) | collective-permute-done | bytes 32800 | tf_op jit(solution)/shard_map/ppermute | solution.py:529
  24.2 1.2 %collective-permute-done.8.second_swap = f32[16,512]{1,0:T(8,128)S(1)} collective-permute-done((f32[16,512]{1,0:T(8,128)S(1)}, f32[16,512]{1,0:T(8,128)S(1)}, u32[]{:S(2)}, u32[]{:S(2)}) %collective-permute-start.8) | collective-permute-done | bytes 32800 | tf_op jit(solution)/shard_map/ppermute | solution.py:529
  25.4 1.7 %shard_map.56 = (f32[4,2,16,32]{3,2,1,0:T(8,128)}, f32[4,16,32]{2,1,0:T(8,128)}) custom-call(f32[16,512]{1,0:T(8,128)S(1)} %collective-permute-done.7.first_swap, f32[16,512]{1,0:T(8,128)S(1)} %shard_map.54.mid_ref, f32[16,512]{1,0:T(8,128)S(1)} %collective-permute-done.8.second_swap, bf16[128,128]{1,0:T(8,128)(2,1)S(1)} %get-tuple-element.39.ns_ref, ...), custom_call_target="tpu_custom_call" | custom-call | tf_op jit(solution)/shard_map/pallas_call | solution.py:501
  (1 shorter events, 0.0 us)
Async XLA Ops:
  0.6 1.8 %copy-start = (f32[4,2,80,640]{3,2,1,0:T(8,128)S(1)}, f32[4,2,80,640]{3,2,1,0:T(8,128)}, u32[]{:S(2)}) copy-start(f32[4,2,80,640]{3,2,1,0:T(8,128)} %stack_ref.3) | copy-start | bytes 4915204
  0.6 1.8 %copy-start.2 = (s32[64,2]{0,1:T(2,128)S(1)}, s32[64,2]{0,1:T(2,128)}, u32[]{:S(2)}) copy-start(s32[64,2]{0,1:T(2,128)} %param.4) | copy-start | bytes 1540
  0.6 3.8 %collective-permute-start.1 = (f32[4,2,80,640]{3,2,1,0:T(8,128)}, f32[4,2,80,640]{3,2,1,0:T(8,128)S(1)}, u32[]{:S(2)}, u32[]{:S(2)}) collective-permute-start(f32[4,2,80,640]{3,2,1,0:T(8,128)} %stack_ref.3), channel_id=1, source_target_pairs={{0,16},{1,17},{2,18},{3,19},{4,20},{5,21},{6,22},{7,23},{8,24},{9,... | collective-permute-start | bytes 4915208 | tf_op jit(solution)/shard_map/ppermute | solution.py:529
  2.1 10.9 %collective-permute-start = (f32[3,5,80,128]{3,2,1,0:T(8,128)S(1)}, f32[3,5,80,128]{3,2,1,0:T(8,128)S(1)}, u32[]{:S(2)}, u32[]{:S(2)}) collective-permute-start(f32[3,5,80,128]{3,2,1,0:T(8,128)S(1)} %shard_map.51), channel_id=1, source_target_pairs={{0,1},{1,0},{2,3},{3,2},{4,5},{5,4},{6,7},{7,6},{8,9},{9,8},{10,11... | collective-permute-start | bytes 1843208 | tf_op jit(solution)/shard_map/ppermute | solution.py:529
  6.1 15.3 %copy-start.1 = (f32[704,256]{1,0:T(8,128)S(1)}, f32[704,256]{1,0:T(8,128)}, u32[]{:S(2)}) copy-start(f32[704,256]{1,0:T(8,128)} %constant.2.clone.trig_ref) | copy-start | bytes 2162692
  6.1 6.9 %collective-permute-start.2 = (f32[16,128]{1,0:T(8,128)S(1)}, f32[16,128]{1,0:T(8,128)S(1)}, u32[]{:S(2)}, u32[]{:S(2)}) collective-permute-start(f32[16,128]{1,0:T(8,128)S(1)} %get-tuple-element.31), channel_id=1, source_target_pairs={{0,1},{1,0},{2,3},{3,2},{4,5},{5,4},{6,7},{7,6},{8,9},{9,8},{10,11... | collective-permute-start | bytes 24584 | tf_op jit(solution)/shard_map/ppermute | solution.py:529
  7.5 5.5 %collective-permute-start.3 = (f32[16,128]{1,0:T(8,128)S(1)}, f32[16,128]{1,0:T(8,128)S(1)}, u32[]{:S(2)}, u32[]{:S(2)}) collective-permute-start(f32[16,128]{1,0:T(8,128)S(1)} %get-tuple-element.32), channel_id=1, source_target_pairs={{0,4},{1,2},{2,1},{3,7},{4,0},{5,6},{6,5},{7,3},{8,12},{9,10},{10,... | collective-permute-start | bytes 24584 | tf_op jit(solution)/shard_map/ppermute | solution.py:529
  13.5 4.3 %collective-permute-start.4 = (f32[32,128]{1,0:T(8,128)S(1)}, f32[32,128]{1,0:T(8,128)S(1)}, u32[]{:S(2)}, u32[]{:S(2)}) collective-permute-start(f32[32,128]{1,0:T(8,128)S(1)} %shard_map.53.left_late), channel_id=1, source_target_pairs={{0,1},{1,0},{2,3},{3,2},{4,5},{5,4},{6,7},{7,6},{8,9},{9,8},{10,11... | collective-permute-start | bytes 49160 | tf_op jit(solution)/shard_map/ppermute | solution.py:529
  14.4 4.4 %collective-permute-start.5 = (f32[32,128]{1,0:T(8,128)S(1)}, f32[32,128]{1,0:T(8,128)S(1)}, u32[]{:S(2)}, u32[]{:S(2)}) collective-permute-start(f32[32,128]{1,0:T(8,128)S(1)} %shard_map.53.left_late), channel_id=1, source_target_pairs={{0,1},{1,0},{2,3},{3,2},{4,5},{5,4},{6,7},{7,6},{8,9},{9,8},{10,11... | collective-permute-start | bytes 49160 | tf_op jit(solution)/shard_map/ppermute | solution.py:529
  16.4 3.7 %collective-permute-start.6 = (f32[32,128]{1,0:T(8,128)S(1)}, f32[32,128]{1,0:T(8,128)S(1)}, u32[]{:S(2)}, u32[]{:S(2)}) collective-permute-start(f32[32,128]{1,0:T(8,128)S(1)} %shard_map.53.left_late), channel_id=1, source_target_pairs={{0,1},{1,2},{2,3},{3,19},{4,5},{5,6},{6,7},{7,23},{8,9},{9,10},{10... | collective-permute-start | bytes 49160 | tf_op jit(solution)/shard_map/ppermute | solution.py:529
  20.2 4.0 %collective-permute-start.7 = (f32[16,512]{1,0:T(8,128)S(1)}, f32[16,512]{1,0:T(8,128)S(1)}, u32[]{:S(2)}, u32[]{:S(2)}) collective-permute-start(f32[16,512]{1,0:T(8,128)S(1)} %shard_map.54.mid_ref), channel_id=1, source_target_pairs={{0,4},{1,5},{2,6},{3,7},{4,0},{5,1},{6,2},{7,3},{8,12},{9,13},{10,... | collective-permute-start | bytes 98312 | tf_op jit(solution)/shard_map/ppermute | solution.py:529
  21.4 3.9 %collective-permute-start.8 = (f32[16,512]{1,0:T(8,128)S(1)}, f32[16,512]{1,0:T(8,128)S(1)}, u32[]{:S(2)}, u32[]{:S(2)}) collective-permute-start(f32[16,512]{1,0:T(8,128)S(1)} %shard_map.54.mid_ref), channel_id=1, source_target_pairs={{0,1},{1,0},{2,3},{3,2},{4,8},{5,9},{6,10},{7,11},{8,4},{9,5},{10,... | collective-permute-start | bytes 98312 | tf_op jit(solution)/shard_map/ppermute | solution.py:529

commit v5 on v4

--- a/solution.py
+++ b/solution.py
@@ -377,17 +377,20 @@
     )(after, jnp.asarray(trig, F32))
 
 
-def late_kernel(index_ref, other_ref, keep, table_ref, back_in, out_ref):
+def late_kernel(index_ref, other_ref, keep, table_ref, back_in, new_ref, out_ref):
     odd = odd_date() == 1
     side = jnp.where(odd, 0, 1)
     index = index_ref[...]
     planes = []
     for p in range(PAIRS_DEV):
         planes += cross(keep.at[side], index[0, p], other_ref, index[0, PAIRS_DEV + p])
-    cells = pooled(planes, table_ref[...])
-    cells = jnp.where(odd, cells[:, :, :128], cells[:, :, 128:])
-    new = message(cells, 0)
-    out_ref[:16] = jnp.where(odd | lower_lanes((16, 128)), new, -new)
+    table = table_ref[:, pl.ds(pl.multiple_of(128 * side, 128), 128)]
+    high, low = split(jnp.concatenate(planes, axis=0))
+    cells = mm(high, table) + mm(low, table)
+    new = message(cells.reshape(len(planes), 16, 128), 0) * (1.0 / (LOOK_R * LOOK_C))
+    new = jnp.where(odd | lower_lanes((16, 128)), new, -new)
+    new_ref[...] = new
+    out_ref[:16] = new
     out_ref[16:] = back_in[...]
 
 
@@ -395,9 +398,9 @@
     vmem = pl.BlockSpec(memory_space=pltpu.VMEM)
     return pl.pallas_call(
         late_kernel,
-        out_shape=jax.ShapeDtypeStruct((32, 128), F32),
+        out_shape=(jax.ShapeDtypeStruct((16, 128), F32), jax.ShapeDtypeStruct((32, 128), F32)),
         in_specs=[vmem] * 5,
-        out_specs=vmem,
+        out_specs=(vmem, vmem),
         compiler_params=pltpu.CompilerParams(vmem_limit_bytes=24 * 2**20),
     )(*arrays)
 
@@ -409,9 +412,9 @@
     col = lax.axis_index("col")
     odd_col = col % 2 == 1
     before = jnp.where(crossing, before_late[:16], jnp.where(odd_col, first_ref[...], second_ref[...]))
-    after = jnp.where(crossing, after_late[:16], jnp.where(odd_col, second_ref[...], first_ref[...]))
+    after = jnp.where(crossing, after_late[...], jnp.where(odd_col, second_ref[...], first_ref[...]))
     mid_ref[:, :128] = jnp.where(col == 0, 0.0, before)
-    mid_ref[:, 128:256] = jnp.where(crossing, left_late[:16], left_early[...])
+    mid_ref[:, 128:256] = jnp.where(crossing, left_late[...], left_early[...])
     mid_ref[:, 256:384] = jnp.where(crossing, right_late[:16], right_early[...])
     mid_ref[:, 384:] = jnp.where(col == lax.axis_size("col") - 1, 0.0, after)
 
@@ -575,10 +578,10 @@
     two = send(two, swap_cols(False))
     tables = filter_tables(right)
     other, one, two = lax.optimization_barrier((other, one, two))
-    new = late(index, other, keep, look, back)
+    new, with_powers = late(index, other, keep, look, back)
     after = send(new, ring)
-    before = send(new, from_left)
-    right_late = send(new, straight)
+    before = send(with_powers, from_left)
+    right_late = send(with_powers, straight)
     mid = merge(crossing, before, right_late, after, new, one, two, left, right)
     one = send(mid, swap_rows(True))
     two = send(mid, swap_rows(False))

time: 27.6 us -> 27.5 us (level)
  transfers between devices with their start and end apart: 9 -> 9, of which waited for: 6 -> 5; matrix products, arithmetic and copies ran while one was open for 0% -> 0% of each run, Pallas kernels for 18% -> 19%
where the time goes in v5:
time: 27.5 us; the launch traced here: 26.9 us
  waiting for transfers between devices  11.7 us (43%)
  starting transfers between devices  7.27 us (26%)
  Pallas kernels  7.1 us (26%)
  between operations  0.72 us (3%)
    ppermute x9, waiting for transfers between devices, send(): return lax.ppermute(x, names, pairs)  11.7 us
    ppermute x9, starting transfers between devices, send(): return lax.ppermute(x, names, pairs)  7.27 us
    pallas_call x1, Pallas kernels, early(): pl.pallas_call(early_kernel, out_shape=out_shape, in_specs=[smem, pl.Bloc...  1.8 us
    pallas_call x1, Pallas kernels, goldstein(): pl.pallas_call(goldstein_kernel, out_shape=(jax.ShapeDtypeStruct((PAIRS_D...  1.71 us
    pallas_call x1, Pallas kernels, within_chip(): pl.pallas_call(chip_kernel, out_shape=[jax.ShapeDtypeStruct((16, 128), F3...  1.67 us
    pallas_call x1, Pallas kernels, pack(): pl.pallas_call(pack_kernel, out_shape=pltpu.VMEM((SPAN, 5, 80, 128), F32)...  1.37 us
  transfers between devices with their start and end apart: 9, of which 5 were waited for; matrix products, arithmetic and copies ran while one was open for 0% of the time, Pallas kernels for 19%

profile of v5, /device:TPU:148, one launch (start us, length us, event | category | flops | bytes accessed | tf_op | source)
XLA Modules:
  0.0 26.9 jit_solution(10888044979655330169)
XLA Ops:
  0.6 0.0 copy-start
  0.6 0.0 copy-start.2
  0.6 0.1 collective-permute-start.1
  0.7 1.4 %shard_map.51 = f32[3,5,80,128]{3,2,1,0:T(8,128)S(1)} custom-call(f32[4,2,80,640]{3,2,1,0:T(8,128)} %stack_ref.3), custom_call_target="tpu_custom_call" | custom-call | tf_op jit(solution)/shard_map/pallas_call | solution.py:159
  2.1 0.2 collective-permute-start
  2.3 0.1 copy-done
  2.4 0.0 copy-done.2
  2.4 1.8 %shard_map.50 = (f32[16,128]{1,0:T(8,128)S(1)}, f32[16,128]{1,0:T(8,128)S(1)}, f32[16,128]{1,0:T(8,128)S(1)}, f32[16,128]{1,0:T(8,128)S(1)}, f32[16,128]{1,0:T(8...) custom-call(s32[2,64]{1,0:T(2,128)S(1)} %bitcast.1, ...), custom_call_target="tpu_custom_call" | custom-call | flops 1000000000 | bytes 10000000 | tf_op jit(solution)/shard_map/pallas_call | solution.py:279
  4.2 0.2 collective-permute-done.1.other_ref
  4.5 1.7 %shard_map.52 = (f32[16,128]{1,0:T(8,128)S(1)}, f32[16,128]{1,0:T(8,128)S(1)}, f32[16,128]{1,0:T(8,128)S(1)}, f32[16,128]{1,0:T(8,128)S(1)}, f32[16,128]{1,0:T(8,128)S(1)}) custom-call(s32[2,64]{1,0:T(2,128)S(1)} %bitcast.2, f32[4,2,80,640]{3,2,1,0:T(8,128)S(1)} %collective-permute-done.1.other_ref, f32[2,4,5,80,128]{4,3,2,1,0:T(8,128)S(1)} %get-tuple-element.28.keep, ...), custom_call_target="tpu_custom_call" | custom-call | flops 1000000000 | bytes 10000000 | tf_op jit(solution)/shard_map/pallas_call | solution.py:333
  6.1 0.0 copy-start.1
  6.1 1.4 %collective-permute-start.2 = (f32[16,128]{1,0:T(8,128)S(1)}, f32[16,128]{1,0:T(8,128)S(1)}, u32[]{:S(2)}, u32[]{:S(2)}) collective-permute-start(f32[16,128]{1,0:T(8,128)S(1)} %get-tuple-element.33), channel_id=1, source_target_pairs={{0,1},{1,0},{2,3},{3,2},{4,5},{5,4},{6,7},{7,6},{8,9},{9,8},{10,11... | collective-permute-start | bytes 24584 | tf_op jit(solution)/shard_map/ppermute | solution.py:532
  7.5 0.0 collective-permute-start.3
  7.5 5.5 %collective-permute-done.other_ref = f32[3,5,80,128]{3,2,1,0:T(8,128)S(1)} collective-permute-done((f32[3,5,80,128]{3,2,1,0:T(8,128)S(1)}, f32[3,5,80,128]{3,2,1,0:T(8,128)S(1)}, u32[]{:S(2)}, u32[]{:S(2)}) %collective-permute-start) | collective-permute-done | bytes 614432 | tf_op jit(solution)/shard_map/ppermute | solution.py:532
  13.0 0.0 collective-permute-done.2.first_ref
  13.0 0.0 collective-permute-done.3.second_ref
  13.0 0.4 %shard_map.53 = (f32[16,128]{1,0:T(8,128)S(1)}, f32[32,128]{1,0:T(8,128)S(1)}) custom-call(s32[8,128]{1,0:T(8,128)S(1)} %get-tuple-element.27.index_ref, f32[3,5,80,128]{3,2,1,0:T(8,128)S(1)} %collective-permute-done.other_ref, f32[2,4,5,80,128]{4,3,2,1,0:T(8,128)S(1)} %get-tuple-element.28.keep, bf16[384,256]{1,0:T(8,128)(2,1)S(1)} %get-tuple-element.29.table_ref, ...), custom_call_target="tpu_custom_call" | custom-call | tf_op jit(solution)/shard_map/pallas_call | solution.py:399
  13.4 0.9 %collective-permute-start.4 = (f32[32,128]{1,0:T(8,128)S(1)}, f32[32,128]{1,0:T(8,128)S(1)}, u32[]{:S(2)}, u32[]{:S(2)}) collective-permute-start(f32[32,128]{1,0:T(8,128)S(1)} %get-tuple-element.37), channel_id=1, source_target_pairs={{0,1},{1,0},{2,3},{3,2},{4,5},{5,4},{6,7},{7,6},{8,9},{9,8},{10,11... | collective-permute-start | bytes 49160 | tf_op jit(solution)/shard_map/ppermute | solution.py:532
  14.3 2.0 %collective-permute-start.5 = (f32[32,128]{1,0:T(8,128)S(1)}, f32[32,128]{1,0:T(8,128)S(1)}, u32[]{:S(2)}, u32[]{:S(2)}) collective-permute-start(f32[32,128]{1,0:T(8,128)S(1)} %get-tuple-element.37), channel_id=1, source_target_pairs={{0,1},{1,0},{2,3},{3,2},{4,5},{5,4},{6,7},{7,6},{8,9},{9,8},{10,11... | collective-permute-start | bytes 49160 | tf_op jit(solution)/shard_map/ppermute | solution.py:532
  16.3 1.4 %collective-permute-start.6 = (f32[16,128]{1,0:T(8,128)S(1)}, f32[16,128]{1,0:T(8,128)S(1)}, u32[]{:S(2)}, u32[]{:S(2)}) collective-permute-start(f32[16,128]{1,0:T(8,128)S(1)} %get-tuple-element.38.left_late), channel_id=1, source_target_pairs={{0,1},{1,2},{2,3},{3,19},{4,5},{5,6},{6,7},{7,23},{8,9},{9,10},{10... | collective-permute-start | bytes 24584 | tf_op jit(solution)/shard_map/ppermute | solution.py:532
  17.7 2.3 %collective-permute-done.6.after_late = f32[16,128]{1,0:T(8,128)S(1)} collective-permute-done((f32[16,128]{1,0:T(8,128)S(1)}, f32[16,128]{1,0:T(8,128)S(1)}, u32[]{:S(2)}, u32[]{:S(2)}) %collective-permute-start.6) | collective-permute-done | bytes 8224 | tf_op jit(solution)/shard_map/ppermute | solution.py:532
  20.0 0.0 collective-permute-done.4.before_late
  20.0 0.0 collective-permute-done.5.right_late.late_ref
  20.0 1.3 %collective-permute-start.7 = (f32[16,512]{1,0:T(8,128)S(1)}, f32[16,512]{1,0:T(8,128)S(1)}, u32[]{:S(2)}, u32[]{:S(2)}) collective-permute-start(f32[16,512]{1,0:T(8,128)S(1)} %shard_map.54.mid_ref), channel_id=1, source_target_pairs={{0,4},{1,5},{2,6},{3,7},{4,0},{5,1},{6,2},{7,3},{8,12},{9,13},{10,... | collective-permute-start | bytes 98312 | tf_op jit(solution)/shard_map/ppermute | solution.py:532
  21.3 0.0 collective-permute-start.8
  21.3 0.0 copy-done.1
  21.3 0.1 shard_map.55
  21.5 2.6 %collective-permute-done.7.first_swap = f32[16,512]{1,0:T(8,128)S(1)} collective-permute-done((f32[16,512]{1,0:T(8,128)S(1)}, f32[16,512]{1,0:T(8,128)S(1)}, u32[]{:S(2)}, u32[]{:S(2)}) %collective-permute-start.7) | collective-permute-done | bytes 32800 | tf_op jit(solution)/shard_map/ppermute | solution.py:532
  24.0 1.2 %collective-permute-done.8.second_swap = f32[16,512]{1,0:T(8,128)S(1)} collective-permute-done((f32[16,512]{1,0:T(8,128)S(1)}, f32[16,512]{1,0:T(8,128)S(1)}, u32[]{:S(2)}, u32[]{:S(2)}) %collective-permute-start.8) | collective-permute-done | bytes 32800 | tf_op jit(solution)/shard_map/ppermute | solution.py:532
  25.2 1.7 %shard_map.56 = (f32[4,2,16,32]{3,2,1,0:T(8,128)}, f32[4,16,32]{2,1,0:T(8,128)}) custom-call(f32[16,512]{1,0:T(8,128)S(1)} %collective-permute-done.7.first_swap, f32[16,512]{1,0:T(8,128)S(1)} %shard_map.54.mid_ref, f32[16,512]{1,0:T(8,128)S(1)} %collective-permute-done.8.second_swap, bf16[128,128]{1,0:T(8,128)(2,1)S(1)} %get-tuple-element.43.ns_ref, ...), custom_call_target="tpu_custom_call" | custom-call | tf_op jit(solution)/shard_map/pallas_call | solution.py:504
  (1 shorter events, 0.0 us)
Async XLA Ops:
  0.6 1.8 %copy-start = (f32[4,2,80,640]{3,2,1,0:T(8,128)S(1)}, f32[4,2,80,640]{3,2,1,0:T(8,128)}, u32[]{:S(2)}) copy-start(f32[4,2,80,640]{3,2,1,0:T(8,128)} %stack_ref.3) | copy-start | bytes 4915204
  0.6 1.8 %copy-start.2 = (s32[64,2]{0,1:T(2,128)S(1)}, s32[64,2]{0,1:T(2,128)}, u32[]{:S(2)}) copy-start(s32[64,2]{0,1:T(2,128)} %param.4) | copy-start | bytes 1540
  0.6 3.8 %collective-permute-start.1 = (f32[4,2,80,640]{3,2,1,0:T(8,128)}, f32[4,2,80,640]{3,2,1,0:T(8,128)S(1)}, u32[]{:S(2)}, u32[]{:S(2)}) collective-permute-start(f32[4,2,80,640]{3,2,1,0:T(8,128)} %stack_ref.3), channel_id=1, source_target_pairs={{0,16},{1,17},{2,18},{3,19},{4,20},{5,21},{6,22},{7,23},{8,24},{9,... | collective-permute-start | bytes 4915208 | tf_op jit(solution)/shard_map/ppermute | solution.py:532
  2.1 10.9 %collective-permute-start = (f32[3,5,80,128]{3,2,1,0:T(8,128)S(1)}, f32[3,5,80,128]{3,2,1,0:T(8,128)S(1)}, u32[]{:S(2)}, u32[]{:S(2)}) collective-permute-start(f32[3,5,80,128]{3,2,1,0:T(8,128)S(1)} %shard_map.51), channel_id=1, source_target_pairs={{0,1},{1,0},{2,3},{3,2},{4,5},{5,4},{6,7},{7,6},{8,9},{9,8},{10,11... | collective-permute-start | bytes 1843208 | tf_op jit(solution)/shard_map/ppermute | solution.py:532
  6.1 15.2 %copy-start.1 = (f32[704,256]{1,0:T(8,128)S(1)}, f32[704,256]{1,0:T(8,128)}, u32[]{:S(2)}) copy-start(f32[704,256]{1,0:T(8,128)} %constant.2.clone.trig_ref) | copy-start | bytes 2162692
  6.1 6.9 %collective-permute-start.2 = (f32[16,128]{1,0:T(8,128)S(1)}, f32[16,128]{1,0:T(8,128)S(1)}, u32[]{:S(2)}, u32[]{:S(2)}) collective-permute-start(f32[16,128]{1,0:T(8,128)S(1)} %get-tuple-element.33), channel_id=1, source_target_pairs={{0,1},{1,0},{2,3},{3,2},{4,5},{5,4},{6,7},{7,6},{8,9},{9,8},{10,11... | collective-permute-start | bytes 24584 | tf_op jit(solution)/shard_map/ppermute | solution.py:532
  7.5 5.5 %collective-permute-start.3 = (f32[16,128]{1,0:T(8,128)S(1)}, f32[16,128]{1,0:T(8,128)S(1)}, u32[]{:S(2)}, u32[]{:S(2)}) collective-permute-start(f32[16,128]{1,0:T(8,128)S(1)} %get-tuple-element.34), channel_id=1, source_target_pairs={{0,4},{1,2},{2,1},{3,7},{4,0},{5,6},{6,5},{7,3},{8,12},{9,10},{10,... | collective-permute-start | bytes 24584 | tf_op jit(solution)/shard_map/ppermute | solution.py:532
  13.4 6.6 %collective-permute-start.4 = (f32[32,128]{1,0:T(8,128)S(1)}, f32[32,128]{1,0:T(8,128)S(1)}, u32[]{:S(2)}, u32[]{:S(2)}) collective-permute-start(f32[32,128]{1,0:T(8,128)S(1)} %get-tuple-element.37), channel_id=1, source_target_pairs={{0,1},{1,0},{2,3},{3,2},{4,5},{5,4},{6,7},{7,6},{8,9},{9,8},{10,11... | collective-permute-start | bytes 49160 | tf_op jit(solution)/shard_map/ppermute | solution.py:532
  14.3 5.7 %collective-permute-start.5 = (f32[32,128]{1,0:T(8,128)S(1)}, f32[32,128]{1,0:T(8,128)S(1)}, u32[]{:S(2)}, u32[]{:S(2)}) collective-permute-start(f32[32,128]{1,0:T(8,128)S(1)} %get-tuple-element.37), channel_id=1, source_target_pairs={{0,1},{1,0},{2,3},{3,2},{4,5},{5,4},{6,7},{7,6},{8,9},{9,8},{10,11... | collective-permute-start | bytes 49160 | tf_op jit(solution)/shard_map/ppermute | solution.py:532
  16.3 3.7 %collective-permute-start.6 = (f32[16,128]{1,0:T(8,128)S(1)}, f32[16,128]{1,0:T(8,128)S(1)}, u32[]{:S(2)}, u32[]{:S(2)}) collective-permute-start(f32[16,128]{1,0:T(8,128)S(1)} %get-tuple-element.38.left_late), channel_id=1, source_target_pairs={{0,1},{1,2},{2,3},{3,19},{4,5},{5,6},{6,7},{7,23},{8,9},{9,10},{10... | collective-permute-start | bytes 24584 | tf_op jit(solution)/shard_map/ppermute | solution.py:532
  20.0 4.0 %collective-permute-start.7 = (f32[16,512]{1,0:T(8,128)S(1)}, f32[16,512]{1,0:T(8,128)S(1)}, u32[]{:S(2)}, u32[]{:S(2)}) collective-permute-start(f32[16,512]{1,0:T(8,128)S(1)} %shard_map.54.mid_ref), channel_id=1, source_target_pairs={{0,4},{1,5},{2,6},{3,7},{4,0},{5,1},{6,2},{7,3},{8,12},{9,13},{10,... | collective-permute-start | bytes 98312 | tf_op jit(solution)/shard_map/ppermute | solution.py:532
  21.3 3.9 %collective-permute-start.8 = (f32[16,512]{1,0:T(8,128)S(1)}, f32[16,512]{1,0:T(8,128)S(1)}, u32[]{:S(2)}, u32[]{:S(2)}) collective-permute-start(f32[16,512]{1,0:T(8,128)S(1)} %shard_map.54.mid_ref), channel_id=1, source_target_pairs={{0,1},{1,0},{2,3},{3,2},{4,8},{5,9},{6,10},{7,11},{8,4},{9,5},{10,... | collective-permute-start | bytes 98312 | tf_op jit(solution)/shard_map/ppermute | solution.py:532

commit v6 on v5

--- a/solution.py
+++ b/solution.py
@@ -541,7 +541,7 @@
     def swap_rows(first):
         def target(d, r, c):
             b = neighbour(r, rows, first)
-            return (d, b, c) if b != r else (d, r, c ^ 1)
+            return (d, b, c) if b != r else (d ^ 1, r, c)
 
         return target
 

time: 27.5 us -> 27.2 us (0.989); the launches traced: 26.9 us -> 26.9 us
  no operation moved by 1% of the time
where the time goes in v6:
time: 27.2 us; the launch traced here: 26.9 us
  waiting for transfers between devices  11.7 us (43%)
  starting transfers between devices  7.27 us (27%)
  Pallas kernels  7.12 us (26%)
  between operations  0.72 us (3%)
    ppermute x9, waiting for transfers between devices, send(): return lax.ppermute(x, names, pairs)  11.7 us
    ppermute x9, starting transfers between devices, send(): return lax.ppermute(x, names, pairs)  7.27 us
    pallas_call x1, Pallas kernels, early(): pl.pallas_call(early_kernel, out_shape=out_shape, in_specs=[smem, pl.Bloc...  1.81 us
    pallas_call x1, Pallas kernels, goldstein(): pl.pallas_call(goldstein_kernel, out_shape=(jax.ShapeDtypeStruct((PAIRS_D...  1.71 us
    pallas_call x1, Pallas kernels, within_chip(): pl.pallas_call(chip_kernel, out_shape=[jax.ShapeDtypeStruct((16, 128), F3...  1.68 us
    pallas_call x1, Pallas kernels, pack(): pl.pallas_call(pack_kernel, out_shape=pltpu.VMEM((SPAN, 5, 80, 128), F32)...  1.37 us
  transfers between devices with their start and end apart: 9, of which 5 were waited for; matrix products, arithmetic and copies ran while one was open for 0% of the time, Pallas kernels for 19%

profile of v6, /device:TPU:148, one launch (start us, length us, event | category | flops | bytes accessed | tf_op | source)
XLA Modules:
  0.0 26.9 jit_solution(7115491703699855736)
XLA Ops:
  0.6 0.0 copy-start
  0.6 0.0 copy-start.2
  0.6 0.1 collective-permute-start.1
  0.7 1.4 %shard_map.51 = f32[3,5,80,128]{3,2,1,0:T(8,128)S(1)} custom-call(f32[4,2,80,640]{3,2,1,0:T(8,128)} %stack_ref.3), custom_call_target="tpu_custom_call" | custom-call | tf_op jit(solution)/shard_map/pallas_call | solution.py:159
  2.1 0.2 collective-permute-start
  2.3 0.1 copy-done
  2.4 0.0 copy-done.2
  2.4 1.8 %shard_map.50 = (f32[16,128]{1,0:T(8,128)S(1)}, f32[16,128]{1,0:T(8,128)S(1)}, f32[16,128]{1,0:T(8,128)S(1)}, f32[16,128]{1,0:T(8,128)S(1)}, f32[16,128]{1,0:T(8...) custom-call(s32[2,64]{1,0:T(2,128)S(1)} %bitcast.1, ...), custom_call_target="tpu_custom_call" | custom-call | flops 1000000000 | bytes 10000000 | tf_op jit(solution)/shard_map/pallas_call | solution.py:279
  4.2 0.2 collective-permute-done.1.other_ref
  4.5 1.7 %shard_map.52 = (f32[16,128]{1,0:T(8,128)S(1)}, f32[16,128]{1,0:T(8,128)S(1)}, f32[16,128]{1,0:T(8,128)S(1)}, f32[16,128]{1,0:T(8,128)S(1)}, f32[16,128]{1,0:T(8,128)S(1)}) custom-call(s32[2,64]{1,0:T(2,128)S(1)} %bitcast.2, f32[4,2,80,640]{3,2,1,0:T(8,128)S(1)} %collective-permute-done.1.other_ref, f32[2,4,5,80,128]{4,3,2,1,0:T(8,128)S(1)} %get-tuple-element.28.keep, ...), custom_call_target="tpu_custom_call" | custom-call | flops 1000000000 | bytes 10000000 | tf_op jit(solution)/shard_map/pallas_call | solution.py:333
  6.1 0.0 copy-start.1
  6.1 1.4 %collective-permute-start.2 = (f32[16,128]{1,0:T(8,128)S(1)}, f32[16,128]{1,0:T(8,128)S(1)}, u32[]{:S(2)}, u32[]{:S(2)}) collective-permute-start(f32[16,128]{1,0:T(8,128)S(1)} %get-tuple-element.33), channel_id=1, source_target_pairs={{0,1},{1,0},{2,3},{3,2},{4,5},{5,4},{6,7},{7,6},{8,9},{9,8},{10,11... | collective-permute-start | bytes 24584 | tf_op jit(solution)/shard_map/ppermute | solution.py:532
  7.5 0.0 collective-permute-start.3
  7.5 5.5 %collective-permute-done.other_ref = f32[3,5,80,128]{3,2,1,0:T(8,128)S(1)} collective-permute-done((f32[3,5,80,128]{3,2,1,0:T(8,128)S(1)}, f32[3,5,80,128]{3,2,1,0:T(8,128)S(1)}, u32[]{:S(2)}, u32[]{:S(2)}) %collective-permute-start) | collective-permute-done | bytes 614432 | tf_op jit(solution)/shard_map/ppermute | solution.py:532
  13.0 0.0 collective-permute-done.2.first_ref
  13.0 0.0 collective-permute-done.3.second_ref
  13.0 0.4 %shard_map.53 = (f32[16,128]{1,0:T(8,128)S(1)}, f32[32,128]{1,0:T(8,128)S(1)}) custom-call(s32[8,128]{1,0:T(8,128)S(1)} %get-tuple-element.27.index_ref, f32[3,5,80,128]{3,2,1,0:T(8,128)S(1)} %collective-permute-done.other_ref, f32[2,4,5,80,128]{4,3,2,1,0:T(8,128)S(1)} %get-tuple-element.28.keep, bf16[384,256]{1,0:T(8,128)(2,1)S(1)} %get-tuple-element.29.table_ref, ...), custom_call_target="tpu_custom_call" | custom-call | tf_op jit(solution)/shard_map/pallas_call | solution.py:399
  13.4 0.9 %collective-permute-start.4 = (f32[32,128]{1,0:T(8,128)S(1)}, f32[32,128]{1,0:T(8,128)S(1)}, u32[]{:S(2)}, u32[]{:S(2)}) collective-permute-start(f32[32,128]{1,0:T(8,128)S(1)} %get-tuple-element.37), channel_id=1, source_target_pairs={{0,1},{1,0},{2,3},{3,2},{4,5},{5,4},{6,7},{7,6},{8,9},{9,8},{10,11... | collective-permute-start | bytes 49160 | tf_op jit(solution)/shard_map/ppermute | solution.py:532
  14.3 2.0 %collective-permute-start.5 = (f32[32,128]{1,0:T(8,128)S(1)}, f32[32,128]{1,0:T(8,128)S(1)}, u32[]{:S(2)}, u32[]{:S(2)}) collective-permute-start(f32[32,128]{1,0:T(8,128)S(1)} %get-tuple-element.37), channel_id=1, source_target_pairs={{0,1},{1,0},{2,3},{3,2},{4,5},{5,4},{6,7},{7,6},{8,9},{9,8},{10,11... | collective-permute-start | bytes 49160 | tf_op jit(solution)/shard_map/ppermute | solution.py:532
  16.3 1.4 %collective-permute-start.6 = (f32[16,128]{1,0:T(8,128)S(1)}, f32[16,128]{1,0:T(8,128)S(1)}, u32[]{:S(2)}, u32[]{:S(2)}) collective-permute-start(f32[16,128]{1,0:T(8,128)S(1)} %get-tuple-element.38.left_late), channel_id=1, source_target_pairs={{0,1},{1,2},{2,3},{3,19},{4,5},{5,6},{6,7},{7,23},{8,9},{9,10},{10... | collective-permute-start | bytes 24584 | tf_op jit(solution)/shard_map/ppermute | solution.py:532
  17.7 2.3 %collective-permute-done.6.after_late = f32[16,128]{1,0:T(8,128)S(1)} collective-permute-done((f32[16,128]{1,0:T(8,128)S(1)}, f32[16,128]{1,0:T(8,128)S(1)}, u32[]{:S(2)}, u32[]{:S(2)}) %collective-permute-start.6) | collective-permute-done | bytes 8224 | tf_op jit(solution)/shard_map/ppermute | solution.py:532
  20.0 0.0 collective-permute-done.4.before_late
  20.0 0.0 collective-permute-done.5.right_late.late_ref
  20.0 1.3 %collective-permute-start.7 = (f32[16,512]{1,0:T(8,128)S(1)}, f32[16,512]{1,0:T(8,128)S(1)}, u32[]{:S(2)}, u32[]{:S(2)}) collective-permute-start(f32[16,512]{1,0:T(8,128)S(1)} %shard_map.54.mid_ref), channel_id=1, source_target_pairs={{0,4},{1,5},{2,6},{3,7},{4,0},{5,1},{6,2},{7,3},{8,12},{9,13},{10,... | collective-permute-start | bytes 98312 | tf_op jit(solution)/shard_map/ppermute | solution.py:532
  21.3 0.0 collective-permute-start.8
  21.3 0.0 copy-done.1
  21.3 0.1 shard_map.55
  21.5 2.6 %collective-permute-done.7.first_swap = f32[16,512]{1,0:T(8,128)S(1)} collective-permute-done((f32[16,512]{1,0:T(8,128)S(1)}, f32[16,512]{1,0:T(8,128)S(1)}, u32[]{:S(2)}, u32[]{:S(2)}) %collective-permute-start.7) | collective-permute-done | bytes 32800 | tf_op jit(solution)/shard_map/ppermute | solution.py:532
  24.0 1.2 %collective-permute-done.8.second_swap = f32[16,512]{1,0:T(8,128)S(1)} collective-permute-done((f32[16,512]{1,0:T(8,128)S(1)}, f32[16,512]{1,0:T(8,128)S(1)}, u32[]{:S(2)}, u32[]{:S(2)}) %collective-permute-start.8) | collective-permute-done | bytes 32800 | tf_op jit(solution)/shard_map/ppermute | solution.py:532
  25.2 1.7 %shard_map.56 = (f32[4,2,16,32]{3,2,1,0:T(8,128)}, f32[4,16,32]{2,1,0:T(8,128)}) custom-call(f32[16,512]{1,0:T(8,128)S(1)} %collective-permute-done.7.first_swap, f32[16,512]{1,0:T(8,128)S(1)} %shard_map.54.mid_ref, f32[16,512]{1,0:T(8,128)S(1)} %collective-permute-done.8.second_swap, bf16[128,128]{1,0:T(8,128)(2,1)S(1)} %get-tuple-element.43.ns_ref, ...), custom_call_target="tpu_custom_call" | custom-call | tf_op jit(solution)/shard_map/pallas_call | solution.py:504
  (1 shorter events, 0.0 us)
Async XLA Ops:
  0.6 1.8 %copy-start = (f32[4,2,80,640]{3,2,1,0:T(8,128)S(1)}, f32[4,2,80,640]{3,2,1,0:T(8,128)}, u32[]{:S(2)}) copy-start(f32[4,2,80,640]{3,2,1,0:T(8,128)} %stack_ref.3) | copy-start | bytes 4915204
  0.6 1.8 %copy-start.2 = (s32[64,2]{0,1:T(2,128)S(1)}, s32[64,2]{0,1:T(2,128)}, u32[]{:S(2)}) copy-start(s32[64,2]{0,1:T(2,128)} %param.4) | copy-start | bytes 1540
  0.6 3.8 %collective-permute-start.1 = (f32[4,2,80,640]{3,2,1,0:T(8,128)}, f32[4,2,80,640]{3,2,1,0:T(8,128)S(1)}, u32[]{:S(2)}, u32[]{:S(2)}) collective-permute-start(f32[4,2,80,640]{3,2,1,0:T(8,128)} %stack_ref.3), channel_id=1, source_target_pairs={{0,16},{1,17},{2,18},{3,19},{4,20},{5,21},{6,22},{7,23},{8,24},{9,... | collective-permute-start | bytes 4915208 | tf_op jit(solution)/shard_map/ppermute | solution.py:532
  2.1 10.9 %collective-permute-start = (f32[3,5,80,128]{3,2,1,0:T(8,128)S(1)}, f32[3,5,80,128]{3,2,1,0:T(8,128)S(1)}, u32[]{:S(2)}, u32[]{:S(2)}) collective-permute-start(f32[3,5,80,128]{3,2,1,0:T(8,128)S(1)} %shard_map.51), channel_id=1, source_target_pairs={{0,1},{1,0},{2,3},{3,2},{4,5},{5,4},{6,7},{7,6},{8,9},{9,8},{10,11... | collective-permute-start | bytes 1843208 | tf_op jit(solution)/shard_map/ppermute | solution.py:532
  6.1 15.2 %copy-start.1 = (f32[704,256]{1,0:T(8,128)S(1)}, f32[704,256]{1,0:T(8,128)}, u32[]{:S(2)}) copy-start(f32[704,256]{1,0:T(8,128)} %constant.2.clone.trig_ref) | copy-start | bytes 2162692
  6.1 6.9 %collective-permute-start.2 = (f32[16,128]{1,0:T(8,128)S(1)}, f32[16,128]{1,0:T(8,128)S(1)}, u32[]{:S(2)}, u32[]{:S(2)}) collective-permute-start(f32[16,128]{1,0:T(8,128)S(1)} %get-tuple-element.33), channel_id=1, source_target_pairs={{0,1},{1,0},{2,3},{3,2},{4,5},{5,4},{6,7},{7,6},{8,9},{9,8},{10,11... | collective-permute-start | bytes 24584 | tf_op jit(solution)/shard_map/ppermute | solution.py:532
  7.5 5.5 %collective-permute-start.3 = (f32[16,128]{1,0:T(8,128)S(1)}, f32[16,128]{1,0:T(8,128)S(1)}, u32[]{:S(2)}, u32[]{:S(2)}) collective-permute-start(f32[16,128]{1,0:T(8,128)S(1)} %get-tuple-element.34), channel_id=1, source_target_pairs={{0,4},{1,2},{2,1},{3,7},{4,0},{5,6},{6,5},{7,3},{8,12},{9,10},{10,... | collective-permute-start | bytes 24584 | tf_op jit(solution)/shard_map/ppermute | solution.py:532
  13.4 6.6 %collective-permute-start.4 = (f32[32,128]{1,0:T(8,128)S(1)}, f32[32,128]{1,0:T(8,128)S(1)}, u32[]{:S(2)}, u32[]{:S(2)}) collective-permute-start(f32[32,128]{1,0:T(8,128)S(1)} %get-tuple-element.37), channel_id=1, source_target_pairs={{0,1},{1,0},{2,3},{3,2},{4,5},{5,4},{6,7},{7,6},{8,9},{9,8},{10,11... | collective-permute-start | bytes 49160 | tf_op jit(solution)/shard_map/ppermute | solution.py:532
  14.3 5.7 %collective-permute-start.5 = (f32[32,128]{1,0:T(8,128)S(1)}, f32[32,128]{1,0:T(8,128)S(1)}, u32[]{:S(2)}, u32[]{:S(2)}) collective-permute-start(f32[32,128]{1,0:T(8,128)S(1)} %get-tuple-element.37), channel_id=1, source_target_pairs={{0,1},{1,0},{2,3},{3,2},{4,5},{5,4},{6,7},{7,6},{8,9},{9,8},{10,11... | collective-permute-start | bytes 49160 | tf_op jit(solution)/shard_map/ppermute | solution.py:532
  16.3 3.7 %collective-permute-start.6 = (f32[16,128]{1,0:T(8,128)S(1)}, f32[16,128]{1,0:T(8,128)S(1)}, u32[]{:S(2)}, u32[]{:S(2)}) collective-permute-start(f32[16,128]{1,0:T(8,128)S(1)} %get-tuple-element.38.left_late), channel_id=1, source_target_pairs={{0,1},{1,2},{2,3},{3,19},{4,5},{5,6},{6,7},{7,23},{8,9},{9,10},{10... | collective-permute-start | bytes 24584 | tf_op jit(solution)/shard_map/ppermute | solution.py:532
  20.0 4.0 %collective-permute-start.7 = (f32[16,512]{1,0:T(8,128)S(1)}, f32[16,512]{1,0:T(8,128)S(1)}, u32[]{:S(2)}, u32[]{:S(2)}) collective-permute-start(f32[16,512]{1,0:T(8,128)S(1)} %shard_map.54.mid_ref), channel_id=1, source_target_pairs={{0,4},{1,5},{2,6},{3,7},{4,0},{5,1},{6,2},{7,3},{8,12},{9,13},{10,... | collective-permute-start | bytes 98312 | tf_op jit(solution)/shard_map/ppermute | solution.py:532
  21.3 3.9 %collective-permute-start.8 = (f32[16,512]{1,0:T(8,128)S(1)}, f32[16,512]{1,0:T(8,128)S(1)}, u32[]{:S(2)}, u32[]{:S(2)}) collective-permute-start(f32[16,512]{1,0:T(8,128)S(1)} %shard_map.54.mid_ref), channel_id=1, source_target_pairs={{0,16},{1,17},{2,18},{3,19},{4,8},{5,9},{6,10},{7,11},{8,4},{9,5},... | collective-permute-start | bytes 98312 | tf_op jit(solution)/shard_map/ppermute | solution.py:532

commit v7 on v6

--- a/solution.py
+++ b/solution.py
@@ -229,7 +229,7 @@
 
 def early_kernel(
     list_ref, stack_ref, left_ref, right_ref, first_ref, second_ref, back_ref, crossing_ref, index_ref, keep, look_out,
-    powers, middle, sem,
+    mine_ref, powers, middle, sem,
 ):
     keep_l, keep_r = keep.at[0], keep.at[1]
     copies = half_pair(stack_ref, 4, keep_l, keep_r, middle, sem)
@@ -243,12 +243,15 @@
     crossing_ref[...] = by_pair([jnp.full((16, 128), (b >= 4).astype(jnp.int32)) for a, b in own])
     lane = lax.broadcasted_iota(jnp.int32, (8, 128), 1)
     index = jnp.zeros((8, 128), jnp.int32)
+    mines = []
     for p in range(PAIRS_DEV):
-        mine = jnp.where(odd, own[p][0], jnp.clip(others[p][1] - 4, 0, 3))
+        mines.append(jnp.where(odd, own[p][0], jnp.clip(others[p][1] - 4, 0, 3)))
         theirs = jnp.where(odd, jnp.clip(own[p][1] - 4, 0, 2), jnp.clip(others[p][0] - 1, 0, 2))
-        index = jnp.where(lane == p, mine, jnp.where(lane == PAIRS_DEV + p, theirs, index))
+        index = jnp.where(lane == p, theirs, index)
     index_ref[...] = index
     half_pair_end(copies, 4, keep_l, keep_r, middle)
+    for p in range(PAIRS_DEV):
+        mine_ref[p] = keep[jnp.where(odd, 0, 1), mines[p]]
     planes_l, planes_r = [], []
     for a, b in own:
         planes_l += cross(keep_l, a, keep_l, jnp.minimum(b, 3))
@@ -275,6 +278,7 @@
         jax.ShapeDtypeStruct((8, 128), jnp.int32),
         jax.ShapeDtypeStruct((2, 4, 5, 80, 128), F32),
         jax.ShapeDtypeStruct((384, 256), BF16),
+        jax.ShapeDtypeStruct((PAIRS_DEV, 5, 80, 128), F32),
     ]
     return pl.pallas_call(
         early_kernel,
@@ -377,13 +381,13 @@
     )(after, jnp.asarray(trig, F32))
 
 
-def late_kernel(index_ref, other_ref, keep, table_ref, back_in, new_ref, out_ref):
+def late_kernel(index_ref, other_ref, mine_ref, table_ref, back_in, new_ref, out_ref):
     odd = odd_date() == 1
     side = jnp.where(odd, 0, 1)
     index = index_ref[...]
     planes = []
     for p in range(PAIRS_DEV):
-        planes += cross(keep.at[side], index[0, p], other_ref, index[0, PAIRS_DEV + p])
+        planes += cross(mine_ref, p, other_ref, index[0, p])
     table = table_ref[:, pl.ds(pl.multiple_of(128 * side, 128), 128)]
     high, low = split(jnp.concatenate(planes, axis=0))
     cells = mm(high, table) + mm(low, table)
@@ -572,13 +576,13 @@
     listed = pair_list.T
     other = send(pack(stack), straight)
     chip = send(stack, lambda d, r, c: (d ^ 1, r, c))
-    left, right, first, second, back, crossing, index, keep, look = early(listed, stack)
+    left, right, first, second, back, crossing, index, keep, look, mine = early(listed, stack)
     left, right, second, one, two = within_chip(listed, chip, keep, look, crossing, left, right, second)
     one = send(one, swap_cols(True))
     two = send(two, swap_cols(False))
     tables = filter_tables(right)
     other, one, two = lax.optimization_barrier((other, one, two))
-    new, with_powers = late(index, other, keep, look, back)
+    new, with_powers = late(index, other, mine, look, back)
     after = send(new, ring)
     before = send(with_powers, from_left)
     right_late = send(with_powers, straight)

time: 27.2 us -> 27.1 us (level)
  no operation moved by 1% of the time
where the time goes in v7:
time: 27.1 us; the launch traced here: 26.9 us
  waiting for transfers between devices  11.7 us (43%)
  starting transfers between devices  7.27 us (27%)
  Pallas kernels  7.13 us (26%)
  between operations  0.72 us (3%)
    ppermute x9, waiting for transfers between devices, send(): return lax.ppermute(x, names, pairs)  11.7 us
    ppermute x9, starting transfers between devices, send(): return lax.ppermute(x, names, pairs)  7.27 us
    pallas_call x1, Pallas kernels, early(): pl.pallas_call(early_kernel, out_shape=out_shape, in_specs=[smem, pl.Bloc...  1.89 us
    pallas_call x1, Pallas kernels, goldstein(): pl.pallas_call(goldstein_kernel, out_shape=(jax.ShapeDtypeStruct((PAIRS_D...  1.71 us
    pallas_call x1, Pallas kernels, within_chip(): pl.pallas_call(chip_kernel, out_shape=[jax.ShapeDtypeStruct((16, 128), F3...  1.64 us
    pallas_call x1, Pallas kernels, pack(): pl.pallas_call(pack_kernel, out_shape=pltpu.VMEM((SPAN, 5, 80, 128), F32)...  1.37 us
  transfers between devices with their start and end apart: 9, of which 5 were waited for; matrix products, arithmetic and copies ran while one was open for 0% of the time, Pallas kernels for 19%

profile of v7, /device:TPU:148, one launch (start us, length us, event | category | flops | bytes accessed | tf_op | source)
XLA Modules:
  0.0 26.9 jit_solution(17538564666027566021)
XLA Ops:
  0.6 0.0 copy-start
  0.6 0.0 copy-start.2
  0.6 0.1 collective-permute-start.1
  0.7 1.4 %shard_map.51 = f32[3,5,80,128]{3,2,1,0:T(8,128)S(1)} custom-call(f32[4,2,80,640]{3,2,1,0:T(8,128)} %stack_ref.3), custom_call_target="tpu_custom_call" | custom-call | tf_op jit(solution)/shard_map/pallas_call | solution.py:159
  2.1 0.2 collective-permute-start
  2.3 0.1 copy-done
  2.4 0.0 copy-done.2
  2.4 1.9 %shard_map.50 = (f32[16,128]{1,0:T(8,128)S(1)}, f32[16,128]{1,0:T(8,128)S(1)}, f32[16,128]{1,0:T(8,128)S(1)}, f32[16,128]{1,0:T(8,128)S(1)}, f32[16,128]{1,0:T(8...) custom-call(s32[2,64]{1,0:T(2,128)S(1)} %bitcast.1, ...), custom_call_target="tpu_custom_call" | custom-call | flops 1000000000 | bytes 10000000 | tf_op jit(solution)/shard_map/pallas_call | solution.py:283
  4.3 0.1 collective-permute-done.1.other_ref
  4.5 1.6 %shard_map.52 = (f32[16,128]{1,0:T(8,128)S(1)}, f32[16,128]{1,0:T(8,128)S(1)}, f32[16,128]{1,0:T(8,128)S(1)}, f32[16,128]{1,0:T(8,128)S(1)}, f32[16,128]{1,0:T(8,128)S(1)}) custom-call(s32[2,64]{1,0:T(2,128)S(1)} %bitcast.2, f32[4,2,80,640]{3,2,1,0:T(8,128)S(1)} %collective-permute-done.1.other_ref, f32[2,4,5,80,128]{4,3,2,1,0:T(8,128)S(1)} %get-tuple-element.29.keep, ...), custom_call_target="tpu_custom_call" | custom-call | flops 1000000000 | bytes 10000000 | tf_op jit(solution)/shard_map/pallas_call | solution.py:337
  6.1 0.0 copy-start.1
  6.1 1.4 %collective-permute-start.2 = (f32[16,128]{1,0:T(8,128)S(1)}, f32[16,128]{1,0:T(8,128)S(1)}, u32[]{:S(2)}, u32[]{:S(2)}) collective-permute-start(f32[16,128]{1,0:T(8,128)S(1)} %get-tuple-element.34), channel_id=1, source_target_pairs={{0,1},{1,0},{2,3},{3,2},{4,5},{5,4},{6,7},{7,6},{8,9},{9,8},{10,11... | collective-permute-start | bytes 24584 | tf_op jit(solution)/shard_map/ppermute | solution.py:536
  7.5 0.0 collective-permute-start.3
  7.5 5.5 %collective-permute-done.other_ref = f32[3,5,80,128]{3,2,1,0:T(8,128)S(1)} collective-permute-done((f32[3,5,80,128]{3,2,1,0:T(8,128)S(1)}, f32[3,5,80,128]{3,2,1,0:T(8,128)S(1)}, u32[]{:S(2)}, u32[]{:S(2)}) %collective-permute-start) | collective-permute-done | bytes 614432 | tf_op jit(solution)/shard_map/ppermute | solution.py:536
  13.0 0.0 collective-permute-done.2.first_ref
  13.0 0.0 collective-permute-done.3.second_ref
  13.0 0.4 %shard_map.53 = (f32[16,128]{1,0:T(8,128)S(1)}, f32[32,128]{1,0:T(8,128)S(1)}) custom-call(s32[8,128]{1,0:T(8,128)S(1)} %get-tuple-element.28.index_ref, f32[3,5,80,128]{3,2,1,0:T(8,128)S(1)} %collective-permute-done.other_ref, f32[4,5,80,128]{3,2,1,0:T(8,128)S(1)} %get-tuple-element.37.mine_ref, bf16[384,256]{1,0:T(8,128)(2,1)S(1)} %get-tuple-element.30.table_ref, ...), custom_call_target="tpu_custom_call" | custom-call | tf_op jit(solution)/shard_map/pallas_call | solution.py:403
  13.4 0.9 %collective-permute-start.4 = (f32[32,128]{1,0:T(8,128)S(1)}, f32[32,128]{1,0:T(8,128)S(1)}, u32[]{:S(2)}, u32[]{:S(2)}) collective-permute-start(f32[32,128]{1,0:T(8,128)S(1)} %get-tuple-element.39), channel_id=1, source_target_pairs={{0,1},{1,0},{2,3},{3,2},{4,5},{5,4},{6,7},{7,6},{8,9},{9,8},{10,11... | collective-permute-start | bytes 49160 | tf_op jit(solution)/shard_map/ppermute | solution.py:536
  14.3 2.0 %collective-permute-start.5 = (f32[32,128]{1,0:T(8,128)S(1)}, f32[32,128]{1,0:T(8,128)S(1)}, u32[]{:S(2)}, u32[]{:S(2)}) collective-permute-start(f32[32,128]{1,0:T(8,128)S(1)} %get-tuple-element.39), channel_id=1, source_target_pairs={{0,1},{1,0},{2,3},{3,2},{4,5},{5,4},{6,7},{7,6},{8,9},{9,8},{10,11... | collective-permute-start | bytes 49160 | tf_op jit(solution)/shard_map/ppermute | solution.py:536
  16.3 1.4 %collective-permute-start.6 = (f32[16,128]{1,0:T(8,128)S(1)}, f32[16,128]{1,0:T(8,128)S(1)}, u32[]{:S(2)}, u32[]{:S(2)}) collective-permute-start(f32[16,128]{1,0:T(8,128)S(1)} %get-tuple-element.40.left_late), channel_id=1, source_target_pairs={{0,1},{1,2},{2,3},{3,19},{4,5},{5,6},{6,7},{7,23},{8,9},{9,10},{10... | collective-permute-start | bytes 24584 | tf_op jit(solution)/shard_map/ppermute | solution.py:536
  17.7 2.3 %collective-permute-done.6.after_late = f32[16,128]{1,0:T(8,128)S(1)} collective-permute-done((f32[16,128]{1,0:T(8,128)S(1)}, f32[16,128]{1,0:T(8,128)S(1)}, u32[]{:S(2)}, u32[]{:S(2)}) %collective-permute-start.6) | collective-permute-done | bytes 8224 | tf_op jit(solution)/shard_map/ppermute | solution.py:536
  20.0 0.0 collective-permute-done.4.before_late
  20.0 0.0 collective-permute-done.5.right_late.late_ref
  20.0 1.3 %collective-permute-start.7 = (f32[16,512]{1,0:T(8,128)S(1)}, f32[16,512]{1,0:T(8,128)S(1)}, u32[]{:S(2)}, u32[]{:S(2)}) collective-permute-start(f32[16,512]{1,0:T(8,128)S(1)} %shard_map.54.mid_ref), channel_id=1, source_target_pairs={{0,4},{1,5},{2,6},{3,7},{4,0},{5,1},{6,2},{7,3},{8,12},{9,13},{10,... | collective-permute-start | bytes 98312 | tf_op jit(solution)/shard_map/ppermute | solution.py:536
  21.3 0.0 collective-permute-start.8
  21.3 0.0 copy-done.1
  21.3 0.1 shard_map.55
  21.4 2.6 %collective-permute-done.7.first_swap = f32[16,512]{1,0:T(8,128)S(1)} collective-permute-done((f32[16,512]{1,0:T(8,128)S(1)}, f32[16,512]{1,0:T(8,128)S(1)}, u32[]{:S(2)}, u32[]{:S(2)}) %collective-permute-start.7) | collective-permute-done | bytes 32800 | tf_op jit(solution)/shard_map/ppermute | solution.py:536
  24.0 1.2 %collective-permute-done.8.second_swap = f32[16,512]{1,0:T(8,128)S(1)} collective-permute-done((f32[16,512]{1,0:T(8,128)S(1)}, f32[16,512]{1,0:T(8,128)S(1)}, u32[]{:S(2)}, u32[]{:S(2)}) %collective-permute-start.8) | collective-permute-done | bytes 32800 | tf_op jit(solution)/shard_map/ppermute | solution.py:536
  25.2 1.7 %shard_map.56 = (f32[4,2,16,32]{3,2,1,0:T(8,128)}, f32[4,16,32]{2,1,0:T(8,128)}) custom-call(f32[16,512]{1,0:T(8,128)S(1)} %collective-permute-done.7.first_swap, f32[16,512]{1,0:T(8,128)S(1)} %shard_map.54.mid_ref, f32[16,512]{1,0:T(8,128)S(1)} %collective-permute-done.8.second_swap, bf16[128,128]{1,0:T(8,128)(2,1)S(1)} %get-tuple-element.45.ns_ref, ...), custom_call_target="tpu_custom_call" | custom-call | tf_op jit(solution)/shard_map/pallas_call | solution.py:508
  (1 shorter events, 0.0 us)
Async XLA Ops:
  0.6 1.8 %copy-start = (f32[4,2,80,640]{3,2,1,0:T(8,128)S(1)}, f32[4,2,80,640]{3,2,1,0:T(8,128)}, u32[]{:S(2)}) copy-start(f32[4,2,80,640]{3,2,1,0:T(8,128)} %stack_ref.3) | copy-start | bytes 4915204
  0.6 1.8 %copy-start.2 = (s32[64,2]{0,1:T(2,128)S(1)}, s32[64,2]{0,1:T(2,128)}, u32[]{:S(2)}) copy-start(s32[64,2]{0,1:T(2,128)} %param.4) | copy-start | bytes 1540
  0.6 3.8 %collective-permute-start.1 = (f32[4,2,80,640]{3,2,1,0:T(8,128)}, f32[4,2,80,640]{3,2,1,0:T(8,128)S(1)}, u32[]{:S(2)}, u32[]{:S(2)}) collective-permute-start(f32[4,2,80,640]{3,2,1,0:T(8,128)} %stack_ref.3), channel_id=1, source_target_pairs={{0,16},{1,17},{2,18},{3,19},{4,20},{5,21},{6,22},{7,23},{8,24},{9,... | collective-permute-start | bytes 4915208 | tf_op jit(solution)/shard_map/ppermute | solution.py:536
  2.1 10.9 %collective-permute-start = (f32[3,5,80,128]{3,2,1,0:T(8,128)S(1)}, f32[3,5,80,128]{3,2,1,0:T(8,128)S(1)}, u32[]{:S(2)}, u32[]{:S(2)}) collective-permute-start(f32[3,5,80,128]{3,2,1,0:T(8,128)S(1)} %shard_map.51), channel_id=1, source_target_pairs={{0,1},{1,0},{2,3},{3,2},{4,5},{5,4},{6,7},{7,6},{8,9},{9,8},{10,11... | collective-permute-start | bytes 1843208 | tf_op jit(solution)/shard_map/ppermute | solution.py:536
  6.1 15.2 %copy-start.1 = (f32[704,256]{1,0:T(8,128)S(1)}, f32[704,256]{1,0:T(8,128)}, u32[]{:S(2)}) copy-start(f32[704,256]{1,0:T(8,128)} %constant.2.clone.trig_ref) | copy-start | bytes 2162692
  6.1 6.9 %collective-permute-start.2 = (f32[16,128]{1,0:T(8,128)S(1)}, f32[16,128]{1,0:T(8,128)S(1)}, u32[]{:S(2)}, u32[]{:S(2)}) collective-permute-start(f32[16,128]{1,0:T(8,128)S(1)} %get-tuple-element.34), channel_id=1, source_target_pairs={{0,1},{1,0},{2,3},{3,2},{4,5},{5,4},{6,7},{7,6},{8,9},{9,8},{10,11... | collective-permute-start | bytes 24584 | tf_op jit(solution)/shard_map/ppermute | solution.py:536
  7.5 5.5 %collective-permute-start.3 = (f32[16,128]{1,0:T(8,128)S(1)}, f32[16,128]{1,0:T(8,128)S(1)}, u32[]{:S(2)}, u32[]{:S(2)}) collective-permute-start(f32[16,128]{1,0:T(8,128)S(1)} %get-tuple-element.35), channel_id=1, source_target_pairs={{0,4},{1,2},{2,1},{3,7},{4,0},{5,6},{6,5},{7,3},{8,12},{9,10},{10,... | collective-permute-start | bytes 24584 | tf_op jit(solution)/shard_map/ppermute | solution.py:536
  13.4 6.6 %collective-permute-start.4 = (f32[32,128]{1,0:T(8,128)S(1)}, f32[32,128]{1,0:T(8,128)S(1)}, u32[]{:S(2)}, u32[]{:S(2)}) collective-permute-start(f32[32,128]{1,0:T(8,128)S(1)} %get-tuple-element.39), channel_id=1, source_target_pairs={{0,1},{1,0},{2,3},{3,2},{4,5},{5,4},{6,7},{7,6},{8,9},{9,8},{10,11... | collective-permute-start | bytes 49160 | tf_op jit(solution)/shard_map/ppermute | solution.py:536
  14.3 5.7 %collective-permute-start.5 = (f32[32,128]{1,0:T(8,128)S(1)}, f32[32,128]{1,0:T(8,128)S(1)}, u32[]{:S(2)}, u32[]{:S(2)}) collective-permute-start(f32[32,128]{1,0:T(8,128)S(1)} %get-tuple-element.39), channel_id=1, source_target_pairs={{0,1},{1,0},{2,3},{3,2},{4,5},{5,4},{6,7},{7,6},{8,9},{9,8},{10,11... | collective-permute-start | bytes 49160 | tf_op jit(solution)/shard_map/ppermute | solution.py:536
  16.3 3.7 %collective-permute-start.6 = (f32[16,128]{1,0:T(8,128)S(1)}, f32[16,128]{1,0:T(8,128)S(1)}, u32[]{:S(2)}, u32[]{:S(2)}) collective-permute-start(f32[16,128]{1,0:T(8,128)S(1)} %get-tuple-element.40.left_late), channel_id=1, source_target_pairs={{0,1},{1,2},{2,3},{3,19},{4,5},{5,6},{6,7},{7,23},{8,9},{9,10},{10... | collective-permute-start | bytes 24584 | tf_op jit(solution)/shard_map/ppermute | solution.py:536
  20.0 4.0 %collective-permute-start.7 = (f32[16,512]{1,0:T(8,128)S(1)}, f32[16,512]{1,0:T(8,128)S(1)}, u32[]{:S(2)}, u32[]{:S(2)}) collective-permute-start(f32[16,512]{1,0:T(8,128)S(1)} %shard_map.54.mid_ref), channel_id=1, source_target_pairs={{0,4},{1,5},{2,6},{3,7},{4,0},{5,1},{6,2},{7,3},{8,12},{9,13},{10,... | collective-permute-start | bytes 98312 | tf_op jit(solution)/shard_map/ppermute | solution.py:536
  21.3 3.9 %collective-permute-start.8 = (f32[16,512]{1,0:T(8,128)S(1)}, f32[16,512]{1,0:T(8,128)S(1)}, u32[]{:S(2)}, u32[]{:S(2)}) collective-permute-start(f32[16,512]{1,0:T(8,128)S(1)} %shard_map.54.mid_ref), channel_id=1, source_target_pairs={{0,16},{1,17},{2,18},{3,19},{4,8},{5,9},{6,10},{7,11},{8,4},{9,5},... | collective-permute-start | bytes 98312 | tf_op jit(solution)/shard_map/ppermute | solution.py:536

commit v8 on v6

--- a/solution.py
+++ b/solution.py
@@ -534,7 +534,7 @@
     def swap_cols(first):
         def target(d, r, c):
             e = neighbour(c, cols, first)
-            return (d, r, e) if e != c else (d, r ^ 1, c)
+            return (d, r, e) if e != c else (d ^ 1, r, c)
 
         return target
 
@@ -565,8 +565,8 @@
         return (d, r, c + 1) if c < end else (d + 1, r, c)
 
     from_left = between_dates(
-        lambda c: (1, 0) if c == 0 else (0, 0) if c == 1 else (1, c - 1) if c < end else (1, end),
-        lambda c: (1, c + 1) if c < end else (0, end - 1),
+        lambda c: (0, 0) if c == 1 else (1, c),
+        lambda c: (1, c + 1) if c < end else (0, 1),
     )
 
     listed = pair_list.T

time: 27.2 us -> 27.2 us (level)
  no operation moved by 1% of the time
where the time goes in v8:
time: 27.2 us; the launch traced here: 27 us
  waiting for transfers between devices  11.8 us (43%)
  starting transfers between devices  7.27 us (27%)
  Pallas kernels  7.12 us (26%)
  between operations  0.72 us (3%)
    ppermute x9, waiting for transfers between devices, send(): return lax.ppermute(x, names, pairs)  11.8 us
    ppermute x9, starting transfers between devices, send(): return lax.ppermute(x, names, pairs)  7.27 us
    pallas_call x1, Pallas kernels, early(): pl.pallas_call(early_kernel, out_shape=out_shape, in_specs=[smem, pl.Bloc...  1.82 us
    pallas_call x1, Pallas kernels, goldstein(): pl.pallas_call(goldstein_kernel, out_shape=(jax.ShapeDtypeStruct((PAIRS_D...  1.71 us
    pallas_call x1, Pallas kernels, within_chip(): pl.pallas_call(chip_kernel, out_shape=[jax.ShapeDtypeStruct((16, 128), F3...  1.67 us
    pallas_call x1, Pallas kernels, pack(): pl.pallas_call(pack_kernel, out_shape=pltpu.VMEM((SPAN, 5, 80, 128), F32)...  1.37 us
  transfers between devices with their start and end apart: 9, of which 5 were waited for; matrix products, arithmetic and copies ran while one was open for 0% of the time, Pallas kernels for 19%

profile of v8, /device:TPU:148, one launch (start us, length us, event | category | flops | bytes accessed | tf_op | source)
XLA Modules:
  0.0 27.0 jit_solution(12163027339818211650)
XLA Ops:
  0.6 0.0 copy-start
  0.6 0.0 copy-start.2
  0.6 0.1 collective-permute-start.1
  0.7 1.4 %shard_map.51 = f32[3,5,80,128]{3,2,1,0:T(8,128)S(1)} custom-call(f32[4,2,80,640]{3,2,1,0:T(8,128)} %stack_ref.3), custom_call_target="tpu_custom_call" | custom-call | tf_op jit(solution)/shard_map/pallas_call | solution.py:159
  2.1 0.2 collective-permute-start
  2.3 0.1 copy-done
  2.4 0.0 copy-done.2
  2.4 1.8 %shard_map.50 = (f32[16,128]{1,0:T(8,128)S(1)}, f32[16,128]{1,0:T(8,128)S(1)}, f32[16,128]{1,0:T(8,128)S(1)}, f32[16,128]{1,0:T(8,128)S(1)}, f32[16,128]{1,0:T(8...) custom-call(s32[2,64]{1,0:T(2,128)S(1)} %bitcast.1, ...), custom_call_target="tpu_custom_call" | custom-call | flops 1000000000 | bytes 10000000 | tf_op jit(solution)/shard_map/pallas_call | solution.py:279
  4.2 0.2 collective-permute-done.1.other_ref
  4.5 1.7 %shard_map.52 = (f32[16,128]{1,0:T(8,128)S(1)}, f32[16,128]{1,0:T(8,128)S(1)}, f32[16,128]{1,0:T(8,128)S(1)}, f32[16,128]{1,0:T(8,128)S(1)}, f32[16,128]{1,0:T(8,128)S(1)}) custom-call(s32[2,64]{1,0:T(2,128)S(1)} %bitcast.2, f32[4,2,80,640]{3,2,1,0:T(8,128)S(1)} %collective-permute-done.1.other_ref, f32[2,4,5,80,128]{4,3,2,1,0:T(8,128)S(1)} %get-tuple-element.28.keep, ...), custom_call_target="tpu_custom_call" | custom-call | flops 1000000000 | bytes 10000000 | tf_op jit(solution)/shard_map/pallas_call | solution.py:333
  6.1 0.0 copy-start.1
  6.1 1.4 %collective-permute-start.2 = (f32[16,128]{1,0:T(8,128)S(1)}, f32[16,128]{1,0:T(8,128)S(1)}, u32[]{:S(2)}, u32[]{:S(2)}) collective-permute-start(f32[16,128]{1,0:T(8,128)S(1)} %get-tuple-element.33), channel_id=1, source_target_pairs={{0,1},{1,0},{2,3},{3,2},{4,5},{5,4},{6,7},{7,6},{8,9},{9,8},{10,11... | collective-permute-start | bytes 24584 | tf_op jit(solution)/shard_map/ppermute | solution.py:532
  7.5 0.0 collective-permute-start.3
  7.5 5.5 %collective-permute-done.other_ref = f32[3,5,80,128]{3,2,1,0:T(8,128)S(1)} collective-permute-done((f32[3,5,80,128]{3,2,1,0:T(8,128)S(1)}, f32[3,5,80,128]{3,2,1,0:T(8,128)S(1)}, u32[]{:S(2)}, u32[]{:S(2)}) %collective-permute-start) | collective-permute-done | bytes 614432 | tf_op jit(solution)/shard_map/ppermute | solution.py:532
  13.0 0.0 collective-permute-done.2.first_ref
  13.0 0.0 collective-permute-done.3.second_ref
  13.0 0.4 %shard_map.53 = (f32[16,128]{1,0:T(8,128)S(1)}, f32[32,128]{1,0:T(8,128)S(1)}) custom-call(s32[8,128]{1,0:T(8,128)S(1)} %get-tuple-element.27.index_ref, f32[3,5,80,128]{3,2,1,0:T(8,128)S(1)} %collective-permute-done.other_ref, f32[2,4,5,80,128]{4,3,2,1,0:T(8,128)S(1)} %get-tuple-element.28.keep, bf16[384,256]{1,0:T(8,128)(2,1)S(1)} %get-tuple-element.29.table_ref, ...), custom_call_target="tpu_custom_call" | custom-call | tf_op jit(solution)/shard_map/pallas_call | solution.py:399
  13.4 0.9 %collective-permute-start.4 = (f32[32,128]{1,0:T(8,128)S(1)}, f32[32,128]{1,0:T(8,128)S(1)}, u32[]{:S(2)}, u32[]{:S(2)}) collective-permute-start(f32[32,128]{1,0:T(8,128)S(1)} %get-tuple-element.37), channel_id=1, source_target_pairs={{0,1},{1,0},{2,3},{3,2},{4,5},{5,4},{6,7},{7,6},{8,9},{9,8},{10,11... | collective-permute-start | bytes 49160 | tf_op jit(solution)/shard_map/ppermute | solution.py:532
  14.3 2.1 %collective-permute-start.5 = (f32[32,128]{1,0:T(8,128)S(1)}, f32[32,128]{1,0:T(8,128)S(1)}, u32[]{:S(2)}, u32[]{:S(2)}) collective-permute-start(f32[32,128]{1,0:T(8,128)S(1)} %get-tuple-element.37), channel_id=1, source_target_pairs={{0,1},{1,0},{2,3},{3,2},{4,5},{5,4},{6,7},{7,6},{8,9},{9,8},{10,11... | collective-permute-start | bytes 49160 | tf_op jit(solution)/shard_map/ppermute | solution.py:532
  16.5 1.3 %collective-permute-start.6 = (f32[16,128]{1,0:T(8,128)S(1)}, f32[16,128]{1,0:T(8,128)S(1)}, u32[]{:S(2)}, u32[]{:S(2)}) collective-permute-start(f32[16,128]{1,0:T(8,128)S(1)} %get-tuple-element.38.left_late), channel_id=1, source_target_pairs={{0,1},{1,2},{2,3},{3,19},{4,5},{5,6},{6,7},{7,23},{8,9},{9,10},{10... | collective-permute-start | bytes 24584 | tf_op jit(solution)/shard_map/ppermute | solution.py:532
  17.7 2.4 %collective-permute-done.6.after_late = f32[16,128]{1,0:T(8,128)S(1)} collective-permute-done((f32[16,128]{1,0:T(8,128)S(1)}, f32[16,128]{1,0:T(8,128)S(1)}, u32[]{:S(2)}, u32[]{:S(2)}) %collective-permute-start.6) | collective-permute-done | bytes 8224 | tf_op jit(solution)/shard_map/ppermute | solution.py:532
  20.1 0.0 collective-permute-done.4.before_late
  20.1 0.0 collective-permute-done.5.right_late.late_ref
  20.1 1.3 %collective-permute-start.7 = (f32[16,512]{1,0:T(8,128)S(1)}, f32[16,512]{1,0:T(8,128)S(1)}, u32[]{:S(2)}, u32[]{:S(2)}) collective-permute-start(f32[16,512]{1,0:T(8,128)S(1)} %shard_map.54.mid_ref), channel_id=1, source_target_pairs={{0,4},{1,5},{2,6},{3,7},{4,0},{5,1},{6,2},{7,3},{8,12},{9,13},{10,... | collective-permute-start | bytes 98312 | tf_op jit(solution)/shard_map/ppermute | solution.py:532
  21.4 0.0 collective-permute-start.8
  21.4 0.0 copy-done.1
  21.4 0.1 shard_map.55
  21.6 2.6 %collective-permute-done.7.first_swap = f32[16,512]{1,0:T(8,128)S(1)} collective-permute-done((f32[16,512]{1,0:T(8,128)S(1)}, f32[16,512]{1,0:T(8,128)S(1)}, u32[]{:S(2)}, u32[]{:S(2)}) %collective-permute-start.7) | collective-permute-done | bytes 32800 | tf_op jit(solution)/shard_map/ppermute | solution.py:532
  24.1 1.2 %collective-permute-done.8.second_swap = f32[16,512]{1,0:T(8,128)S(1)} collective-permute-done((f32[16,512]{1,0:T(8,128)S(1)}, f32[16,512]{1,0:T(8,128)S(1)}, u32[]{:S(2)}, u32[]{:S(2)}) %collective-permute-start.8) | collective-permute-done | bytes 32800 | tf_op jit(solution)/shard_map/ppermute | solution.py:532
  25.3 1.7 %shard_map.56 = (f32[4,2,16,32]{3,2,1,0:T(8,128)}, f32[4,16,32]{2,1,0:T(8,128)}) custom-call(f32[16,512]{1,0:T(8,128)S(1)} %collective-permute-done.7.first_swap, f32[16,512]{1,0:T(8,128)S(1)} %shard_map.54.mid_ref, f32[16,512]{1,0:T(8,128)S(1)} %collective-permute-done.8.second_swap, bf16[128,128]{1,0:T(8,128)(2,1)S(1)} %get-tuple-element.43.ns_ref, ...), custom_call_target="tpu_custom_call" | custom-call | tf_op jit(solution)/shard_map/pallas_call | solution.py:504
  (1 shorter events, 0.0 us)
Async XLA Ops:
  0.6 1.8 %copy-start = (f32[4,2,80,640]{3,2,1,0:T(8,128)S(1)}, f32[4,2,80,640]{3,2,1,0:T(8,128)}, u32[]{:S(2)}) copy-start(f32[4,2,80,640]{3,2,1,0:T(8,128)} %stack_ref.3) | copy-start | bytes 4915204
  0.6 1.8 %copy-start.2 = (s32[64,2]{0,1:T(2,128)S(1)}, s32[64,2]{0,1:T(2,128)}, u32[]{:S(2)}) copy-start(s32[64,2]{0,1:T(2,128)} %param.4) | copy-start | bytes 1540
  0.6 3.8 %collective-permute-start.1 = (f32[4,2,80,640]{3,2,1,0:T(8,128)}, f32[4,2,80,640]{3,2,1,0:T(8,128)S(1)}, u32[]{:S(2)}, u32[]{:S(2)}) collective-permute-start(f32[4,2,80,640]{3,2,1,0:T(8,128)} %stack_ref.3), channel_id=1, source_target_pairs={{0,16},{1,17},{2,18},{3,19},{4,20},{5,21},{6,22},{7,23},{8,24},{9,... | collective-permute-start | bytes 4915208 | tf_op jit(solution)/shard_map/ppermute | solution.py:532
  2.1 10.9 %collective-permute-start = (f32[3,5,80,128]{3,2,1,0:T(8,128)S(1)}, f32[3,5,80,128]{3,2,1,0:T(8,128)S(1)}, u32[]{:S(2)}, u32[]{:S(2)}) collective-permute-start(f32[3,5,80,128]{3,2,1,0:T(8,128)S(1)} %shard_map.51), channel_id=1, source_target_pairs={{0,1},{1,0},{2,3},{3,2},{4,5},{5,4},{6,7},{7,6},{8,9},{9,8},{10,11... | collective-permute-start | bytes 1843208 | tf_op jit(solution)/shard_map/ppermute | solution.py:532
  6.1 15.3 %copy-start.1 = (f32[704,256]{1,0:T(8,128)S(1)}, f32[704,256]{1,0:T(8,128)}, u32[]{:S(2)}) copy-start(f32[704,256]{1,0:T(8,128)} %constant.2.clone.trig_ref) | copy-start | bytes 2162692
  6.1 6.9 %collective-permute-start.2 = (f32[16,128]{1,0:T(8,128)S(1)}, f32[16,128]{1,0:T(8,128)S(1)}, u32[]{:S(2)}, u32[]{:S(2)}) collective-permute-start(f32[16,128]{1,0:T(8,128)S(1)} %get-tuple-element.33), channel_id=1, source_target_pairs={{0,1},{1,0},{2,3},{3,2},{4,5},{5,4},{6,7},{7,6},{8,9},{9,8},{10,11... | collective-permute-start | bytes 24584 | tf_op jit(solution)/shard_map/ppermute | solution.py:532
  7.5 5.5 %collective-permute-start.3 = (f32[16,128]{1,0:T(8,128)S(1)}, f32[16,128]{1,0:T(8,128)S(1)}, u32[]{:S(2)}, u32[]{:S(2)}) collective-permute-start(f32[16,128]{1,0:T(8,128)S(1)} %get-tuple-element.34), channel_id=1, source_target_pairs={{0,16},{1,2},{2,1},{3,19},{4,20},{5,6},{6,5},{7,23},{8,24},{9,10},... | collective-permute-start | bytes 24584 | tf_op jit(solution)/shard_map/ppermute | solution.py:532
  13.4 6.7 %collective-permute-start.4 = (f32[32,128]{1,0:T(8,128)S(1)}, f32[32,128]{1,0:T(8,128)S(1)}, u32[]{:S(2)}, u32[]{:S(2)}) collective-permute-start(f32[32,128]{1,0:T(8,128)S(1)} %get-tuple-element.37), channel_id=1, source_target_pairs={{0,1},{1,0},{2,3},{3,2},{4,5},{5,4},{6,7},{7,6},{8,9},{9,8},{10,11... | collective-permute-start | bytes 49160 | tf_op jit(solution)/shard_map/ppermute | solution.py:532
  14.3 5.8 %collective-permute-start.5 = (f32[32,128]{1,0:T(8,128)S(1)}, f32[32,128]{1,0:T(8,128)S(1)}, u32[]{:S(2)}, u32[]{:S(2)}) collective-permute-start(f32[32,128]{1,0:T(8,128)S(1)} %get-tuple-element.37), channel_id=1, source_target_pairs={{0,1},{1,0},{2,3},{3,2},{4,5},{5,4},{6,7},{7,6},{8,9},{9,8},{10,11... | collective-permute-start | bytes 49160 | tf_op jit(solution)/shard_map/ppermute | solution.py:532
  16.5 3.7 %collective-permute-start.6 = (f32[16,128]{1,0:T(8,128)S(1)}, f32[16,128]{1,0:T(8,128)S(1)}, u32[]{:S(2)}, u32[]{:S(2)}) collective-permute-start(f32[16,128]{1,0:T(8,128)S(1)} %get-tuple-element.38.left_late), channel_id=1, source_target_pairs={{0,1},{1,2},{2,3},{3,19},{4,5},{5,6},{6,7},{7,23},{8,9},{9,10},{10... | collective-permute-start | bytes 24584 | tf_op jit(solution)/shard_map/ppermute | solution.py:532
  20.1 4.0 %collective-permute-start.7 = (f32[16,512]{1,0:T(8,128)S(1)}, f32[16,512]{1,0:T(8,128)S(1)}, u32[]{:S(2)}, u32[]{:S(2)}) collective-permute-start(f32[16,512]{1,0:T(8,128)S(1)} %shard_map.54.mid_ref), channel_id=1, source_target_pairs={{0,4},{1,5},{2,6},{3,7},{4,0},{5,1},{6,2},{7,3},{8,12},{9,13},{10,... | collective-permute-start | bytes 98312 | tf_op jit(solution)/shard_map/ppermute | solution.py:532
  21.4 3.9 %collective-permute-start.8 = (f32[16,512]{1,0:T(8,128)S(1)}, f32[16,512]{1,0:T(8,128)S(1)}, u32[]{:S(2)}, u32[]{:S(2)}) collective-permute-start(f32[16,512]{1,0:T(8,128)S(1)} %shard_map.54.mid_ref), channel_id=1, source_target_pairs={{0,16},{1,17},{2,18},{3,19},{4,8},{5,9},{6,10},{7,11},{8,4},{9,5},... | collective-permute-start | bytes 98312 | tf_op jit(solution)/shard_map/ppermute | solution.py:532

commit v9 on v7

--- a/solution.py
+++ b/solution.py
@@ -538,7 +538,7 @@
     def swap_cols(first):
         def target(d, r, c):
             e = neighbour(c, cols, first)
-            return (d, r, e) if e != c else (d, r ^ 1, c)
+            return (d, r, e) if e != c else (d ^ 1, r, c)
 
         return target
 
@@ -569,8 +569,8 @@
         return (d, r, c + 1) if c < end else (d + 1, r, c)
 
     from_left = between_dates(
-        lambda c: (1, 0) if c == 0 else (0, 0) if c == 1 else (1, c - 1) if c < end else (1, end),
-        lambda c: (1, c + 1) if c < end else (0, end - 1),
+        lambda c: (0, 0) if c == 1 else (1, c),
+        lambda c: (1, c + 1) if c < end else (0, 1),
     )
 
     listed = pair_list.T

time: 27.1 us -> 27.1 us (level)
  no operation moved by 1% of the time
where the time goes in v9:
time: 27.1 us; the launch traced here: 27 us
  waiting for transfers between devices  11.8 us (44%)
  starting transfers between devices  7.27 us (27%)
  Pallas kernels  7.1 us (26%)
  between operations  0.72 us (3%)
    ppermute x9, waiting for transfers between devices, send(): return lax.ppermute(x, names, pairs)  11.8 us
    ppermute x9, starting transfers between devices, send(): return lax.ppermute(x, names, pairs)  7.27 us
    pallas_call x1, Pallas kernels, early(): pl.pallas_call(early_kernel, out_shape=out_shape, in_specs=[smem, pl.Bloc...  1.88 us
    pallas_call x1, Pallas kernels, goldstein(): pl.pallas_call(goldstein_kernel, out_shape=(jax.ShapeDtypeStruct((PAIRS_D...  1.71 us
    pallas_call x1, Pallas kernels, within_chip(): pl.pallas_call(chip_kernel, out_shape=[jax.ShapeDtypeStruct((16, 128), F3...  1.63 us
    pallas_call x1, Pallas kernels, pack(): pl.pallas_call(pack_kernel, out_shape=pltpu.VMEM((SPAN, 5, 80, 128), F32)...  1.37 us
  transfers between devices with their start and end apart: 9, of which 5 were waited for; matrix products, arithmetic and copies ran while one was open for 0% of the time, Pallas kernels for 19%

profile of v9, /device:TPU:148, one launch (start us, length us, event | category | flops | bytes accessed | tf_op | source)
XLA Modules:
  0.0 27.0 jit_solution(12372638601885296406)
XLA Ops:
  0.6 0.0 copy-start
  0.6 0.0 copy-start.2
  0.6 0.1 collective-permute-start.1
  0.7 1.4 %shard_map.51 = f32[3,5,80,128]{3,2,1,0:T(8,128)S(1)} custom-call(f32[4,2,80,640]{3,2,1,0:T(8,128)} %stack_ref.3), custom_call_target="tpu_custom_call" | custom-call | tf_op jit(solution)/shard_map/pallas_call | solution.py:159
  2.1 0.2 collective-permute-start
  2.3 0.1 copy-done
  2.4 0.0 copy-done.2
  2.4 1.9 %shard_map.50 = (f32[16,128]{1,0:T(8,128)S(1)}, f32[16,128]{1,0:T(8,128)S(1)}, f32[16,128]{1,0:T(8,128)S(1)}, f32[16,128]{1,0:T(8,128)S(1)}, f32[16,128]{1,0:T(8...) custom-call(s32[2,64]{1,0:T(2,128)S(1)} %bitcast.1, ...), custom_call_target="tpu_custom_call" | custom-call | flops 1000000000 | bytes 10000000 | tf_op jit(solution)/shard_map/pallas_call | solution.py:283
  4.3 0.2 collective-permute-done.1.other_ref
  4.5 1.6 %shard_map.52 = (f32[16,128]{1,0:T(8,128)S(1)}, f32[16,128]{1,0:T(8,128)S(1)}, f32[16,128]{1,0:T(8,128)S(1)}, f32[16,128]{1,0:T(8,128)S(1)}, f32[16,128]{1,0:T(8,128)S(1)}) custom-call(s32[2,64]{1,0:T(2,128)S(1)} %bitcast.2, f32[4,2,80,640]{3,2,1,0:T(8,128)S(1)} %collective-permute-done.1.other_ref, f32[2,4,5,80,128]{4,3,2,1,0:T(8,128)S(1)} %get-tuple-element.29.keep, ...), custom_call_target="tpu_custom_call" | custom-call | flops 1000000000 | bytes 10000000 | tf_op jit(solution)/shard_map/pallas_call | solution.py:337
  6.1 0.0 copy-start.1
  6.1 1.4 %collective-permute-start.2 = (f32[16,128]{1,0:T(8,128)S(1)}, f32[16,128]{1,0:T(8,128)S(1)}, u32[]{:S(2)}, u32[]{:S(2)}) collective-permute-start(f32[16,128]{1,0:T(8,128)S(1)} %get-tuple-element.34), channel_id=1, source_target_pairs={{0,1},{1,0},{2,3},{3,2},{4,5},{5,4},{6,7},{7,6},{8,9},{9,8},{10,11... | collective-permute-start | bytes 24584 | tf_op jit(solution)/shard_map/ppermute | solution.py:536
  7.5 0.0 collective-permute-start.3
  7.5 5.5 %collective-permute-done.other_ref = f32[3,5,80,128]{3,2,1,0:T(8,128)S(1)} collective-permute-done((f32[3,5,80,128]{3,2,1,0:T(8,128)S(1)}, f32[3,5,80,128]{3,2,1,0:T(8,128)S(1)}, u32[]{:S(2)}, u32[]{:S(2)}) %collective-permute-start) | collective-permute-done | bytes 614432 | tf_op jit(solution)/shard_map/ppermute | solution.py:536
  13.0 0.0 collective-permute-done.2.first_ref
  13.0 0.0 collective-permute-done.3.second_ref
  13.0 0.4 %shard_map.53 = (f32[16,128]{1,0:T(8,128)S(1)}, f32[32,128]{1,0:T(8,128)S(1)}) custom-call(s32[8,128]{1,0:T(8,128)S(1)} %get-tuple-element.28.index_ref, f32[3,5,80,128]{3,2,1,0:T(8,128)S(1)} %collective-permute-done.other_ref, f32[4,5,80,128]{3,2,1,0:T(8,128)S(1)} %get-tuple-element.37.mine_ref, bf16[384,256]{1,0:T(8,128)(2,1)S(1)} %get-tuple-element.30.table_ref, ...), custom_call_target="tpu_custom_call" | custom-call | tf_op jit(solution)/shard_map/pallas_call | solution.py:403
  13.4 0.9 %collective-permute-start.4 = (f32[32,128]{1,0:T(8,128)S(1)}, f32[32,128]{1,0:T(8,128)S(1)}, u32[]{:S(2)}, u32[]{:S(2)}) collective-permute-start(f32[32,128]{1,0:T(8,128)S(1)} %get-tuple-element.39), channel_id=1, source_target_pairs={{0,1},{1,0},{2,3},{3,2},{4,5},{5,4},{6,7},{7,6},{8,9},{9,8},{10,11... | collective-permute-start | bytes 49160 | tf_op jit(solution)/shard_map/ppermute | solution.py:536
  14.3 2.1 %collective-permute-start.5 = (f32[32,128]{1,0:T(8,128)S(1)}, f32[32,128]{1,0:T(8,128)S(1)}, u32[]{:S(2)}, u32[]{:S(2)}) collective-permute-start(f32[32,128]{1,0:T(8,128)S(1)} %get-tuple-element.39), channel_id=1, source_target_pairs={{0,1},{1,0},{2,3},{3,2},{4,5},{5,4},{6,7},{7,6},{8,9},{9,8},{10,11... | collective-permute-start | bytes 49160 | tf_op jit(solution)/shard_map/ppermute | solution.py:536
  16.4 1.3 %collective-permute-start.6 = (f32[16,128]{1,0:T(8,128)S(1)}, f32[16,128]{1,0:T(8,128)S(1)}, u32[]{:S(2)}, u32[]{:S(2)}) collective-permute-start(f32[16,128]{1,0:T(8,128)S(1)} %get-tuple-element.40.left_late), channel_id=1, source_target_pairs={{0,1},{1,2},{2,3},{3,19},{4,5},{5,6},{6,7},{7,23},{8,9},{9,10},{10... | collective-permute-start | bytes 24584 | tf_op jit(solution)/shard_map/ppermute | solution.py:536
  17.7 2.4 %collective-permute-done.6.after_late = f32[16,128]{1,0:T(8,128)S(1)} collective-permute-done((f32[16,128]{1,0:T(8,128)S(1)}, f32[16,128]{1,0:T(8,128)S(1)}, u32[]{:S(2)}, u32[]{:S(2)}) %collective-permute-start.6) | collective-permute-done | bytes 8224 | tf_op jit(solution)/shard_map/ppermute | solution.py:536
  20.1 0.0 collective-permute-done.4.before_late
  20.1 0.0 collective-permute-done.5.right_late.late_ref
  20.1 1.3 %collective-permute-start.7 = (f32[16,512]{1,0:T(8,128)S(1)}, f32[16,512]{1,0:T(8,128)S(1)}, u32[]{:S(2)}, u32[]{:S(2)}) collective-permute-start(f32[16,512]{1,0:T(8,128)S(1)} %shard_map.54.mid_ref), channel_id=1, source_target_pairs={{0,4},{1,5},{2,6},{3,7},{4,0},{5,1},{6,2},{7,3},{8,12},{9,13},{10,... | collective-permute-start | bytes 98312 | tf_op jit(solution)/shard_map/ppermute | solution.py:536
  21.4 0.0 collective-permute-start.8
  21.4 0.0 copy-done.1
  21.4 0.1 shard_map.55
  21.5 2.6 %collective-permute-done.7.first_swap = f32[16,512]{1,0:T(8,128)S(1)} collective-permute-done((f32[16,512]{1,0:T(8,128)S(1)}, f32[16,512]{1,0:T(8,128)S(1)}, u32[]{:S(2)}, u32[]{:S(2)}) %collective-permute-start.7) | collective-permute-done | bytes 32800 | tf_op jit(solution)/shard_map/ppermute | solution.py:536
  24.1 1.2 %collective-permute-done.8.second_swap = f32[16,512]{1,0:T(8,128)S(1)} collective-permute-done((f32[16,512]{1,0:T(8,128)S(1)}, f32[16,512]{1,0:T(8,128)S(1)}, u32[]{:S(2)}, u32[]{:S(2)}) %collective-permute-start.8) | collective-permute-done | bytes 32800 | tf_op jit(solution)/shard_map/ppermute | solution.py:536
  25.3 1.7 %shard_map.56 = (f32[4,2,16,32]{3,2,1,0:T(8,128)}, f32[4,16,32]{2,1,0:T(8,128)}) custom-call(f32[16,512]{1,0:T(8,128)S(1)} %collective-permute-done.7.first_swap, f32[16,512]{1,0:T(8,128)S(1)} %shard_map.54.mid_ref, f32[16,512]{1,0:T(8,128)S(1)} %collective-permute-done.8.second_swap, bf16[128,128]{1,0:T(8,128)(2,1)S(1)} %get-tuple-element.45.ns_ref, ...), custom_call_target="tpu_custom_call" | custom-call | tf_op jit(solution)/shard_map/pallas_call | solution.py:508
  (1 shorter events, 0.0 us)
Async XLA Ops:
  0.6 1.8 %copy-start = (f32[4,2,80,640]{3,2,1,0:T(8,128)S(1)}, f32[4,2,80,640]{3,2,1,0:T(8,128)}, u32[]{:S(2)}) copy-start(f32[4,2,80,640]{3,2,1,0:T(8,128)} %stack_ref.3) | copy-start | bytes 4915204
  0.6 1.8 %copy-start.2 = (s32[64,2]{0,1:T(2,128)S(1)}, s32[64,2]{0,1:T(2,128)}, u32[]{:S(2)}) copy-start(s32[64,2]{0,1:T(2,128)} %param.4) | copy-start | bytes 1540
  0.6 3.8 %collective-permute-start.1 = (f32[4,2,80,640]{3,2,1,0:T(8,128)}, f32[4,2,80,640]{3,2,1,0:T(8,128)S(1)}, u32[]{:S(2)}, u32[]{:S(2)}) collective-permute-start(f32[4,2,80,640]{3,2,1,0:T(8,128)} %stack_ref.3), channel_id=1, source_target_pairs={{0,16},{1,17},{2,18},{3,19},{4,20},{5,21},{6,22},{7,23},{8,24},{9,... | collective-permute-start | bytes 4915208 | tf_op jit(solution)/shard_map/ppermute | solution.py:536
  2.1 10.9 %collective-permute-start = (f32[3,5,80,128]{3,2,1,0:T(8,128)S(1)}, f32[3,5,80,128]{3,2,1,0:T(8,128)S(1)}, u32[]{:S(2)}, u32[]{:S(2)}) collective-permute-start(f32[3,5,80,128]{3,2,1,0:T(8,128)S(1)} %shard_map.51), channel_id=1, source_target_pairs={{0,1},{1,0},{2,3},{3,2},{4,5},{5,4},{6,7},{7,6},{8,9},{9,8},{10,11... | collective-permute-start | bytes 1843208 | tf_op jit(solution)/shard_map/ppermute | solution.py:536
  6.1 15.3 %copy-start.1 = (f32[704,256]{1,0:T(8,128)S(1)}, f32[704,256]{1,0:T(8,128)}, u32[]{:S(2)}) copy-start(f32[704,256]{1,0:T(8,128)} %constant.2.clone.trig_ref) | copy-start | bytes 2162692
  6.1 6.9 %collective-permute-start.2 = (f32[16,128]{1,0:T(8,128)S(1)}, f32[16,128]{1,0:T(8,128)S(1)}, u32[]{:S(2)}, u32[]{:S(2)}) collective-permute-start(f32[16,128]{1,0:T(8,128)S(1)} %get-tuple-element.34), channel_id=1, source_target_pairs={{0,1},{1,0},{2,3},{3,2},{4,5},{5,4},{6,7},{7,6},{8,9},{9,8},{10,11... | collective-permute-start | bytes 24584 | tf_op jit(solution)/shard_map/ppermute | solution.py:536
  7.5 5.5 %collective-permute-start.3 = (f32[16,128]{1,0:T(8,128)S(1)}, f32[16,128]{1,0:T(8,128)S(1)}, u32[]{:S(2)}, u32[]{:S(2)}) collective-permute-start(f32[16,128]{1,0:T(8,128)S(1)} %get-tuple-element.35), channel_id=1, source_target_pairs={{0,16},{1,2},{2,1},{3,19},{4,20},{5,6},{6,5},{7,23},{8,24},{9,10},... | collective-permute-start | bytes 24584 | tf_op jit(solution)/shard_map/ppermute | solution.py:536
  13.4 6.7 %collective-permute-start.4 = (f32[32,128]{1,0:T(8,128)S(1)}, f32[32,128]{1,0:T(8,128)S(1)}, u32[]{:S(2)}, u32[]{:S(2)}) collective-permute-start(f32[32,128]{1,0:T(8,128)S(1)} %get-tuple-element.39), channel_id=1, source_target_pairs={{0,1},{1,0},{2,3},{3,2},{4,5},{5,4},{6,7},{7,6},{8,9},{9,8},{10,11... | collective-permute-start | bytes 49160 | tf_op jit(solution)/shard_map/ppermute | solution.py:536
  14.3 5.8 %collective-permute-start.5 = (f32[32,128]{1,0:T(8,128)S(1)}, f32[32,128]{1,0:T(8,128)S(1)}, u32[]{:S(2)}, u32[]{:S(2)}) collective-permute-start(f32[32,128]{1,0:T(8,128)S(1)} %get-tuple-element.39), channel_id=1, source_target_pairs={{0,1},{1,0},{2,3},{3,2},{4,5},{5,4},{6,7},{7,6},{8,9},{9,8},{10,11... | collective-permute-start | bytes 49160 | tf_op jit(solution)/shard_map/ppermute | solution.py:536
  16.4 3.7 %collective-permute-start.6 = (f32[16,128]{1,0:T(8,128)S(1)}, f32[16,128]{1,0:T(8,128)S(1)}, u32[]{:S(2)}, u32[]{:S(2)}) collective-permute-start(f32[16,128]{1,0:T(8,128)S(1)} %get-tuple-element.40.left_late), channel_id=1, source_target_pairs={{0,1},{1,2},{2,3},{3,19},{4,5},{5,6},{6,7},{7,23},{8,9},{9,10},{10... | collective-permute-start | bytes 24584 | tf_op jit(solution)/shard_map/ppermute | solution.py:536
  20.1 4.0 %collective-permute-start.7 = (f32[16,512]{1,0:T(8,128)S(1)}, f32[16,512]{1,0:T(8,128)S(1)}, u32[]{:S(2)}, u32[]{:S(2)}) collective-permute-start(f32[16,512]{1,0:T(8,128)S(1)} %shard_map.54.mid_ref), channel_id=1, source_target_pairs={{0,4},{1,5},{2,6},{3,7},{4,0},{5,1},{6,2},{7,3},{8,12},{9,13},{10,... | collective-permute-start | bytes 98312 | tf_op jit(solution)/shard_map/ppermute | solution.py:536
  21.4 3.9 %collective-permute-start.8 = (f32[16,512]{1,0:T(8,128)S(1)}, f32[16,512]{1,0:T(8,128)S(1)}, u32[]{:S(2)}, u32[]{:S(2)}) collective-permute-start(f32[16,512]{1,0:T(8,128)S(1)} %shard_map.54.mid_ref), channel_id=1, source_target_pairs={{0,16},{1,17},{2,18},{3,19},{4,8},{5,9},{6,10},{7,11},{8,4},{9,5},... | collective-permute-start | bytes 98312 | tf_op jit(solution)/shard_map/ppermute | solution.py:536
